TPU v7x, 128 devices: a whole 4x4x4 slice. The times are simulated.
128 devices in a mesh: blk: 32 (over z, y_lo, x), rel: 4 (over y_hi, core).
Axes of the slice: x: 4, y: 4 (y_hi: 2, y_lo: 2; y = y_hi * 2 + y_lo), z: 4, core: 2. Of those that a mesh axis runs over, the one named last changes fastest.
Arguments:
- left: float32 [131072, 400], P(('blk', 'rel')), may hold values from -1.5 to 1.5
- left_state: float32 [131072], P(('blk', 'rel')), may hold values from 0.02 to 1
- right: float32 [131072, 400], P(('blk', 'rel')), may hold values from -1.5 to 1.5
- right_state: float32 [131072], P(('blk', 'rel')), may hold values from 0.02 to 1
- operators: bfloat16 [24, 400, 400], P('rel'), may hold values from -0.3125 to 0.3125
- need_list: int32 [128, 4, 4], P(('blk', 'rel')), may hold values from -1 to 23, as said below
- block_slot: int32 [128, 3, 8], P(('blk', 'rel')), may hold values from 0 to 15, as said below
- sources: int32 [128, 3, 2048], P(('blk', 'rel')), may hold values from 0 to 1023
- targets: int32 [128, 3, 2048], P(('blk', 'rel')), may hold values from 0 to 1023
- negatives: int32 [128, 3, 8, 256], P(('blk', 'rel')), may hold values from 0 to 1023
Outputs:
- new_left: float32 [131072, 400], P(('blk', 'rel'))
- new_left_state: float32 [131072], P(('blk', 'rel'))
- new_right: float32 [131072, 400], P(('blk', 'rel'))
- new_right_state: float32 [131072], P(('blk', 'rel'))
- op_grad: float32 [24, 160000], P('rel', 'blk')
Inputs may be any that keep to these rules, and one draw needn't show every extreme that they name: `need_list`: row o of a device's list holds distinct relations of owner o (ids o * 6 to (o + 1) * 6 - 1) first, then -1; every device fills all 4 slots of some owner. `block_slot`: every entry points at a relation of the list, and every relation of a device's list is named by some block of that device.
All inputs are finite; a program needn't handle non-finite values.
Results may differ from a plain program's by a relative error of at most 0.006.
Values may be sent and summed in bfloat16 or wider, within the bound.
A program may use at most 192 MiB of HBM per device.

v0:
```python
import jax
import jax.numpy as jnp
from jax import lax
from jax.sharding import PartitionSpec as P

BUCKETS = 3


step_size = 0.3


def from_behind(value, axis, steps):
    count = lax.axis_size(axis)
    pairs = [(source, (source + steps) % count) for source in range(count)]
    return lax.ppermute(value, axis, pairs)


def bucket_step(left_rows, left_acc, right_rows, right_acc, ops, src, dst, neg):
    nblk = neg.shape[0]
    width = left_rows.shape[1]
    left_half = left_rows.astype(jnp.bfloat16)
    right_half = right_rows.astype(jnp.bfloat16)
    heads = left_half[src].reshape(nblk, -1, width)
    tails = right_half[dst].reshape(nblk, -1, width)
    noise = right_half[neg]
    query = jnp.einsum("bed,bdf->bef", heads, ops, preferred_element_type=jnp.float32)
    query_half = query.astype(jnp.bfloat16)
    positive = jnp.sum(query * tails.astype(jnp.float32), axis=-1)
    negative = jnp.einsum("bef,bnf->ben", query_half, noise, preferred_element_type=jnp.float32)
    pull = -jax.nn.sigmoid(-positive)
    push = (jax.nn.sigmoid(negative) / noise.shape[1]).astype(jnp.bfloat16)
    grad_query = pull[..., None] * tails.astype(jnp.float32) + jnp.einsum(
        "ben,bnf->bef", push, noise, preferred_element_type=jnp.float32
    )
    grad_half = grad_query.astype(jnp.bfloat16)
    grad_heads = jnp.einsum("bef,bdf->bed", grad_half, ops, preferred_element_type=jnp.float32)
    grad_ops = jnp.einsum("bed,bef->bdf", heads, grad_half, preferred_element_type=jnp.float32)
    grad_tails = pull[..., None] * query
    grad_noise = jnp.einsum("ben,bef->bnf", push, query_half, preferred_element_type=jnp.float32)
    left_grad = jnp.zeros_like(left_rows).at[src].add(grad_heads.reshape(-1, width))
    right_grad = jnp.zeros_like(right_rows).at[dst].add(grad_tails.reshape(-1, width))
    right_grad = right_grad.at[neg.reshape(-1)].add(grad_noise.reshape(-1, width))
    left_acc = left_acc + jnp.mean(left_grad * left_grad, axis=-1)
    left_rows = left_rows - step_size * left_grad / jnp.sqrt(left_acc)[:, None]
    right_acc = right_acc + jnp.mean(right_grad * right_grad, axis=-1)
    right_rows = right_rows - step_size * right_grad / jnp.sqrt(right_acc)[:, None]
    return (left_rows, left_acc, right_rows, right_acc, grad_ops)


def body(
    left,
    left_state,
    right,
    right_state,
    operators,
    need_list,
    block_slot,
    sources,
    targets,
    negatives,
):
    owners = lax.axis_size("rel")
    owned_count = operators.shape[0]
    width = left.shape[1]
    needed = need_list[0]
    slots = block_slot[0]
    lookup = lax.all_gather(operators, "rel", axis=0, tiled=True)
    table_ids = needed.reshape(-1)[slots]
    entries = owned_count * owners
    grads = jnp.zeros((entries, width * width), jnp.float32)
    for bucket in range(BUCKETS):
        ids = table_ids[bucket]
        left, left_state, right, right_state, grad_ops = bucket_step(
            left,
            left_state,
            right,
            right_state,
            lookup[ids],
            sources[0, bucket],
            targets[0, bucket],
            negatives[0, bucket],
        )
        grads = grads.at[ids].add(grad_ops.reshape(ids.shape[0], width * width))
        right, right_state = from_behind((right, right_state), "blk", 1)
    owned = lax.psum_scatter(grads, "rel", scatter_dimension=0, tiled=True)
    op_grad = lax.psum_scatter(owned, "blk", scatter_dimension=1, tiled=True)
    return (left, left_state, right, right_state, op_grad)


def solution(mesh):
    in_specs = (
        P(("blk", "rel"), None),
        P(("blk", "rel")),
        P(("blk", "rel"), None),
        P(("blk", "rel")),
        P("rel", None, None),
        P(("blk", "rel"), None, None),
        P(("blk", "rel"), None, None),
        P(("blk", "rel"), None, None),
        P(("blk", "rel"), None, None),
        P(("blk", "rel"), None, None, None),
    )
    out_specs = (
        P(("blk", "rel"), None),
        P(("blk", "rel")),
        P(("blk", "rel"), None),
        P(("blk", "rel")),
        P("rel", "blk"),
    )
    return jax.shard_map(body, mesh=mesh, in_specs=in_specs, out_specs=out_specs, check_vma=False)
```

profile of v0, /device:TPU:8, one launch (start us, length us, event | category | flops | bytes accessed | tf_op | source)
XLA Modules:
  0.0 1554.9 jit_solution(12160863965968384105)
XLA Ops:
  15.4 9.2 gather_fusion.3
  33.4 9.2 gather_fusion.4
  43.4 9.2 gather_fusion
  53.8 27.8 %all-gather.2.cloned.1.call-done = bf16[24,400,400]{2,1,0:T(8,128)(2,1)} async-done(((bf16[6,400,400]{2,1,0:T(8,128)(2,1)}), bf16[24,400,400]{2,1,0:T(8,128)(2,1)}) %all-gather.2.cloned.1.call-update) | async-done | bytes 7680016 | tf_op jit(solution)/shard_map/all_gather | solution.py:67
  102.1 13.7 scatter_custom_fusion.1
  115.9 14.3 scatter_fusion
  159.4 174.2 %while.3 = (s32[]{:T(128)}, f32[24,160000]{1,0:T(8,128)}, s32[8]{0:T(128)S(1)}, f32[8,160000]{1,0:T(8,128)}, s32[]{:T(128)}, /*index=5*/s32[2]{0:T(128)S(1)}, s32[1]{0:T(128)}, s32[]{:T(128)}) while((s32[]{:T(128)}, f32[24,160000]{1,0:T(8,128)}, s32[8]{0:T(128)S(1)}, f32[8,160000]{1,0:T(8,128)}, s32[]{:T(128)}, /*index=5*/s32[2]{0:T(128)S(1)}, ...), condition=%wide.while_cond, body=%wide.while_body.sunk | while | flops 320011 | bytes 3200135 | solution.py:83
  167.4 13.9 dynamic-update-slice.9
  189.1 13.9 dynamic-update-slice.9
  210.9 13.9 dynamic-update-slice.9
  232.7 13.9 dynamic-update-slice.9
  254.5 13.9 dynamic-update-slice.9
  276.3 13.8 dynamic-update-slice.9
  298.0 13.9 dynamic-update-slice.9
  319.8 13.9 dynamic-update-slice.9
  338.9 23.9 %scatter_custom_fusion = f32[1024,400]{1,0:T(8,128)S(1)} fusion(s32[2048]{0:T(1024)S(1)} %bitcast.203, f32[2048,400]{1,0:T(8,128)} %bitcast.183, f32[]{:T(128)} %constant.9.clone.1), kind=kCustom, calls=%fused_computation.71 | custom fusion | flops 819200 | bytes 1638912 | tf_op jit(solution)/shard_map/scatter-add | solution.py:40
  389.2 9.2 gather_fusion.7
  405.7 9.2 gather_fusion.8
  430.6 13.7 scatter_custom_fusion.4
  444.3 14.0 scatter_fusion.1
  480.3 173.3 %while.4 = (s32[]{:T(128)}, f32[24,160000]{1,0:T(8,128)}, s32[8]{0:T(128)S(1)}, f32[8,160000]{1,0:T(8,128)}, s32[]{:T(128)}, /*index=5*/s32[2]{0:T(128)S(1)}, s32[1]{0:T(128)}, s32[]{:T(128)}) while((s32[]{:T(128)}, f32[24,160000]{1,0:T(8,128)}, s32[8]{0:T(128)S(1)}, f32[8,160000]{1,0:T(8,128)}, s32[]{:T(128)}, /*index=5*/s32[2]{0:T(128)S(1)}, ...), condition=%wide.while_cond.1, body=%wide.while_body.1.sunk | while | flops 320011 | bytes 3200135 | solution.py:83
  488.1 13.8 dynamic-update-slice.10
  509.8 13.8 dynamic-update-slice.10
  531.4 13.8 dynamic-update-slice.10
  553.1 13.8 dynamic-update-slice.10
  574.8 13.8 dynamic-update-slice.10
  596.4 13.8 dynamic-update-slice.10
  618.1 13.8 dynamic-update-slice.10
  639.7 13.8 dynamic-update-slice.10
  658.8 14.7 scatter_custom_fusion.3
  679.3 9.3 gather_fusion.9
  690.6 9.2 gather_fusion.11
  707.1 9.2 gather_fusion.12
  738.9 172.8 %while.5 = (s32[]{:T(128)}, f32[24,160000]{1,0:T(8,128)}, s32[8]{0:T(128)S(1)}, f32[8,160000]{1,0:T(8,128)}, s32[]{:T(128)}, /*index=5*/s32[2]{0:T(128)S(1)}, s32[1]{0:T(128)}, s32[]{:T(128)}) while((s32[]{:T(128)}, f32[24,160000]{1,0:T(8,128)}, s32[8]{0:T(128)S(1)}, f32[8,160000]{1,0:T(8,128)}, s32[]{:T(128)}, /*index=5*/s32[2]{0:T(128)S(1)}, ...), condition=%wide.while_cond.2, body=%wide.while_body.2.sunk | while | flops 320011 | bytes 3200135 | solution.py:83
  746.6 13.8 dynamic-update-slice.11
  768.2 13.8 dynamic-update-slice.11
  789.9 13.8 dynamic-update-slice.11
  811.5 13.8 dynamic-update-slice.11
  833.1 13.8 dynamic-update-slice.11
  854.7 13.8 dynamic-update-slice.11
  876.3 13.8 dynamic-update-slice.11
  897.9 13.8 dynamic-update-slice.11
  911.7 177.6 %fusion = f32[8,160000]{1,0:T(8,128)} fusion(f32[24,160000]{1,0:T(8,128)} %get-tuple-element.26), kind=kCustom, calls=%all-reduce-scatter | all-reduce-scatter fusion | flops 5120001 | bytes 20480512
  1103.3 58.2 %concatenate.3 = f32[14,160000]{1,0:T(8,128)} concatenate(f32[6,160000]{1,0:T(8,128)} %collective-permute-done.6, f32[8,160000]{1,0:T(8,128)} %fusion), dimensions={0} | concatenate | bytes 17920000
  1177.4 13.8 scatter_custom_fusion.7
  1196.0 14.0 scatter_fusion.2
  1223.7 14.0 scatter_custom_fusion.6
  1247.0 295.5 %all-reduce.5.cloned.1.call-done = f32[6,160000]{1,0:T(8,128)} async-done(((f32[6,160000]{1,0:T(8,128)}), f32[6,160000]{1,0:T(8,128)}) %all-reduce.5.cloned.1.call-update) | async-done | bytes 3840016
  (291 shorter events, 437.4 us)
Async XLA Ops:
  7.2 74.5 %all-gather.2.cloned.1.call-start = ((), (), s32[]{:S(2)}) async-start(), calls=%async_computation | async-start | bytes 12288000 | tf_op jit(solution)/shard_map/all_gather | solution.py:67
  7.9 1534.6 %all-reduce.5.cloned.1.call-start = ((), (), s32[]{:S(2)}) async-start(), calls=%async_computation.1 | async-start | bytes 10240000
  8.7 1.9 copy-start.40
  8.7 1.9 copy-start.43
  13.6 1.7 copy-start.37
  15.4 37.8 %copy-start.35 = (s32[2048,1]{0,1:T(1,128)}, s32[2048,1]{0,1:T(1,128)S(1)}, u32[]{:S(2)}) copy-start(s32[2048,1]{0,1:T(1,128)S(1)} %get-tuple-element.89) | copy-start | bytes 24580
  28.6 4.2 copy-start.31
  43.3 10.5 copy-start.34
  86.2 5.1 copy-start.5
  91.3 1.6 copy-start.23
  93.9 2.7 copy-start.6
  130.1 1.6 copy-start.15
  133.5 5.8 copy-start.9
  136.4 250.8 %collective-permute-start = (f32[1024,400]{0,1:T(8,128)}, f32[1024,400]{0,1:T(8,128)}, u32[]{:S(2)}, u32[]{:S(2)}) collective-permute-start(f32[1024,400]{0,1:T(8,128)} %copy.157), channel_id=1, source_target_pairs={{0,4},{4,8},{8,12},{12,16},{16,20},{20,24},{24,28},{28,32},{32,36}... | collective-permute-start | bytes 4915208 | tf_op jit(solution)/shard_map/ppermute | solution.py:15
  137.9 320.7 %collective-permute-start.1 = (f32[1024]{0:T(1024)S(1)}, f32[1024]{0:T(1024)S(1)}, u32[]{:S(2)}, u32[]{:S(2)}) collective-permute-start(f32[1024]{0:T(1024)S(1)} %get-tuple-element.82), channel_id=1, source_target_pairs={{0,4},{4,8},{8,12},{12,16},{16,20},{20,24},{24,28},{28,32},{32,36}... | collective-permute-start | bytes 12296 | tf_op jit(solution)/shard_map/ppermute | solution.py:15
  153.7 5.7 copy-start.30
  159.4 174.2 %copy-start.22 = (bf16[8,256,400]{1,2,0:T(8,128)(2,1)S(1)}, bf16[8,256,400]{1,2,0:T(8,128)(2,1)}, u32[]{:S(2)}) copy-start(bf16[8,256,400]{1,2,0:T(8,128)(2,1)} %fusion.9) | copy-start | bytes 4915204
  338.9 24.2 %copy-start.32 = (f32[1024]{0:T(1024)S(1)}, f32[1024]{0:T(1024)}, u32[]{:S(2)}) copy-start(f32[1024]{0:T(1024)} %param.11) | copy-start | bytes 12292
  362.8 2.8 copy-start
  362.8 2.3 copy-start.18
  389.1 9.3 copy-start.16
  405.7 9.2 copy-start.10
  415.0 4.4 copy-start.24
  420.3 1.9 copy-start.7
  458.3 1.6 copy-start.17
  461.6 4.4 copy-start.11
  464.5 224.1 %collective-permute-start.2 = (f32[1024,400]{0,1:T(8,128)}, f32[1024,400]{0,1:T(8,128)}, u32[]{:S(2)}, u32[]{:S(2)}) collective-permute-start(f32[1024,400]{0,1:T(8,128)} %copy.173), channel_id=1, source_target_pairs={{0,4},{4,8},{8,12},{12,16},{16,20},{20,24},{24,28},{28,32},{32,36}... | collective-permute-start | bytes 4915208 | tf_op jit(solution)/shard_map/ppermute | solution.py:15
  480.3 173.3 %copy-start.21 = (bf16[8,256,400]{1,2,0:T(8,128)(2,1)S(1)}, bf16[8,256,400]{1,2,0:T(8,128)(2,1)}, u32[]{:S(2)}) copy-start(bf16[8,256,400]{1,2,0:T(8,128)(2,1)} %fusion.6) | copy-start | bytes 4915204
  658.8 16.7 %copy-start.1 = (f32[1024,400]{1,0:T(8,128)S(1)}, f32[1024,400]{1,0:T(8,128)}, u32[]{:S(2)}) copy-start(f32[1024,400]{1,0:T(8,128)} %copy-done) | copy-start | bytes 4915204
  673.5 2.2 copy-start.19
  690.5 9.3 copy-start.13
  703.6 3.5 copy-start.33
  707.1 9.2 copy-start.12
  716.3 4.4 copy-start.25
  720.7 1.7 copy-start.3
  720.7 3.1 copy-start.8
  730.0 8.9 copy-start.42
  1089.3 7.9 copy-start.44
  1093.6 9.7 collective-permute-start.6
  1167.8 2.6 copy-start.4
  1168.6 41.6 %collective-permute-start.3 = (f32[1024]{0:T(1024)S(1)}, f32[1024]{0:T(1024)S(1)}, u32[]{:S(2)}, u32[]{:S(2)}) collective-permute-start(f32[1024]{0:T(1024)S(1)} %get-tuple-element.80), channel_id=1, source_target_pairs={{0,4},{4,8},{8,12},{12,16},{16,20},{20,24},{24,28},{28,32},{32,36}... | collective-permute-start | bytes 12296 | tf_op jit(solution)/shard_map/ppermute | solution.py:15
  1177.4 13.8 copy-start.29
  1210.0 1.6 copy-start.14
  1213.3 4.4 copy-start.45
  1213.3 5.6 copy-start.2
  1216.3 30.8 %collective-permute-start.4 = (f32[1024,400]{0,1:T(8,128)}, f32[1024,400]{0,1:T(8,128)}, u32[]{:S(2)}, u32[]{:S(2)}) collective-permute-start(f32[1024,400]{0,1:T(8,128)} %copy.187), channel_id=1, source_target_pairs={{0,4},{4,8},{8,12},{12,16},{16,20},{20,24},{24,28},{28,32},{32,36}... | collective-permute-start | bytes 4915208 | tf_op jit(solution)/shard_map/ppermute | solution.py:15
  1237.7 2.5 copy-start.26
  1237.7 9.4 collective-permute-start.5
  (7 other events, 6.3 us)
Sparse Core Ops, SparseCore 0:
  9.7 71.9 all-gather.1
  1168.0 374.4 all-reduce.4
where the time goes:
time: 1580 us; the launch traced here: 1550 us
  local copies, waits for them, and re-layouts  614 us (39%)
  other arithmetic  340 us (22%)
  waiting for transfers between devices  331 us (21%)
  blocking collectives  178 us (11%)
  matrix products  61.9 us (4%)
  between operations  16.5 us (1%)
    scatter-add x48, local copies, waits for them, and re-layouts  347 us
    unnamed x4, waiting for transfers between devices  301 us
    unnamed x1, blocking collectives  178 us
    scatter-add x48, other arithmetic  173 us
    unnamed x110, local copies, waits for them, and re-layouts  97.7 us
    scatter-add x3, other arithmetic, bucket_step(): jnp.zeros_like(left_rows).at[src].add(grad_heads.reshape(-1, width))  52.6 us
    scatter-add x3, other arithmetic, bucket_step(): right_grad.at[neg.reshape(-1)].add(grad_noise.reshape(-1, width))  42.3 us
    scatter-add x3, other arithmetic, bucket_step(): jnp.zeros_like(right_rows).at[dst].add(grad_tails.reshape(-1, width))  41.3 us
  transfers between devices with their start and end apart: 9, of which 4 were waited for; matrix products, arithmetic and copies ran while one was open for 42% of the time, Pallas kernels for 0%

commit v1 on v0

v1 whole, which is shorter than its diff:
```python
import functools
import jax
import jax.numpy as jnp
from jax import lax
from jax.experimental import pallas as pl
from jax.experimental.pallas import tpu as pltpu
from jax.sharding import PartitionSpec as P

BUCKETS = 3
STEP = 0.3
NT = (((1,), (1,)), ((), ()))
TN = (((0,), (0,)), ((), ()))
VMEM_LIMIT = 56 * 1024 * 1024


def onehot(index, rows):
    index = index.astype(jnp.int16)
    row = lax.broadcasted_iota(jnp.int16, (rows, index.shape[1]), 0)
    one = jnp.ones((), jnp.bfloat16)
    return jnp.where(row == index, one, jnp.zeros((), jnp.bfloat16))


def dot(a, b, dims=None):
    if dims is None:
        return jnp.dot(a, b, preferred_element_type=jnp.float32)
    return lax.dot_general(a, b, dims, preferred_element_type=jnp.float32)


def query_step(half_ref, src_ref, op_ref, s_ref, q_ref):
    width = half_ref.shape[0]
    hot = onehot(src_ref[0], half_ref.shape[1])
    s = dot(half_ref[...], hot).astype(jnp.bfloat16)
    s_ref[0] = s
    op = op_ref[0][:width, :width]
    q_ref[0] = dot(op, s, TN).astype(jnp.bfloat16)


def first_kernel(rel_ref, left_ref, src_ref, op_ref, s_ref, q_ref, half_ref):
    @pl.when(pl.program_id(0) == 0)
    def _():
        half_ref[...] = left_ref[...].astype(jnp.bfloat16)

    query_step(half_ref, src_ref, op_ref, s_ref, q_ref)


def first_call(rel, left, src, ops, nblk):
    width, rows = left.shape
    edges = src.shape[-1]
    pad = ops.shape[1:]
    part = lambda k, rel: (k, 0, 0)
    return pl.pallas_call(
        first_kernel,
        grid_spec=pltpu.PrefetchScalarGridSpec(
            num_scalar_prefetch=1,
            grid=(nblk,),
            in_specs=[
                pl.BlockSpec((width, rows), lambda k, rel: (0, 0)),
                pl.BlockSpec((1, 1, edges), part),
                pl.BlockSpec((1,) + pad, lambda k, rel: (rel[k], 0, 0)),
            ],
            out_specs=[pl.BlockSpec((1, width, edges), part)] * 2,
            scratch_shapes=[pltpu.VMEM((width, rows), jnp.bfloat16)],
        ),
        out_shape=[jax.ShapeDtypeStruct((nblk, width, edges), jnp.bfloat16)] * 2,
        compiler_params=pltpu.CompilerParams(vmem_limit_bytes=VMEM_LIMIT),
        name="first_queries",
    )(rel, left, src, ops)


def right_kernel(right_ref, acc_ref, q_ref, tgt_ref, neg_ref, p_ref, new_ref, newacc_ref, half_ref, grad_ref):
    k = pl.program_id(0)
    width, rows = right_ref.shape
    edges = q_ref.shape[2]

    @pl.when(k == 0)
    def _():
        half_ref[...] = right_ref[...].astype(jnp.bfloat16).T
        grad_ref[...] = jnp.zeros_like(grad_ref)

    q = q_ref[0]
    score = dot(half_ref[...], q)
    hits = onehot(neg_ref[0], rows)
    count = dot(hits, jnp.ones((hits.shape[1], 128), jnp.bfloat16)) * (1.0 / hits.shape[1])
    count = jnp.concatenate([count] * (edges // 128), axis=1)
    row = lax.broadcasted_iota(jnp.int32, (rows, edges), 0)
    hit = jnp.where(row == tgt_ref[0], 1.0, 0.0)
    sig = 0.5 * jnp.tanh(0.5 * score) + 0.5
    push = (sig * (count + hit) - hit).astype(jnp.bfloat16)
    p_ref[0] = push
    grad_ref[...] += dot(q, push, NT)

    @pl.when(k == pl.num_programs(0) - 1)
    def _():
        grad = grad_ref[...]
        acc = acc_ref[...] + jnp.sum(grad * grad, axis=0, keepdims=True) * (1.0 / width)
        newacc_ref[...] = acc
        new = right_ref[...].astype(jnp.float32) - STEP * grad * lax.rsqrt(acc)
        new_ref[...] = new.astype(jnp.bfloat16)


def right_call(right, acc, q, tgt, neg):
    width, rows = right.shape
    nblk, _, edges = q.shape
    whole = lambda k: (0, 0)
    part = lambda k: (k, 0, 0)
    return pl.pallas_call(
        right_kernel,
        grid=(nblk,),
        in_specs=[
            pl.BlockSpec((width, rows), whole),
            pl.BlockSpec((1, rows), whole),
            pl.BlockSpec((1, width, edges), part),
            pl.BlockSpec((1, 1, edges), part),
            pl.BlockSpec((1, 1, neg.shape[-1]), part),
        ],
        out_specs=[
            pl.BlockSpec((1, rows, edges), part),
            pl.BlockSpec((width, rows), whole),
            pl.BlockSpec((1, rows), whole),
        ],
        out_shape=[
            jax.ShapeDtypeStruct((nblk, rows, edges), jnp.bfloat16),
            jax.ShapeDtypeStruct((width, rows), jnp.bfloat16),
            jax.ShapeDtypeStruct((1, rows), jnp.float32),
        ],
        scratch_shapes=[pltpu.VMEM((rows, width), jnp.bfloat16), pltpu.VMEM((width, rows), jnp.float32)],
        compiler_params=pltpu.CompilerParams(vmem_limit_bytes=VMEM_LIMIT),
        name="right_update",
    )(right, acc, q, tgt, neg)


def left_kernel(nblk, more, rel_ref, left_ref, acc_ref, right_ref, p_ref, src_ref, op_ref, *rest):
    if more:
        g_ref, new_ref, newacc_ref, s_ref, q_ref, rhalf_ref, half_ref, grad_ref = rest
    else:
        g_ref, new_ref, newacc_ref, rhalf_ref, half_ref, grad_ref = rest
    k = pl.program_id(0)
    width, rows = left_ref.shape

    @pl.when(k == 0)
    def _():
        rhalf_ref[...] = right_ref[...].astype(jnp.bfloat16)
        grad_ref[...] = jnp.zeros_like(grad_ref)

    @pl.when(k < nblk)
    def _():
        g = dot(rhalf_ref[...], p_ref[0]).astype(jnp.bfloat16)
        g_ref[0] = g
        back = dot(op_ref[0][:width, :width], g).astype(jnp.bfloat16)
        grad_ref[...] += dot(back, onehot(src_ref[0], rows), NT)

    @pl.when(k == nblk - 1)
    def _():
        grad = grad_ref[...]
        acc = acc_ref[...] + jnp.sum(grad * grad, axis=0, keepdims=True) * (1.0 / width)
        newacc_ref[...] = acc
        new = left_ref[...] - STEP * grad * lax.rsqrt(acc)
        new_ref[...] = new
        half_ref[...] = new.astype(jnp.bfloat16)

    if more:
        @pl.when(k >= nblk)
        def _():
            query_step(half_ref, src_ref, op_ref, s_ref, q_ref)


def left_call(rel, left, acc, right, p, src, ops, more):
    width, rows = left.shape
    nblk, _, edges = p.shape
    steps = 2 * nblk if more else nblk
    pad = ops.shape[1:]
    whole = lambda k, rel: (0, 0)
    early = lambda k, rel: (jnp.minimum(k, nblk - 1), 0, 0)
    late = lambda k, rel: (jnp.maximum(k - nblk, 0), 0, 0)
    out_specs = [
        pl.BlockSpec((1, width, edges), early),
        pl.BlockSpec((width, rows), whole),
        pl.BlockSpec((1, rows), whole),
    ]
    out_shape = [
        jax.ShapeDtypeStruct((nblk, width, edges), jnp.bfloat16),
        jax.ShapeDtypeStruct((width, rows), jnp.float32),
        jax.ShapeDtypeStruct((1, rows), jnp.float32),
    ]
    if more:
        out_specs += [pl.BlockSpec((1, width, edges), late)] * 2
        out_shape += [jax.ShapeDtypeStruct((nblk, width, edges), jnp.bfloat16)] * 2
    return pl.pallas_call(
        functools.partial(left_kernel, nblk, more),
        grid_spec=pltpu.PrefetchScalarGridSpec(
            num_scalar_prefetch=1,
            grid=(steps,),
            in_specs=[
                pl.BlockSpec((width, rows), whole),
                pl.BlockSpec((1, rows), whole),
                pl.BlockSpec((width, rows), whole),
                pl.BlockSpec((1, rows, edges), early),
                pl.BlockSpec((1, 1, edges), lambda k, rel: (k, 0, 0)),
                pl.BlockSpec((1,) + pad, lambda k, rel: (rel[k], 0, 0)),
            ],
            out_specs=out_specs,
            scratch_shapes=[
                pltpu.VMEM((width, rows), jnp.bfloat16),
                pltpu.VMEM((width, rows), jnp.bfloat16),
                pltpu.VMEM((width, rows), jnp.float32),
            ],
        ),
        out_shape=out_shape,
        compiler_params=pltpu.CompilerParams(vmem_limit_bytes=VMEM_LIMIT),
        cost_estimate=pl.CostEstimate(flops=2 * steps * 320_000_000, bytes_accessed=16_000_000, transcendentals=0),
        name="left_update",
    )(rel, left, acc, right, p, src, ops)


def opgrad_kernel(rel_ref, *refs):
    s_refs, g_refs, out_ref, acc_ref, count_ref, list_ref = refs[:3], refs[3:6], refs[6], refs[7], refs[8], refs[9]
    j = pl.program_id(0)
    nblk = s_refs[0].shape[0]
    width = s_refs[0].shape[1]
    acc_ref[...] = jnp.zeros_like(acc_ref)
    for t in range(3):
        def add(k, carry):
            @pl.when(rel_ref[t * nblk + k] == j)
            def _():
                acc_ref[...] += dot(s_refs[t][k], g_refs[t][k], NT)
            return carry
        lax.fori_loop(0, nblk, add, 0)
    out_ref[0, 0, 0, :, :width] = acc_ref[...].astype(jnp.bfloat16)
    out_ref[0, 0, 0, :, width:] = jnp.zeros((width, out_ref.shape[-1] - width), jnp.bfloat16)


def opgrad_call(rel, s, g, nrel):
    nblk, width, edges = s[0].shape
    whole = pl.BlockSpec((nblk, width, edges), lambda j, rel: (0, 0, 0))

    def place(j, rel):
        owner, i = j // 6, j % 6
        return (owner % 2, i // 2, (owner // 2) * 2 + i % 2, 0, 0)

    return pl.pallas_call(
        opgrad_kernel,
        grid_spec=pltpu.PrefetchScalarGridSpec(
            num_scalar_prefetch=1,
            grid=(nrel,),
            in_specs=[whole] * 6,
            out_specs=pl.BlockSpec((1, 1, 1, width, 512), place),
            scratch_shapes=[pltpu.VMEM((width, width), jnp.float32), pltpu.SMEM((nrel,), jnp.int32), pltpu.SMEM((nrel, 24), jnp.int32)],
        ),
        out_shape=jax.ShapeDtypeStruct((2, 3, 4, width, 512), jnp.bfloat16),
        compiler_params=pltpu.CompilerParams(vmem_limit_bytes=VMEM_LIMIT),
        name="operator_gradients",
    )(rel, *s, *g)
MESH = pl.DeviceIdType.MESH
UNITS = 4
UNIT_ROWS = 112
LANES = 512


def place():
    b, r = lax.axis_index("blk"), lax.axis_index("rel")
    return b // 8, (b // 4) % 2, b % 4, r // 2, r % 2


def device(z, ylo, x, yhi, core):
    return (z * 8 + ylo * 4 + x, yhi * 2 + core)


def greet(peers):
    barrier = pltpu.get_barrier_semaphore()
    for peer in peers:
        pl.semaphore_signal(barrier, inc=1, device_id=peer, device_id_type=MESH)
    pl.semaphore_wait(barrier, len(peers))


def send(src, dst, sems, index, peer):
    copy = pltpu.make_async_remote_copy(
        src_ref=src,
        dst_ref=dst,
        send_sem=sems[0].at[index],
        recv_sem=sems[1].at[index],
        device_id=peer,
        device_id_type=MESH,
    )
    copy.start()
    return copy


def gather_kernel(own_ref, table_ref, own_sem, cross_s, cross_r, ring_s, ring_r, whole_s, whole_r, pass_s, pass_r):
    z, ylo, x, yhi, core = place()
    me = yhi * 2 + core
    far = (1 - yhi) * 2 + core
    count = own_ref.shape[0]
    third = count // 8
    sibling = device(z, ylo, x, yhi, 1 - core)
    cross = device(z, 1 - ylo, x, 1 - yhi, core)
    x_ring = [device(z, ylo, (x + d) % 4, yhi, core) for d in (1, 2, 3)]
    z_ring = [device((z + d) % 4, ylo, x, yhi, core) for d in (1, 2, 3)]
    greet([sibling, cross] + x_ring + z_ring)

    here = pltpu.make_async_copy(own_ref, table_ref.at[pl.ds(me * count, count)], own_sem)
    here.start()
    copies = []
    first = [x * third, count // 2 + z * third]
    arrivals = {}
    for i in range(third):
        for ring in range(2):
            unit = first[ring] + i
            arrivals[ring, i] = send(
                own_ref.at[unit], table_ref.at[me * count + unit], (cross_s, cross_r), ring * third + i, cross
            )
    copies.append(
        send(own_ref, table_ref.at[pl.ds(me * count, count)], (whole_s, whole_r), 0, sibling)
    )
    rings = (x_ring, z_ring)
    landed = {}
    for i in range(third):
        for ring in range(2):
            arrivals[ring, i].wait()
            slot = far * count + first[ring] + i
            for d in (2, 1, 3):
                landed[ring, d, i] = send(
                    table_ref.at[slot], table_ref.at[slot], (ring_s, ring_r), (ring * 3 + d - 1) * third + i, rings[ring][d - 1]
                )
            copies.append(
                send(table_ref.at[slot], table_ref.at[slot], (pass_s, pass_r), ring * 4 * third + i, sibling)
            )
    for i in range(third):
        for ring in range(2):
            for d in (1, 3, 2):
                landed[ring, d, i].wait()
                axis = (x, z)[ring]
                behind = (axis - d + 4) % 4
                slot = far * count + ring * (count // 2) + behind * third + i
                copies.append(
                    send(table_ref.at[slot], table_ref.at[slot], (pass_s, pass_r), (ring * 4 + d) * third + i, sibling)
                )
    here.wait()
    for copy in copies:
        copy.wait()


def gather_call(own, owners):
    count = own.shape[0]
    third = count // 8
    dma = lambda n: [pltpu.SemaphoreType.DMA((n,))] * 2
    return pl.pallas_call(
        gather_kernel,
        in_specs=[pl.BlockSpec(memory_space=pl.ANY)],
        out_specs=pl.BlockSpec(memory_space=pl.ANY),
        out_shape=jax.ShapeDtypeStruct((owners * count,) + own.shape[1:], own.dtype),
        scratch_shapes=[pltpu.SemaphoreType.DMA] + dma(2 * third) + dma(6 * third) + dma(1) + dma(8 * third),
        compiler_params=pltpu.CompilerParams(collective_id=0, has_side_effects=True),
        name="gather_operators",
    )(own)


def row_of(t):
    return 25 * t // 2


def last_window(s, t):
    if s == 0:
        base, top = 96 * (t // 8) + 48 * ((t // 4) % 2), 48
    elif s == 1:
        base, top = 192 * (t // 16) + 48 * ((t // 4) % 4), 48
    else:
        z = (t // 2) % 4
        base, top = 96 * (t // 8) + 16 * z + 16 * (z // 2), 32
    part = row_of(t) - base
    local = 16 * (part // 16) - 16 * (part // top)
    return base + local, local


def window(start, size):
    return pl.ds(pl.multiple_of(start, 16), size)


def total(out, own, parts):
    value = own.astype(jnp.float32)
    for part in parts:
        value = value + part.astype(jnp.float32)
    out[...] = value.astype(out.dtype)


def reduce_kernel(
    grads_ref, out_ref, own, near,
    a0, b0, c0, a1, b1, c1, a2, b2, c2, m0, n0, m1, n1, m2, n2, own_sem, send_sem, recv_sem,
):
    z, ylo, x, yhi, core = place()
    sems = (send_sem, recv_sem)
    sibling = device(z, ylo, x, yhi, 1 - core)
    z_at = [(z + d) % 4 for d in (1, 2, 3)]
    x_at = [(x + d) % 4 for d in (1, 2, 3)]
    y_at = [(yhi, 1 - ylo), (1 - yhi, ylo), (1 - yhi, 1 - ylo)]
    z_ring = [device(v, ylo, x, yhi, core) for v in z_at]
    x_ring = [device(z, ylo, v, yhi, core) for v in x_at]
    y_ring = [device(z, v, x, h, core) for h, v in y_at]
    greet([sibling] + z_ring + x_ring + y_ring)

    mine, pairs = [], []
    for s in range(3):
        pairs.append(send(grads_ref.at[1 - core, s], near.at[s], sems, s, sibling))
        mine.append(pltpu.make_async_copy(grads_ref.at[core, s], own.at[s], own_sem.at[s]))
        mine[-1].start()

    first = []
    for s in range(3):
        mine[s].wait()
        pairs[s].wait()
        for i in range(4):
            total(own.at[s, i], own[s, i], [near[s, i]])
        for d in range(3):
            if s == 0:
                src = own.at[s, :, window(96 * z_at[d], 112)]
                copy = send(src, a0.at[d], sems, 3 + s * 3 + d, z_ring[d])
            elif s == 1:
                h, v = y_at[d]
                src = own.at[s, pl.ds(2 * h, 2), window(192 * v, 208)]
                copy = send(src, a1.at[d], sems, 3 + s * 3 + d, y_ring[d])
            else:
                src = own.at[s, :, window(96 * x_at[d], 112)]
                copy = send(src, a2.at[d], sems, 3 + s * 3 + d, x_ring[d])
            first.append(copy)

    second = []
    for s in range(3):
        for d in range(3):
            first[s * 3 + d].wait()
        if s == 0:
            total(m0, own[s, :, window(96 * z, 112)], [a0[d] for d in range(3)])
        elif s == 1:
            total(m1, own[s, pl.ds(2 * yhi, 2), window(192 * ylo, 208)], [a1[d] for d in range(3)])
        else:
            total(m2, own[s, :, window(96 * x, 112)], [a2[d] for d in range(3)])
        for d in range(3):
            if s == 0:
                h, v = y_at[d]
                copy = send(m0.at[pl.ds(2 * h, 2), window(48 * v, 64)], b0.at[d], sems, 12 + s * 3 + d, y_ring[d])
            elif s == 1:
                copy = send(m1.at[:, window(48 * x_at[d], 64)], b1.at[d], sems, 12 + s * 3 + d, x_ring[d])
            else:
                v = z_at[d]
                copy = send(m2.at[:, window(16 * v + 16 * (v // 2), 48)], b2.at[d], sems, 12 + s * 3 + d, z_ring[d])
            second.append(copy)

    third = []
    for s in range(3):
        for d in range(3):
            second[s * 3 + d].wait()
        if s == 0:
            total(n0, m0[pl.ds(2 * yhi, 2), window(48 * ylo, 64)], [b0[d] for d in range(3)])
        elif s == 1:
            total(n1, m1[:, window(48 * x, 64)], [b1[d] for d in range(3)])
        else:
            total(n2, m2[:, window(16 * z + 16 * (z // 2), 48)], [b2[d] for d in range(3)])
        for d in range(3):
            if s == 0:
                _, at = last_window(0, z * 8 + ylo * 4 + x_at[d])
                copy = send(n0.at[:, window(at, 32)], c0.at[d], sems, 21 + s * 3 + d, x_ring[d])
            elif s == 1:
                _, at = last_window(1, ylo * 16 + x * 4 + z_at[d])
                copy = send(n1.at[:, window(at, 32)], c1.at[d], sems, 21 + s * 3 + d, z_ring[d])
            else:
                h, v = y_at[d]
                _, at = last_window(2, x * 8 + z * 2 + v)
                copy = send(n2.at[pl.ds(2 * h, 2), window(at, 32)], c2.at[d], sems, 21 + s * 3 + d, y_ring[d])
            third.append(copy)

    for s in range(3):
        for d in range(3):
            third[s * 3 + d].wait()
        if s == 0:
            _, at = last_window(0, z * 8 + ylo * 4 + x)
            total(out_ref.at[s], n0[:, window(at, 32)], [c0[d] for d in range(3)])
        elif s == 1:
            _, at = last_window(1, ylo * 16 + x * 4 + z)
            total(out_ref.at[s], n1[:, window(at, 32)], [c1[d] for d in range(3)])
        else:
            _, at = last_window(2, x * 8 + z * 2 + ylo)
            total(out_ref.at[s], n2[pl.ds(2 * yhi, 2), window(at, 32)], [c2[d] for d in range(3)])


def reduce_call(grads):
    _, _, four, rows, lanes = grads.shape
    buf = lambda *shape: pltpu.VMEM(shape + (lanes,), jnp.bfloat16)
    return pl.pallas_call(
        reduce_kernel,
        in_specs=[pl.BlockSpec(memory_space=pl.ANY)],
        out_specs=pl.BlockSpec(memory_space=pltpu.VMEM),
        out_shape=jax.ShapeDtypeStruct((3, 2, 32, lanes), jnp.float32),
        scratch_shapes=[
            buf(3, four, rows), buf(3, four, rows),
            buf(3, 4, 112), buf(3, 2, 64), buf(3, 2, 32),
            buf(3, 2, 208), buf(3, 2, 64), buf(3, 2, 32),
            buf(3, 4, 112), buf(3, 4, 48), buf(3, 2, 32),
            buf(4, 112), buf(2, 64), buf(2, 208), buf(2, 64), buf(4, 112), buf(4, 48),
            pltpu.SemaphoreType.DMA((3,)), pltpu.SemaphoreType.DMA((30,)), pltpu.SemaphoreType.DMA((30,)),
        ],
        compiler_params=pltpu.CompilerParams(
            collective_id=1, has_side_effects=True, vmem_limit_bytes=VMEM_LIMIT
        ),
        name="reduce_operator_gradients",
    )(grads)


def final_share(pieces, width):
    blk = lax.axis_size("blk")
    place_1 = lambda b: ((b // 4) % 2) * 16 + (b % 4) * 4 + b // 8
    place_2 = lambda b: (b % 4) * 8 + (b // 8) * 2 + (b // 4) % 2
    t = lax.axis_index("blk")
    shares = []
    for s, at in enumerate((None, place_1, place_2)):
        piece = pieces[s, :, :, :width]
        if at is not None:
            piece = lax.ppermute(piece, "blk", [(b, at(b)) for b in range(blk)])
        start, _ = last_window(s, t)
        skip = t * (width * width // blk) - start * width
        flat = piece.reshape(2, 32 * width)
        shares.append(lax.dynamic_slice(flat, (0, skip), (2, width * width // blk)))
    return jnp.concatenate(shares, axis=0)


def from_behind(value, axis, steps):
    count = lax.axis_size(axis)
    pairs = [(source, (source + steps) % count) for source in range(count)]
    return lax.ppermute(value, axis, pairs)


def body(left, left_state, right, right_state, operators, need_list, block_slot, sources, targets, negatives):
    owned_count, width, _ = operators.shape
    owners = lax.axis_size("rel")
    nblk = block_slot.shape[-1]
    nrel = owned_count * owners
    rel = need_list[0].reshape(-1)[block_slot[0].reshape(-1)]
    src = sources[0].reshape(BUCKETS * nblk, 1, -1)
    tgt = targets[0].reshape(BUCKETS * nblk, 1, -1)
    neg = negatives[0].reshape(BUCKETS * nblk, 1, -1)
    padded = UNITS * UNIT_ROWS
    own = jnp.pad(operators, ((0, 0), (0, padded - width), (0, LANES - width)))
    table = gather_call(own.reshape(owned_count * UNITS, UNIT_ROWS, LANES), owners)
    ops = table.reshape(nrel, padded, LANES)
    L, LS, R, RS = left.T, left_state[None], right.T, right_state[None]
    s, q = first_call(rel[:nblk], L, src[:nblk], ops, nblk)
    heads, grads = [s], []
    for t in range(BUCKETS):
        at = slice(nblk * t, nblk * t + nblk)
        p, fresh, fresh_acc = right_call(R, RS, q, tgt[at], neg[at])
        moved = from_behind((fresh, fresh_acc), "blk", 1)
        more = t + 1 < BUCKETS
        both = slice(nblk * t, nblk * (t + (2 if more else 1)))
        out = left_call(rel[both], L, LS, R, p, src[both], ops, more)
        grads.append(out[0])
        L, LS = out[1:3]
        if more:
            heads.append(out[3])
            q = out[4]
        R, RS = moved
    partial = opgrad_call(rel, heads, grads, nrel)
    op_grad = final_share(reduce_call(partial), width)
    return (L.T, LS[0], R.T.astype(jnp.float32), RS[0], op_grad)


def solution(mesh):
    in_specs = (
        P(("blk", "rel"), None),
        P(("blk", "rel")),
        P(("blk", "rel"), None),
        P(("blk", "rel")),
        P("rel", None, None),
        P(("blk", "rel"), None, None),
        P(("blk", "rel"), None, None),
        P(("blk", "rel"), None, None),
        P(("blk", "rel"), None, None),
        P(("blk", "rel"), None, None, None),
    )
    out_specs = (
        P(("blk", "rel"), None),
        P(("blk", "rel")),
        P(("blk", "rel"), None),
        P(("blk", "rel")),
        P("rel", "blk"),
    )
    return jax.shard_map(body, mesh=mesh, in_specs=in_specs, out_specs=out_specs, check_vma=False)
```

time: 1580 us -> 320 us (0.20); the launches traced: 1550 us -> 317 us
  local copies, waits for them, and re-layouts: 614 us -> 15.2 us
  other arithmetic: 340 us -> 2.79 us
  waiting for transfers between devices: 331 us -> 6.28 us
  Pallas kernels: 0 us -> 276 us
  blocking collectives: 178 us -> 0 us
  matrix products: 61.9 us -> 0 us
    scatter-add x48 -> x0, local copies, waits for them, and re-layouts: 347 us -> none
    scatter-add x57 -> x0, other arithmetic: 309 us -> none
    unnamed x4 -> x0, waiting for transfers between devices: 301 us -> none
    pallas_call x0 -> x10, Pallas kernels: none -> 276 us  [the longest x1 89.5 us: gather_call(): pl.pallas_call(gather_kernel, in_specs=[pl.BlockSpec(memory_space=pl.ANY)...]
    unnamed x1 -> x0, blocking collectives: 178 us -> none
    gather x16 -> x1, local copies, waits for them, and re-layouts: 112 us -> 0.7 us  [body(): rel = need_list[0].reshape(-1)[block_slot[0].reshape(-1)]]
    unnamed x110 -> x20, local copies, waits for them, and re-layouts: 97.7 us -> 4.26 us
    reshape x6 -> x2, local copies, waits for them, and re-layouts: 38.7 us -> 0.37 us  [final_share(): flat = piece.reshape(2, 32 * width)]
  transfers between devices with their start and end apart: 9 -> 8, of which waited for: 4 -> 1; matrix products, arithmetic and copies ran while one was open for 42% -> 2% of each run, Pallas kernels for 0% -> 44%
where the time goes in v1:
time: 320 us; the launch traced here: 317 us
  Pallas kernels  276 us (86%)
  starting transfers between devices  16.5 us (5%)
  local copies, waits for them, and re-layouts  15.2 us (5%)
  waiting for transfers between devices  6.28 us (2%)
    pallas_call x1, Pallas kernels, gather_call(): pl.pallas_call(gather_kernel, in_specs=[pl.BlockSpec(memory_space=pl.ANY)...  89.5 us
    pallas_call x3, Pallas kernels, left_call(): pl.pallas_call(functools.partial(left_kernel, nblk, more), grid_spec=pltp...  60.7 us
    pallas_call x1, Pallas kernels, reduce_call(): pl.pallas_call(reduce_kernel, in_specs=[pl.BlockSpec(memory_space=pl.ANY)...  54 us
    pallas_call x3, Pallas kernels, right_call(): pl.pallas_call(right_kernel, grid=(nblk,), in_specs=[pl.BlockSpec((width,...  34.8 us
    pallas_call x1, Pallas kernels, opgrad_call(): pl.pallas_call(opgrad_kernel, grid_spec=pltpu.PrefetchScalarGridSpec(num_...  26.1 us
    pallas_call x1, Pallas kernels, first_call(): pl.pallas_call(first_kernel, grid_spec=pltpu.PrefetchScalarGridSpec(num_s...  10.4 us
    ppermute x6, starting transfers between devices, from_behind(): return lax.ppermute(value, axis, pairs)  8.26 us
    ppermute x2, starting transfers between devices, final_share(): piece = lax.ppermute(piece, 'blk', [(b, at(b)) for b in range(blk)])  8.25 us
  transfers between devices with their start and end apart: 8, of which 1 were waited for; matrix products, arithmetic and copies ran while one was open for 2% of the time, Pallas kernels for 44%

profile of v1, /device:TPU:8, one launch (start us, length us, event | category | flops | bytes accessed | tf_op | source)
XLA Modules:
  0.0 317.2 jit_solution(11879703033696282015)
XLA Ops:
  0.6 0.8 reshape_squeeze.12
  1.4 0.7 reduce
  2.1 0.1 reshape_squeeze.13
  2.2 0.7 gather_fusion
  2.9 0.6 fusion.6
  3.5 1.3 fusion.2
  4.8 3.7 %pad.4 = bf16[6,448,512]{2,1,0:T(8,128)(2,1)} pad(bf16[6,400,400]{2,1,0:T(8,128)(2,1)} %param.14, bf16[]{:T(256)} %constant.134.clone.1), padding=0_0x0_48x0_112 | pad | bytes 4672514 | tf_op jit(solution)/shard_map/jit(_pad)/pad | solution.py:539
  8.5 89.5 %gather_operators.1 = bf16[96,112,512]{2,1,0:T(8,128)(2,1)} custom-call(bf16[24,112,512]{2,1,0:T(8,128)(2,1)} %bitcast.39), custom_call_target="tpu_custom_call" | custom-call | tf_op jit(solution)/shard_map/gather_operators/pallas_call | solution.py:346
  98.0 0.6 fusion.4
  98.6 0.6 copy.29
  99.2 10.4 %first_queries.1 = (bf16[8,400,256]{2,1,0:T(8,128)(2,1)}, bf16[8,400,256]{2,1,0:T(8,128)(2,1)}) custom-call(s32[8]{0:T(128)} %get-tuple-element.66.rel_ref, f32[400,1024]{1,0:T(8,128)} %bitcast.42, s32[8,1,256]{2,1,0:T(1,128)} %bitcast.50, bf16[24,448,512]{2,1,0:T(8,128)(2,1)} %bitcast.35), custom_call_target="tpu_custom_call" | custom-call | tf_op jit(solution)/shard_map/first_queries/pallas_call | solution.py:51
  109.6 11.7 %right_update.3 = (bf16[8,1024,256]{2,1,0:T(8,128)(2,1)}, bf16[400,1024]{1,0:T(8,128)(2,1)}, f32[1,1024]{1,0:T(1,128)}) custom-call(f32[400,1024]{1,0:T(8,128)} %bitcast.40, f32[1,1024]{1,0:T(1,128)} %bitcast.54, bf16[8,400,256]{2,1,0:T(8,128)(2,1)} %get-tuple-element.29.q_ref, s32[8,1,256]{2,1,0:T(1,128)} %bitcast.49, s32[8,1,256]{2,1,0:T(1,128)} %bitcast.46), custom_call_target="tpu_custom_call" | custom-call | tf_op jit(solution)/shard_map/right_update/pallas_call | solution.py:106
  121.3 1.6 collective-permute-start
  122.9 1.5 collective-permute-start.1
  124.4 0.7 fusion.7
  125.0 0.6 fusion.5
  125.7 23.0 %left_update.3 = (bf16[8,400,256]{2,1,0:T(8,128)(2,1)}, f32[400,1024]{1,0:T(8,128)}, f32[1,1024]{1,0:T(1,128)}, bf16[8,400,256]{2,1,0:T(8,128)(2,1)}, bf16[8,400,256]{2,1,0:T(8,128)(2,1)}) custom-call(s32[16]{0:T(128)} %get-tuple-element.68.rel_ref, f32[400,1024]{1,0:T(8,128)} %bitcast.43, f32[1,1024]{1,0:T(1,128)} %bitcast.56, f32[400,1024]{1,0:T(8,128)} %bitcast.41, ...), custom_call_target="tpu_custom_call" | custom-call | flops 10240000000 | bytes 16000000 | tf_op jit(solution)/shard_map/left_update/pallas_call | solution.py:188
  148.8 0.6 copy.28
  149.4 0.6 copy.27
  150.0 0.0 collective-permute-done.right_ref
  150.0 0.6 copy-done.6
  150.6 0.4 copy-done
  151.0 11.5 %right_update.4 = (bf16[8,1024,256]{2,1,0:T(8,128)(2,1)}, bf16[400,1024]{1,0:T(8,128)(2,1)}, f32[1,1024]{1,0:T(1,128)}) custom-call(bf16[400,1024]{1,0:T(8,128)(2,1)} %copy-done, f32[1,1024]{1,0:T(1,128)} %copy-done.6, bf16[8,400,256]{2,1,0:T(8,128)(2,1)} %get-tuple-element.35.q_ref, s32[8,1,256]{2,1,0:T(1,128)} %bitcast.48, s32[8,1,256]{2,1,0:T(1,128)} %bitcast.45), custom_call_target="tpu_custom_call" | custom-call | tf_op jit(solution)/shard_map/right_update/pallas_call | solution.py:106
  162.5 1.4 collective-permute-start.2
  164.0 0.7 collective-permute-start.3
  164.6 23.0 %left_update.4 = (bf16[8,400,256]{2,1,0:T(8,128)(2,1)}, f32[400,1024]{1,0:T(8,128)}, f32[1,1024]{1,0:T(1,128)}, bf16[8,400,256]{2,1,0:T(8,128)(2,1)}, bf16[8,400,256]{2,1,0:T(8,128)(2,1)}) custom-call(s32[16]{0:T(128)} %get-tuple-element.69.rel_ref, f32[400,1024]{1,0:T(8,128)} %get-tuple-element.31.left_ref, f32[1,1024]{1,0:T(1,128)} %get-tuple-element.32.acc_ref, ...), custom_call_target="tpu_custom_call" | custom-call | flops 10240000000 | bytes 16000000 | tf_op jit(solution)/shard_map/left_update/pallas_call | solution.py:188
  187.6 0.0 copy-start.7
  187.7 0.6 copy-done.7
  188.2 0.3 copy-done.1
  188.5 11.6 %right_update.5 = (bf16[8,1024,256]{2,1,0:T(8,128)(2,1)}, bf16[400,1024]{1,0:T(8,128)(2,1)}, f32[1,1024]{1,0:T(1,128)}) custom-call(bf16[400,1024]{1,0:T(8,128)(2,1)} %copy-done.1, f32[1,1024]{1,0:T(1,128)} %copy-done.7, bf16[8,400,256]{2,1,0:T(8,128)(2,1)} %get-tuple-element.41.q_ref, s32[8,1,256]{2,1,0:T(1,128)} %bitcast.47, s32[8,1,256]{2,1,0:T(1,128)} %bitcast.44), custom_call_target="tpu_custom_call" | custom-call | tf_op jit(solution)/shard_map/right_update/pallas_call | solution.py:106
  200.1 1.5 collective-permute-start.4
  201.6 1.6 collective-permute-start.5
  203.2 14.7 %left_update.5 = (bf16[8,400,256]{2,1,0:T(8,128)(2,1)}, f32[400,1024]{1,0:T(8,128)}, f32[1,1024]{1,0:T(1,128)}) custom-call(s32[8]{0:T(128)} %get-tuple-element.67.rel_ref, f32[400,1024]{1,0:T(8,128)} %get-tuple-element.37.left_ref, f32[1,1024]{1,0:T(1,128)} %get-tuple-element.38.acc_ref, bf16[400,1024]{1,0:T(8,128)(2,1)} %copy-done.1, ...), custom_call_target="tpu_custom_call" | custom-call | flops 5120000000 | bytes 16000000 | tf_op jit(solution)/shard_map/left_update/pallas_call | solution.py:188
  217.9 26.1 %operator_gradients.1.grads_ref = bf16[2,3,4,400,512]{4,3,2,1,0:T(8,128)(2,1)} custom-call(s32[24]{0:T(128)} %copy-done.5, bf16[8,400,256]{2,1,0:T(8,128)(2,1)} %get-tuple-element.47.refs_0_, bf16[8,400,256]{2,1,0:T(8,128)(2,1)} %get-tuple-element.48.refs_1_, bf16[8,400,256]{2,1,0:T(8,128)(2,1)} %get-tuple-element.49.refs_2_, ...), custom_call_target="tpu_custom_call" | custom-call | tf_op jit(solution)/shard_map/operator_gradients/pallas_call | solution.py:240
  244.0 54.0 %reduce_operator_gradients.1 = f32[3,2,32,512]{3,2,1,0:T(8,128)} custom-call(bf16[2,3,4,400,512]{4,3,2,1,0:T(8,128)(2,1)} %operator_gradients.1.grads_ref), custom_call_target="tpu_custom_call" | custom-call | tf_op jit(solution)/shard_map/reduce_operator_gradients/pallas_call | solution.py:486
  298.0 1.1 fusion.1
  299.1 2.2 collective-permute-start.7
  301.3 6.1 %collective-permute-start.6 = (f32[2,32,400]{2,1,0:T(8,128)S(1)}, f32[2,32,400]{2,1,0:T(8,128)S(1)}, u32[]{:S(2)}, u32[]{:S(2)}) collective-permute-start(f32[2,32,400]{2,1,0:T(8,128)S(1)} %get-tuple-element.55), channel_id=1, source_target_pairs={{0,0},{4,16},{8,32},{12,48},{16,64},{20,80},{24,96},{28,112},{32,4... | collective-permute-start | bytes 307208 | tf_op jit(solution)/shard_map/ppermute | solution.py:515
  307.4 0.2 reshape_squeeze.14
  307.5 0.1 constant_dynamic-slice_fusion.2
  307.7 6.3 %collective-permute-done.7 = f32[2,32,400]{2,1,0:T(8,128)S(1)} collective-permute-done((f32[2,32,400]{2,1,0:T(8,128)S(1)}, f32[2,32,400]{2,1,0:T(8,128)S(1)}, u32[]{:S(2)}, u32[]{:S(2)}) %collective-permute-start.7) | collective-permute-done | bytes 102432 | tf_op jit(solution)/shard_map/ppermute | solution.py:515
  313.9 0.2 reshape.63
  314.1 0.1 constant_dynamic-slice_fusion
  314.2 0.2 reshape.62
  314.4 0.1 constant_dynamic-slice_fusion.1
  314.5 0.7 pad_maximum_fusion
  315.3 1.3 convert_bitcast_fusion
  316.6 0.6 copy.31
  (20 shorter events, 0.1 us)
Async XLA Ops:
  2.9 121.5 %copy-start.5 = (s32[24]{0:T(128)}, s32[24]{0:T(128)S(1)}, u32[]{:S(2)}) copy-start(s32[24]{0:T(128)S(1)} %gather_fusion) | copy-start | bytes 292
  8.5 89.5 %copy-start.3 = (s32[1,3,2048]{2,0,1:T(1,128)S(1)}, s32[1,3,2048]{2,0,1:T(1,128)}, u32[]{:S(2)}) copy-start(s32[1,3,2048]{2,0,1:T(1,128)} %param.18) | copy-start | bytes 73732
  8.5 90.1 %copy-start.4 = (s32[1,3,8,256]{3,2,1,0:T(8,128)S(1)}, s32[1,3,8,256]{3,2,1,0:T(8,128)}, u32[]{:S(2)}) copy-start(s32[1,3,8,256]{3,2,1,0:T(8,128)} %param.19) | copy-start | bytes 73732
  109.6 15.5 %copy-start.2 = (s32[1,3,2048]{2,0,1:T(1,128)S(1)}, s32[1,3,2048]{2,0,1:T(1,128)}, u32[]{:S(2)}) copy-start(s32[1,3,2048]{2,0,1:T(1,128)} %param.17) | copy-start | bytes 73732
  121.3 28.7 %collective-permute-start = (bf16[400,1024]{1,0:T(8,128)(2,1)}, bf16[400,1024]{1,0:T(8,128)(2,1)S(1)}, u32[]{:S(2)}, u32[]{:S(2)}) collective-permute-start(bf16[400,1024]{1,0:T(8,128)(2,1)} %get-tuple-element.33), channel_id=1, source_target_pairs={{0,4},{4,8},{8,12},{12,16},{16,20},{20,24},{24,28},{28,32},{32,36}... | collective-permute-start | bytes 2457608 | tf_op jit(solution)/shard_map/ppermute | solution.py:526
  122.9 27.1 %collective-permute-start.1 = (f32[1,1024]{1,0:T(1,128)}, f32[1,1024]{1,0:T(1,128)S(1)}, u32[]{:S(2)}, u32[]{:S(2)}) collective-permute-start(f32[1,1024]{1,0:T(1,128)} %get-tuple-element.34), channel_id=1, source_target_pairs={{0,4},{4,8},{8,12},{12,16},{16,20},{20,24},{24,28},{28,32},{32,36}... | collective-permute-start | bytes 12296 | tf_op jit(solution)/shard_map/ppermute | solution.py:526
  150.0 0.6 copy-start.6
  150.0 1.0 copy-start
  162.5 25.1 %collective-permute-start.2 = (bf16[400,1024]{1,0:T(8,128)(2,1)}, bf16[400,1024]{1,0:T(8,128)(2,1)S(1)}, u32[]{:S(2)}, u32[]{:S(2)}) collective-permute-start(bf16[400,1024]{1,0:T(8,128)(2,1)} %get-tuple-element.39), channel_id=1, source_target_pairs={{0,4},{4,8},{8,12},{12,16},{16,20},{20,24},{24,28},{28,32},{32,36}... | collective-permute-start | bytes 2457608 | tf_op jit(solution)/shard_map/ppermute | solution.py:526
  164.0 23.7 %collective-permute-start.3 = (f32[1,1024]{1,0:T(1,128)}, f32[1,1024]{1,0:T(1,128)S(1)}, u32[]{:S(2)}, u32[]{:S(2)}) collective-permute-start(f32[1,1024]{1,0:T(1,128)} %get-tuple-element.40), channel_id=1, source_target_pairs={{0,4},{4,8},{8,12},{12,16},{16,20},{20,24},{24,28},{28,32},{32,36}... | collective-permute-start | bytes 12296 | tf_op jit(solution)/shard_map/ppermute | solution.py:526
  187.6 0.6 copy-start.7
  187.6 0.9 copy-start.1
  200.1 115.2 %collective-permute-start.4 = (bf16[400,1024]{1,0:T(8,128)(2,1)}, bf16[400,1024]{1,0:T(8,128)(2,1)S(1)}, u32[]{:S(2)}, u32[]{:S(2)}) collective-permute-start(bf16[400,1024]{1,0:T(8,128)(2,1)} %get-tuple-element.45), channel_id=1, source_target_pairs={{0,4},{4,8},{8,12},{12,16},{16,20},{20,24},{24,28},{28,32},{32,36}... | collective-permute-start | bytes 2457608 | tf_op jit(solution)/shard_map/ppermute | solution.py:526
  201.6 106.1 %collective-permute-start.5 = (f32[1,1024]{1,0:T(1,128)}, f32[1,1024]{1,0:T(1,128)S(1)}, u32[]{:S(2)}, u32[]{:S(2)}) collective-permute-start(f32[1,1024]{1,0:T(1,128)} %get-tuple-element.46), channel_id=1, source_target_pairs={{0,4},{4,8},{8,12},{12,16},{16,20},{20,24},{24,28},{28,32},{32,36}... | collective-permute-start | bytes 12296 | tf_op jit(solution)/shard_map/ppermute | solution.py:526
  299.1 14.8 %collective-permute-start.7 = (f32[2,32,400]{2,1,0:T(8,128)S(1)}, f32[2,32,400]{2,1,0:T(8,128)S(1)}, u32[]{:S(2)}, u32[]{:S(2)}) collective-permute-start(f32[2,32,400]{2,1,0:T(8,128)S(1)} %get-tuple-element.54), channel_id=1, source_target_pairs={{0,0},{4,32},{8,64},{12,96},{16,4},{20,36},{24,68},{28,100},{32,8}... | collective-permute-start | bytes 307208 | tf_op jit(solution)/shard_map/ppermute | solution.py:515
  301.3 12.9 %collective-permute-start.6 = (f32[2,32,400]{2,1,0:T(8,128)S(1)}, f32[2,32,400]{2,1,0:T(8,128)S(1)}, u32[]{:S(2)}, u32[]{:S(2)}) collective-permute-start(f32[2,32,400]{2,1,0:T(8,128)S(1)} %get-tuple-element.55), channel_id=1, source_target_pairs={{0,0},{4,16},{8,32},{12,48},{16,64},{20,80},{24,96},{28,112},{32,4... | collective-permute-start | bytes 307208 | tf_op jit(solution)/shard_map/ppermute | solution.py:515

commit v2 on v1

v2 whole, which is shorter than its diff:
```python
import functools
import jax
import jax.numpy as jnp
from jax import lax
from jax.experimental import pallas as pl
from jax.experimental.pallas import tpu as pltpu
from jax.sharding import PartitionSpec as P

BUCKETS = 3
STEP = 0.3
NT = (((1,), (1,)), ((), ()))
TN = (((0,), (0,)), ((), ()))
VMEM_LIMIT = 60 * 1024 * 1024
MESH = pl.DeviceIdType.MESH
UNITS = 4
UNIT_ROWS = 112
LANES = 512
CHUNK = 512


def onehot(index, rows):
    index = index.astype(jnp.int16)
    row = lax.broadcasted_iota(jnp.int16, (rows, index.shape[1]), 0)
    one = jnp.ones((), jnp.bfloat16)
    return jnp.where(row == index, one, jnp.zeros((), jnp.bfloat16))


def dot(a, b, dims=None):
    if dims is None:
        return jnp.dot(a, b, preferred_element_type=jnp.float32)
    return lax.dot_general(a, b, dims, preferred_element_type=jnp.float32)


def place():
    b, r = lax.axis_index("blk"), lax.axis_index("rel")
    return b // 8, (b // 4) % 2, b % 4, r // 2, r % 2


def device(z, ylo, x, yhi, core):
    return (z * 8 + ylo * 4 + x, yhi * 2 + core)


def greet(peers):
    barrier = pltpu.get_barrier_semaphore()
    for peer in peers:
        pl.semaphore_signal(barrier, inc=1, device_id=peer, device_id_type=MESH)
    pl.semaphore_wait(barrier, len(peers))


def remote(src, dst, sems, index, peer):
    return pltpu.make_async_remote_copy(
        src_ref=src,
        dst_ref=dst,
        send_sem=sems[0].at[index],
        recv_sem=sems[1].at[index],
        device_id=peer,
        device_id_type=MESH,
    )


def send(src, dst, sems, index, peer):
    copy = remote(src, dst, sems, index, peer)
    copy.start()
    return copy


def adagrad(rows, acc, grad):
    acc = acc + jnp.sum(grad * grad, axis=0, keepdims=True) * (1.0 / grad.shape[0])
    return rows - STEP * grad * lax.rsqrt(acc), acc


def train_kernel(
    rel_ref, own_ref, left_ref, lacc_ref, right_ref, racc_ref, src_ref, tgt_ref, neg_ref,
    newleft_ref, newlacc_ref, fresh_ref, freshacc_ref, s_ref, g_ref,
    table, half, rhalf, rhalf_t, hot, query, scaled, push, scale, back, count, rows_now, acc_now,
    out_rows, out_acc, in_rows, in_acc,
    cross_s, cross_r, ring_s, ring_r, whole_s, whole_r, pass_s, pass_r, move_s, move_r, acc_s, acc_r,
):
    z, ylo, x, yhi, core = place()
    me = yhi * 2 + core
    far = (1 - yhi) * 2 + core
    width, rows = left_ref.shape
    owned = own_ref.shape[0]
    units = owned * UNITS
    third = units // 8
    edges = src_ref.shape[2]
    block = neg_ref.shape[2]
    nblk = edges // block
    blks, rels = 32, 4
    b, r = lax.axis_index("blk"), lax.axis_index("rel")
    ahead, behind_me = ((b + 1) % blks, r), ((b + blks - 1) % blks, r)
    sibling = device(z, ylo, x, yhi, 1 - core)
    cross = device(z, 1 - ylo, x, 1 - yhi, core)
    x_ring = [device(z, ylo, (x + d) % 4, yhi, core) for d in (1, 2, 3)]
    z_ring = [device((z + d) % 4, ylo, x, yhi, core) for d in (1, 2, 3)]
    greet([sibling, cross, ahead, behind_me] + x_ring + z_ring)

    for j in range(owned):
        for u in range(UNITS):
            size = min(UNIT_ROWS, width - u * UNIT_ROWS)
            slot = me * units + j * UNITS + u
            part = own_ref[j, u * UNIT_ROWS : u * UNIT_ROWS + size, :]
            table[slot] = jnp.pad(part, ((0, UNIT_ROWS - size), (0, LANES - width)))
    first = [x * third, units // 2 + z * third]
    arrivals = {}
    for i in range(third):
        for ring in range(2):
            slot = me * units + first[ring] + i
            arrivals[ring, i] = send(table.at[slot], table.at[slot], (cross_s, cross_r), ring * third + i, cross)
    mine = table.at[pl.ds(me * units, units)]
    copies = [send(mine, mine, (whole_s, whole_r), 0, sibling)]

    def heads(t):
        for c in range(0, edges, CHUNK):
            cols = slice(c, c + CHUNK)
            part = onehot(src_ref[t, :, cols], rows)
            hot[:, cols] = part
            s_ref[t, :, cols] = dot(half[...], part).astype(jnp.bfloat16)

    def counts(t):
        def step(k, carry):
            hits = onehot(neg_ref[t * nblk + k], rows)
            ones = jnp.ones((block, 128), jnp.bfloat16)
            count[t * nblk + k] = (dot(hits, ones) * (1.0 / block)).astype(jnp.bfloat16)
            return carry

        lax.fori_loop(0, nblk, step, 0)

    newleft_ref[...] = left_ref[...]
    newlacc_ref[...] = lacc_ref[...]
    half[...] = left_ref[...].astype(jnp.bfloat16)
    rows_now[...] = right_ref[...]
    acc_now[...] = racc_ref[...]
    heads(0)
    rings = (x_ring, z_ring)
    landed = {}
    for i in range(third):
        for ring in range(2):
            arrivals[ring, i].wait()
            slot = far * units + first[ring] + i
            for d in (2, 1, 3):
                landed[ring, d, i] = send(
                    table.at[slot], table.at[slot], (ring_s, ring_r), (ring * 3 + d - 1) * third + i, rings[ring][d - 1]
                )
            copies.append(
                send(table.at[slot], table.at[slot], (pass_s, pass_r), ring * 4 * third + i, sibling)
            )
        counts(i)
    for i in range(third):
        for ring in range(2):
            for d in (1, 3, 2):
                landed[ring, d, i].wait()
                axis = (x, z)[ring]
                from_axis = (axis - d + 4) % 4
                slot = far * units + ring * (units // 2) + from_axis * third + i
                copies.append(
                    send(table.at[slot], table.at[slot], (pass_s, pass_r), (ring * 4 + d) * third + i, sibling)
                )
    for copy in copies:
        copy.wait()

    def operator(t, k):
        op = table[pl.ds(rel_ref[t * nblk + k] * UNITS, UNITS)]
        return op.reshape(UNITS * UNIT_ROWS, LANES)[:width, :width]

    def moves(t):
        return (
            remote(out_rows.at[t], in_rows.at[t], (move_s, move_r), t, ahead),
            remote(out_acc.at[t], in_acc.at[t], (acc_s, acc_r), t, ahead),
        )

    def bucket(t, carry):
        for k in range(nblk):
            cols = slice(k * block, (k + 1) * block)
            query[:, cols] = dot(operator(t, k), s_ref[t, :, cols], TN).astype(jnp.bfloat16)
        rhalf[...] = rows_now[...].astype(jnp.bfloat16)
        rhalf_t[...] = rhalf[...].T

        def scores(k, carry):
            cols = pl.ds(pl.multiple_of(k * block, block), block)
            q = query[:, cols]
            score = dot(rhalf_t[...], q)
            hit = lax.broadcasted_iota(jnp.int32, (rows, block), 0) == tgt_ref[t, :, cols]
            pos = jnp.sum(jnp.where(hit, score, 0.0), axis=0, keepdims=True)
            pull = jax.nn.sigmoid(-pos)
            size = jnp.maximum(pull, 2.0**-8)
            inverse = 1.0 / size
            times = count[t * nblk + k].astype(jnp.float32)
            times = jnp.concatenate([times] * (block // 128), axis=1)
            sig = (0.5 * inverse) * jnp.tanh(0.5 * score) + 0.5 * inverse
            push[:, cols] = (sig * times - jnp.where(hit, pull * inverse, 0.0)).astype(jnp.bfloat16)
            scale[:, cols] = size
            scaled[:, cols] = (q.astype(jnp.float32) * size).astype(jnp.bfloat16)
            return carry

        lax.fori_loop(0, nblk, scores, 0)
        fresh, acc = adagrad(rows_now[...], acc_now[...], dot(scaled[...], push[...], NT))
        fresh = fresh.astype(jnp.bfloat16)

        @pl.when(t < BUCKETS - 1)
        def _():
            out_rows[t] = fresh
            out_acc[t] = acc
            for move in moves(t):
                move.start()

        @pl.when(t == BUCKETS - 1)
        def _():
            fresh_ref[...] = fresh
            freshacc_ref[...] = acc

        for c in range(0, edges, CHUNK):
            cols = slice(c, c + CHUNK)
            g_ref[t, :, cols] = (dot(rhalf[...], push[:, cols]) * scale[:, cols]).astype(jnp.bfloat16)
        for k in range(nblk):
            cols = slice(k * block, (k + 1) * block)
            back[:, cols] = dot(operator(t, k), g_ref[t, :, cols]).astype(jnp.bfloat16)
        left, acc = adagrad(newleft_ref[...], newlacc_ref[...], dot(back[...], hot[...], NT))
        newleft_ref[...] = left
        newlacc_ref[...] = acc
        half[...] = left.astype(jnp.bfloat16)

        @pl.when(t < BUCKETS - 1)
        def _():
            heads(t + 1)
            for move in moves(t):
                move.wait()
            rows_now[...] = in_rows[t].astype(jnp.float32)
            acc_now[...] = in_acc[t]

        return carry

    lax.fori_loop(0, BUCKETS, bucket, 0)


def train_call(rel, own, left, lacc, right, racc, src, tgt, neg):
    width, rows = left.shape
    owned = own.shape[0]
    units = owned * UNITS
    third = units // 8
    buckets, _, edges = src.shape
    dma = lambda n: [pltpu.SemaphoreType.DMA((n,))] * 2
    vmem = pl.BlockSpec(memory_space=pltpu.VMEM)
    f32, bf16 = jnp.float32, jnp.bfloat16
    return pl.pallas_call(
        train_kernel,
        in_specs=[pl.BlockSpec(memory_space=pltpu.SMEM)] + [vmem] * 8,
        out_specs=[vmem] * 6,
        out_shape=[
            jax.ShapeDtypeStruct((width, rows), f32),
            jax.ShapeDtypeStruct((1, rows), f32),
            jax.ShapeDtypeStruct((width, rows), bf16),
            jax.ShapeDtypeStruct((1, rows), f32),
            jax.ShapeDtypeStruct((buckets, width, edges), bf16),
            jax.ShapeDtypeStruct((buckets, width, edges), bf16),
        ],
        scratch_shapes=[
            pltpu.VMEM((4 * units, UNIT_ROWS, LANES), bf16),
            pltpu.VMEM((width, rows), bf16),
            pltpu.VMEM((width, rows), bf16),
            pltpu.VMEM((rows, width), bf16),
            pltpu.VMEM((rows, edges), bf16),
            pltpu.VMEM((width, edges), bf16),
            pltpu.VMEM((width, edges), bf16),
            pltpu.VMEM((rows, edges), bf16),
            pltpu.VMEM((1, edges), f32),
            pltpu.VMEM((width, edges), bf16),
            pltpu.VMEM((neg.shape[0], rows, 128), bf16),
            pltpu.VMEM((width, rows), f32),
            pltpu.VMEM((1, rows), f32),
            pltpu.VMEM((buckets - 1, width, rows), bf16),
            pltpu.VMEM((buckets - 1, 1, rows), f32),
            pltpu.VMEM((buckets - 1, width, rows), bf16),
            pltpu.VMEM((buckets - 1, 1, rows), f32),
        ]
        + dma(2 * third) + dma(6 * third) + dma(1) + dma(8 * third) + dma(buckets - 1) + dma(buckets - 1),
        compiler_params=pltpu.CompilerParams(
            collective_id=0, has_side_effects=True, vmem_limit_bytes=VMEM_LIMIT
        ),
        name="train_buckets",
    )(rel, own, left, lacc, right, racc, src, tgt, neg)


def opgrad_kernel(nrel, rel_ref, s_ref, g_ref, out_ref, acc_ref, count_ref, list_ref):
    core, part = pl.program_id(0), pl.program_id(1)
    _, width, edges = s_ref.shape
    nblk = rel_ref.shape[0] // 3
    block = edges // nblk

    @pl.when((core == 0) & (part == 0))
    def _():
        def clear(j, carry):
            for t in range(3):
                count_ref[t, j] = 0
            return carry

        lax.fori_loop(0, nrel, clear, 0)
        for t in range(3):
            def note(k, carry):
                j = rel_ref[t * nblk + k]
                n = count_ref[t, j]
                list_ref[t, j * nblk + n] = k
                count_ref[t, j] = n + 1
                return carry

            lax.fori_loop(0, nblk, note, 0)

    for i in range(4):
        j = ((i // 2) * 2 + core) * 6 + part * 2 + i % 2
        acc_ref[...] = jnp.zeros_like(acc_ref)
        for t in range(3):
            def add(n, carry):
                k = list_ref[t, j * nblk + n]
                cols = pl.ds(pl.multiple_of(k * block, block), block)
                acc_ref[...] += dot(s_ref[t, :, cols], g_ref[t, :, cols], NT)
                return carry

            lax.fori_loop(0, count_ref[t, j], add, 0)
        out_ref[0, 0, i, :, :width] = acc_ref[...].astype(jnp.bfloat16)
        out_ref[0, 0, i, :, width:] = jnp.zeros((width, out_ref.shape[-1] - width), jnp.bfloat16)


def opgrad_call(rel, s, g, nrel):
    _, width, edges = s.shape
    nblk = rel.shape[0] // 3
    whole = pl.BlockSpec(s.shape, lambda c, p, rel: (0, 0, 0))
    return pl.pallas_call(
        functools.partial(opgrad_kernel, nrel),
        grid_spec=pltpu.PrefetchScalarGridSpec(
            num_scalar_prefetch=1,
            grid=(2, 3),
            in_specs=[whole] * 2,
            out_specs=pl.BlockSpec((1, 1, 4, width, 512), lambda c, p, rel: (c, p, 0, 0, 0)),
            scratch_shapes=[
                pltpu.VMEM((width, width), jnp.float32),
                pltpu.SMEM((3, nrel), jnp.int32),
                pltpu.SMEM((3, nrel * nblk), jnp.int32),
            ],
        ),
        out_shape=jax.ShapeDtypeStruct((2, 3, 4, width, 512), jnp.bfloat16),
        compiler_params=pltpu.CompilerParams(vmem_limit_bytes=VMEM_LIMIT),
        name="operator_gradients",
    )(rel, s, g)


def row_of(t):
    return 25 * t // 2


def last_window(s, t):
    if s == 0:
        base, top = 96 * (t // 8) + 48 * ((t // 4) % 2), 48
    elif s == 1:
        base, top = 192 * (t // 16) + 48 * ((t // 4) % 4), 48
    else:
        z = (t // 2) % 4
        base, top = 96 * (t // 8) + 16 * z + 16 * (z // 2), 32
    part = row_of(t) - base
    local = 16 * (part // 16) - 16 * (part // top)
    return base + local, local


def window(start, size):
    return pl.ds(pl.multiple_of(start, 16), size)


def total(out, own, parts):
    value = own.astype(jnp.float32)
    for part in parts:
        value = value + part.astype(jnp.float32)
    out[...] = value.astype(out.dtype)


def reduce_kernel(
    grads_ref, out_ref, own, near,
    a0, b0, c0, a1, b1, c1, a2, b2, c2, m0, n0, m1, n1, m2, n2, own_sem, send_sem, recv_sem,
):
    z, ylo, x, yhi, core = place()
    sems = (send_sem, recv_sem)
    sibling = device(z, ylo, x, yhi, 1 - core)
    z_at = [(z + d) % 4 for d in (1, 2, 3)]
    x_at = [(x + d) % 4 for d in (1, 2, 3)]
    y_at = [(yhi, 1 - ylo), (1 - yhi, ylo), (1 - yhi, 1 - ylo)]
    z_ring = [device(v, ylo, x, yhi, core) for v in z_at]
    x_ring = [device(z, ylo, v, yhi, core) for v in x_at]
    y_ring = [device(z, v, x, h, core) for h, v in y_at]
    greet([sibling] + z_ring + x_ring + y_ring)

    mine, pairs = [], []
    for s in range(3):
        pairs.append(send(grads_ref.at[1 - core, s], near.at[s], sems, s, sibling))
        mine.append(pltpu.make_async_copy(grads_ref.at[core, s], own.at[s], own_sem.at[s]))
        mine[-1].start()

    first = []
    for s in range(3):
        mine[s].wait()
        pairs[s].wait()
        for i in range(4):
            total(own.at[s, i], own[s, i], [near[s, i]])
        for d in range(3):
            if s == 0:
                src = own.at[s, :, window(96 * z_at[d], 112)]
                copy = send(src, a0.at[d], sems, 3 + s * 3 + d, z_ring[d])
            elif s == 1:
                h, v = y_at[d]
                src = own.at[s, pl.ds(2 * h, 2), window(192 * v, 208)]
                copy = send(src, a1.at[d], sems, 3 + s * 3 + d, y_ring[d])
            else:
                src = own.at[s, :, window(96 * x_at[d], 112)]
                copy = send(src, a2.at[d], sems, 3 + s * 3 + d, x_ring[d])
            first.append(copy)

    second = []
    for s in range(3):
        for d in range(3):
            first[s * 3 + d].wait()
        if s == 0:
            total(m0, own[s, :, window(96 * z, 112)], [a0[d] for d in range(3)])
        elif s == 1:
            total(m1, own[s, pl.ds(2 * yhi, 2), window(192 * ylo, 208)], [a1[d] for d in range(3)])
        else:
            total(m2, own[s, :, window(96 * x, 112)], [a2[d] for d in range(3)])
        for d in range(3):
            if s == 0:
                h, v = y_at[d]
                copy = send(m0.at[pl.ds(2 * h, 2), window(48 * v, 64)], b0.at[d], sems, 12 + s * 3 + d, y_ring[d])
            elif s == 1:
                copy = send(m1.at[:, window(48 * x_at[d], 64)], b1.at[d], sems, 12 + s * 3 + d, x_ring[d])
            else:
                v = z_at[d]
                copy = send(m2.at[:, window(16 * v + 16 * (v // 2), 48)], b2.at[d], sems, 12 + s * 3 + d, z_ring[d])
            second.append(copy)

    third = []
    for s in range(3):
        for d in range(3):
            second[s * 3 + d].wait()
        if s == 0:
            total(n0, m0[pl.ds(2 * yhi, 2), window(48 * ylo, 64)], [b0[d] for d in range(3)])
        elif s == 1:
            total(n1, m1[:, window(48 * x, 64)], [b1[d] for d in range(3)])
        else:
            total(n2, m2[:, window(16 * z + 16 * (z // 2), 48)], [b2[d] for d in range(3)])
        for d in range(3):
            if s == 0:
                _, at = last_window(0, z * 8 + ylo * 4 + x_at[d])
                copy = send(n0.at[:, window(at, 32)], c0.at[d], sems, 21 + s * 3 + d, x_ring[d])
            elif s == 1:
                _, at = last_window(1, ylo * 16 + x * 4 + z_at[d])
                copy = send(n1.at[:, window(at, 32)], c1.at[d], sems, 21 + s * 3 + d, z_ring[d])
            else:
                h, v = y_at[d]
                _, at = last_window(2, x * 8 + z * 2 + v)
                copy = send(n2.at[pl.ds(2 * h, 2), window(at, 32)], c2.at[d], sems, 21 + s * 3 + d, y_ring[d])
            third.append(copy)

    for s in range(3):
        for d in range(3):
            third[s * 3 + d].wait()
        if s == 0:
            _, at = last_window(0, z * 8 + ylo * 4 + x)
            total(out_ref.at[s], n0[:, window(at, 32)], [c0[d] for d in range(3)])
        elif s == 1:
            _, at = last_window(1, ylo * 16 + x * 4 + z)
            total(out_ref.at[s], n1[:, window(at, 32)], [c1[d] for d in range(3)])
        else:
            _, at = last_window(2, x * 8 + z * 2 + ylo)
            total(out_ref.at[s], n2[pl.ds(2 * yhi, 2), window(at, 32)], [c2[d] for d in range(3)])


def reduce_call(grads):
    _, _, four, rows, lanes = grads.shape
    buf = lambda *shape: pltpu.VMEM(shape + (lanes,), jnp.bfloat16)
    return pl.pallas_call(
        reduce_kernel,
        in_specs=[pl.BlockSpec(memory_space=pl.ANY)],
        out_specs=pl.BlockSpec(memory_space=pltpu.VMEM),
        out_shape=jax.ShapeDtypeStruct((3, 2, 32, lanes), jnp.float32),
        scratch_shapes=[
            buf(3, four, rows), buf(3, four, rows),
            buf(3, 4, 112), buf(3, 2, 64), buf(3, 2, 32),
            buf(3, 2, 208), buf(3, 2, 64), buf(3, 2, 32),
            buf(3, 4, 112), buf(3, 4, 48), buf(3, 2, 32),
            buf(4, 112), buf(2, 64), buf(2, 208), buf(2, 64), buf(4, 112), buf(4, 48),
            pltpu.SemaphoreType.DMA((3,)), pltpu.SemaphoreType.DMA((30,)), pltpu.SemaphoreType.DMA((30,)),
        ],
        compiler_params=pltpu.CompilerParams(
            collective_id=1, has_side_effects=True, vmem_limit_bytes=VMEM_LIMIT
        ),
        name="reduce_operator_gradients",
    )(grads)


def final_share(pieces, width):
    blk = lax.axis_size("blk")
    place_1 = lambda b: ((b // 4) % 2) * 16 + (b % 4) * 4 + b // 8
    place_2 = lambda b: (b % 4) * 8 + (b // 8) * 2 + (b // 4) % 2
    t = lax.axis_index("blk")
    shares = []
    for s, at in enumerate((None, place_1, place_2)):
        piece = pieces[s, :, :, :width]
        if at is not None:
            piece = lax.ppermute(piece, "blk", [(b, at(b)) for b in range(blk)])
        start, _ = last_window(s, t)
        skip = t * (width * width // blk) - start * width
        flat = piece.reshape(2, 32 * width)
        shares.append(lax.dynamic_slice(flat, (0, skip), (2, width * width // blk)))
    return jnp.concatenate(shares, axis=0)


def from_behind(value, axis, steps):
    count = lax.axis_size(axis)
    pairs = [(source, (source + steps) % count) for source in range(count)]
    return lax.ppermute(value, axis, pairs)


def body(left, left_state, right, right_state, operators, need_list, block_slot, sources, targets, negatives):
    owned_count, width, _ = operators.shape
    owners = lax.axis_size("rel")
    nrel = owned_count * owners
    rel = need_list[0].reshape(-1)[block_slot[0].reshape(-1)]
    src = sources[0][:, None]
    tgt = targets[0][:, None]
    neg = negatives[0].reshape(-1, 1, negatives.shape[-1])
    L, LS, R, RS, s, g = train_call(
        rel, operators, left.T, left_state[None], right.T, right_state[None], src, tgt, neg
    )
    R, RS = from_behind((R, RS), "blk", 1)
    op_grad = final_share(reduce_call(opgrad_call(rel, s, g, nrel)), width)
    return (L.T, LS[0], R.T.astype(jnp.float32), RS[0], op_grad)


def solution(mesh):
    in_specs = (
        P(("blk", "rel"), None),
        P(("blk", "rel")),
        P(("blk", "rel"), None),
        P(("blk", "rel")),
        P("rel", None, None),
        P(("blk", "rel"), None, None),
        P(("blk", "rel"), None, None),
        P(("blk", "rel"), None, None),
        P(("blk", "rel"), None, None),
        P(("blk", "rel"), None, None, None),
    )
    out_specs = (
        P(("blk", "rel"), None),
        P(("blk", "rel")),
        P(("blk", "rel"), None),
        P(("blk", "rel")),
        P("rel", "blk"),
    )
    return jax.shard_map(body, mesh=mesh, in_specs=in_specs, out_specs=out_specs, check_vma=False)
```

time: 320 us -> 234 us (0.73)
  Pallas kernels: 276 us -> 187 us
  waiting for transfers between devices: 6.28 us -> 24.4 us
  local copies, waits for them, and re-layouts: 15.2 us -> 7.73 us
  starting transfers between devices: 16.5 us -> 10.8 us
    pallas_call x9 -> x2, Pallas kernels: 222 us -> 136 us  [the longest x1 120 us: train_call(): pl.pallas_call(train_kernel, in_specs=[pl.BlockSpec(memory_space=pltpu.SM...]
    ppermute x6 -> x2, waiting for transfers between devices: 0.02 us -> 21.3 us  [from_behind(): return lax.ppermute(value, axis, pairs)]
    ppermute x6 -> x2, starting transfers between devices: 8.26 us -> 3.63 us  [from_behind(): return lax.ppermute(value, axis, pairs)]
    slice x6 -> x0, local copies, waits for them, and re-layouts: 3.75 us -> none  [the longest x3 2.58 us: body(): out = left_call(rel[both], L, LS, R, p, src[both], ops, more)]
    pad x1 -> x0, local copies, waits for them, and re-layouts: 3.69 us -> none  [body(): own = jnp.pad(operators, ((0, 0), (0, padded - width), (0, LANES - width)))]
  transfers between devices with their start and end apart: 8 -> 4, of which waited for: 1 -> 2; matrix products, arithmetic and copies ran while one was open for 2% -> 1% of each run, Pallas kernels for 44% -> 0%
where the time goes in v2:
time: 234 us
  Pallas kernels  187 us (80%)
  waiting for transfers between devices  24.4 us (10%)
  starting transfers between devices  10.8 us (5%)
  local copies, waits for them, and re-layouts  7.73 us (3%)
  other arithmetic  2.79 us (1%)
    pallas_call x1, Pallas kernels, train_call(): pl.pallas_call(train_kernel, in_specs=[pl.BlockSpec(memory_space=pltpu.SM...  120 us
    pallas_call x1, Pallas kernels, reduce_call(): pl.pallas_call(reduce_kernel, in_specs=[pl.BlockSpec(memory_space=pl.ANY)...  51.4 us
    ppermute x2, waiting for transfers between devices, from_behind(): return lax.ppermute(value, axis, pairs)  21.3 us
    pallas_call x1, Pallas kernels, opgrad_call(): pl.pallas_call(functools.partial(opgrad_kernel, nrel), grid_spec=pltpu.Pr...  16.3 us
    ppermute x2, starting transfers between devices, final_share(): piece = lax.ppermute(piece, 'blk', [(b, at(b)) for b in range(blk)])  7.2 us
  transfers between devices with their start and end apart: 4, of which 2 were waited for; matrix products, arithmetic and copies ran while one was open for 1% of the time, Pallas kernels for 0%

profile of v2, /device:TPU:8, one launch (start us, length us, event | category | flops | bytes accessed | tf_op | source)
XLA Modules:
  0.0 234.1 jit_solution(18155438172309896798)
XLA Ops:
  0.6 0.7 reduce
  1.3 0.1 reshape_squeeze.13
  1.4 0.8 reshape_squeeze.12
  2.2 1.4 reshape_squeeze.14.neg_ref
  3.6 1.2 gather_fusion
  4.8 119.6 %train_buckets.1 = (f32[400,1024]{1,0:T(8,128)}, f32[1,1024]{1,0:T(1,128)}, bf16[400,1024]{1,0:T(8,128)(2,1)}, f32[1,1024]{1,0:T(1,128)}, bf16[3,400,2048]{2,1,0:T(8,128)(2,1)}, /*index=5*/bf16[3,400,2048]{2,1,0:T(8,128)(2,1)}) custom-call(s32[24]{0:T(128)} %gather_fusion, bf16[6,400,400]{2,1,0:T(8,128)(2,1)} %own_ref.1, f32[400,1024]{1,0:T(8,128)} %bitcast.21, ...), custom_call_target="tpu_custom_call" | custom-call | tf_op jit(solution)/shard_map/train_buckets/pallas_call | solution.py:245
  124.4 16.3 %operator_gradients.1.grads_ref = bf16[2,3,4,400,512]{4,3,2,1,0:T(8,128)(2,1)} custom-call(s32[24]{0:T(128)} %gather_fusion, bf16[3,400,2048]{2,1,0:T(8,128)(2,1)} %get-tuple-element.15.s_ref, bf16[3,400,2048]{2,1,0:T(8,128)(2,1)} %get-tuple-element.16.g_ref), custom_call_target="tpu_custom_call" | custom-call | tf_op jit(solution)/shard_map/operator_gradients/pallas_call | solution.py:327
  140.7 0.0 copy-start.2
  140.7 51.4 %reduce_operator_gradients.1 = f32[3,2,32,512]{3,2,1,0:T(8,128)} custom-call(bf16[2,3,4,400,512]{4,3,2,1,0:T(8,128)(2,1)} %operator_gradients.1.grads_ref), custom_call_target="tpu_custom_call" | custom-call | tf_op jit(solution)/shard_map/reduce_operator_gradients/pallas_call | solution.py:475
  192.2 1.1 fusion.1
  193.2 5.3 %collective-permute-start.2 = (f32[2,32,400]{2,1,0:T(8,128)S(1)}, f32[2,32,400]{2,1,0:T(8,128)S(1)}, u32[]{:S(2)}, u32[]{:S(2)}) collective-permute-start(f32[2,32,400]{2,1,0:T(8,128)S(1)} %get-tuple-element.19), channel_id=1, source_target_pairs={{0,0},{4,16},{8,32},{12,48},{16,64},{20,80},{24,96},{28,112},{32,4... | collective-permute-start | bytes 307208 | tf_op jit(solution)/shard_map/ppermute | solution.py:504
  198.5 1.9 collective-permute-start.3
  200.4 0.1 collective-permute-start
  200.5 0.0 copy-done.2
  200.5 3.6 %collective-permute-start.1 = (f32[1,1024]{1,0:T(1,128)S(1)}, f32[1,1024]{1,0:T(1,128)S(1)}, u32[]{:S(2)}, u32[]{:S(2)}) collective-permute-start(f32[1,1024]{1,0:T(1,128)S(1)} %copy-done.2), channel_id=1, source_target_pairs={{0,4},{4,8},{8,12},{12,16},{16,20},{20,24},{24,28},{28,32},{32,36}... | collective-permute-start | bytes 12296 | tf_op jit(solution)/shard_map/ppermute | solution.py:515
  204.1 0.2 reshape_squeeze.15
  204.3 0.1 constant_dynamic-slice_fusion.2
  204.6 21.3 %collective-permute-done.1 = f32[1,1024]{1,0:T(1,128)S(1)} collective-permute-done((f32[1,1024]{1,0:T(1,128)S(1)}, f32[1,1024]{1,0:T(1,128)S(1)}, u32[]{:S(2)}, u32[]{:S(2)}) %collective-permute-start.1) | collective-permute-done | bytes 4128 | tf_op jit(solution)/shard_map/ppermute | solution.py:515
  225.9 0.0 copy-start
  225.9 0.0 collective-permute-done.2
  225.9 0.2 reshape.44
  226.1 0.1 constant_dynamic-slice_fusion.1
  226.2 3.1 %collective-permute-done.3 = f32[2,32,400]{2,1,0:T(8,128)S(1)} collective-permute-done((f32[2,32,400]{2,1,0:T(8,128)S(1)}, f32[2,32,400]{2,1,0:T(8,128)S(1)}, u32[]{:S(2)}, u32[]{:S(2)}) %collective-permute-start.3) | collective-permute-done | bytes 102432 | tf_op jit(solution)/shard_map/ppermute | solution.py:504
  229.3 0.2 reshape.45
  229.5 0.1 constant_dynamic-slice_fusion
  229.6 0.7 pad_maximum_fusion
  230.3 0.0 collective-permute-done
  230.3 1.3 convert_bitcast_fusion
  231.7 0.0 copy-done
  231.7 0.0 copy-start.1
  231.7 1.2 copy.18
  232.9 0.0 copy-done.1
  232.9 0.6 copy.19
  233.5 0.6 copy.20
  (2 shorter events, 0.0 us)
Async XLA Ops:
  140.7 59.8 %copy-start.2 = (f32[1,1024]{1,0:T(1,128)S(1)}, f32[1,1024]{1,0:T(1,128)}, u32[]{:S(2)}) copy-start(f32[1,1024]{1,0:T(1,128)} %get-tuple-element.14) | copy-start | bytes 12292
  193.2 32.6 %collective-permute-start.2 = (f32[2,32,400]{2,1,0:T(8,128)S(1)}, f32[2,32,400]{2,1,0:T(8,128)S(1)}, u32[]{:S(2)}, u32[]{:S(2)}) collective-permute-start(f32[2,32,400]{2,1,0:T(8,128)S(1)} %get-tuple-element.19), channel_id=1, source_target_pairs={{0,0},{4,16},{8,32},{12,48},{16,64},{20,80},{24,96},{28,112},{32,4... | collective-permute-start | bytes 307208 | tf_op jit(solution)/shard_map/ppermute | solution.py:504
  198.5 30.8 %collective-permute-start.3 = (f32[2,32,400]{2,1,0:T(8,128)S(1)}, f32[2,32,400]{2,1,0:T(8,128)S(1)}, u32[]{:S(2)}, u32[]{:S(2)}) collective-permute-start(f32[2,32,400]{2,1,0:T(8,128)S(1)} %get-tuple-element.18), channel_id=1, source_target_pairs={{0,0},{4,32},{8,64},{12,96},{16,4},{20,36},{24,68},{28,100},{32,8}... | collective-permute-start | bytes 307208 | tf_op jit(solution)/shard_map/ppermute | solution.py:504
  200.4 29.9 %collective-permute-start = (bf16[400,1024]{1,0:T(8,128)(2,1)}, bf16[400,1024]{1,0:T(8,128)(2,1)S(1)}, u32[]{:S(2)}, u32[]{:S(2)}) collective-permute-start(bf16[400,1024]{1,0:T(8,128)(2,1)} %get-tuple-element.13), channel_id=1, source_target_pairs={{0,4},{4,8},{8,12},{12,16},{16,20},{20,24},{24,28},{28,32},{32,36}... | collective-permute-start | bytes 2457608 | tf_op jit(solution)/shard_map/ppermute | solution.py:515
  200.5 25.3 %collective-permute-start.1 = (f32[1,1024]{1,0:T(1,128)S(1)}, f32[1,1024]{1,0:T(1,128)S(1)}, u32[]{:S(2)}, u32[]{:S(2)}) collective-permute-start(f32[1,1024]{1,0:T(1,128)S(1)} %copy-done.2), channel_id=1, source_target_pairs={{0,4},{4,8},{8,12},{12,16},{16,20},{20,24},{24,28},{28,32},{32,36}... | collective-permute-start | bytes 12296 | tf_op jit(solution)/shard_map/ppermute | solution.py:515
  225.9 5.8 %copy-start = (f32[400,1024]{1,0:T(8,128)S(1)}, f32[400,1024]{1,0:T(8,128)}, u32[]{:S(2)}) copy-start(f32[400,1024]{1,0:T(8,128)} %get-tuple-element.11) | copy-start | bytes 4915204
  231.7 1.2 copy-start.1

commit v3 on v2

v3 whole, which is shorter than its diff:
```python
import functools
import jax
import jax.numpy as jnp
from jax import lax
from jax.experimental import pallas as pl
from jax.experimental.pallas import tpu as pltpu
from jax.sharding import PartitionSpec as P

BUCKETS = 3
STEP = 0.3
NT = (((1,), (1,)), ((), ()))
TN = (((0,), (0,)), ((), ()))
VMEM_LIMIT = 60 * 1024 * 1024
MESH = pl.DeviceIdType.MESH
UNITS = 4
LANES = 512
CHUNK = 512


def onehot(index, rows):
    index = index.astype(jnp.int16)
    row = lax.broadcasted_iota(jnp.int16, (rows, index.shape[1]), 0)
    one = jnp.ones((), jnp.bfloat16)
    return jnp.where(row == index, one, jnp.zeros((), jnp.bfloat16))


def dot(a, b, dims=None):
    if dims is None:
        return jnp.dot(a, b, preferred_element_type=jnp.float32)
    return lax.dot_general(a, b, dims, preferred_element_type=jnp.float32)


def place():
    b, r = lax.axis_index("blk"), lax.axis_index("rel")
    return b // 8, (b // 4) % 2, b % 4, r // 2, r % 2


def device(z, ylo, x, yhi, core):
    return (z * 8 + ylo * 4 + x, yhi * 2 + core)


def greet(peers):
    barrier = pltpu.get_barrier_semaphore()
    for peer in peers:
        pl.semaphore_signal(barrier, inc=1, device_id=peer, device_id_type=MESH)
    pl.semaphore_wait(barrier, len(peers))


def remote(src, dst, sems, index, peer):
    return pltpu.make_async_remote_copy(
        src_ref=src,
        dst_ref=dst,
        send_sem=sems[0].at[index],
        recv_sem=sems[1].at[index],
        device_id=peer,
        device_id_type=MESH,
    )


def send(src, dst, sems, index, peer):
    copy = remote(src, dst, sems, index, peer)
    copy.start()
    return copy


def adagrad(rows, acc, grad):
    acc = acc + jnp.sum(grad * grad, axis=0, keepdims=True) * (1.0 / grad.shape[0])
    return rows - STEP * grad * lax.rsqrt(acc), acc


def train_kernel(
    info_ref, own_ref, left_ref, lacc_ref, right_ref, racc_ref, src_ref, tgt_ref, neg_ref,
    newleft_ref, newlacc_ref, newright_ref, newracc_ref, grads_ref, near_ref,
    table, fresh_ref, freshacc_ref, half, rhalf, rhalf_t, hot, query, scaled, heads_now, push, scale, score, count, sums, rows_now, acc_now,
    in_rows, in_acc, load_sem, store_sem,
    cross_s, cross_r, ring_s, ring_r, whole_s, whole_r, pass_s, pass_r, move_s, move_r, acc_s, acc_r, near_s, near_r,
):
    z, ylo, x, yhi, core = place()
    me = yhi * 2 + core
    far = (1 - yhi) * 2 + core
    width, rows = newleft_ref.shape
    owned = own_ref.shape[0]
    units = owned * UNITS
    third = units // 8
    edges = src_ref.shape[2]
    block = neg_ref.shape[2]
    nblk = edges // block
    nrel = table.shape[0]
    total_blocks = BUCKETS * nblk
    blks = 32
    b, r = lax.axis_index("blk"), lax.axis_index("rel")
    ahead, behind = ((b + 1) % blks, r), ((b + blks - 1) % blks, r)
    sibling = device(z, ylo, x, yhi, 1 - core)
    cross = device(z, 1 - ylo, x, 1 - yhi, core)
    x_ring = [device(z, ylo, (x + d) % 4, yhi, core) for d in (1, 2, 3)]
    z_ring = [device((z + d) % 4, ylo, x, yhi, core) for d in (1, 2, 3)]
    loads = [
        pltpu.make_async_copy(left_ref, newleft_ref, load_sem.at[0]),
        pltpu.make_async_copy(right_ref, rows_now, load_sem.at[1]),
    ]
    for load in loads:
        load.start()
    greet([sibling, cross, ahead, behind] + x_ring + z_ring)

    for j in range(owned):
        table[me * owned + j] = jnp.pad(own_ref[j], ((0, 0), (0, LANES - width)))

    def unit(owner, u):
        lanes = LANES // UNITS
        return table.at[owner * owned + u // UNITS, :, pl.ds(pl.multiple_of((u % UNITS) * lanes, lanes), lanes)]

    first = [x * third, units // 2 + z * third]
    arrivals = {}
    for i in range(third):
        for ring in range(2):
            part = unit(me, first[ring] + i)
            arrivals[ring, i] = send(part, part, (cross_s, cross_r), ring * third + i, cross)
    mine = table.at[pl.ds(me * owned, owned)]
    copies = [send(mine, mine, (whole_s, whole_r), 0, sibling)]

    def heads(t):
        for c in range(0, edges, CHUNK):
            cols = slice(c, c + CHUNK)
            hot[:, cols] = onehot(src_ref[t, :, cols], rows)
            heads_now[:, cols] = dot(half[...], hot[:, cols]).astype(jnp.bfloat16)

    def counts(t):
        def step(k, carry):
            hits = onehot(neg_ref[t * nblk + k], rows)
            ones = jnp.ones((block, 128), jnp.bfloat16)
            count[k] = (dot(hits, ones) * (1.0 / block)).astype(jnp.bfloat16)
            return carry

        lax.fori_loop(0, nblk, step, 0)

    def clear(n, carry):
        sums[n] = jnp.zeros(sums.shape[1:], jnp.float32)
        return carry

    newlacc_ref[...] = lacc_ref[...]
    acc_now[...] = racc_ref[...]
    for load in loads:
        load.wait()
    half[...] = newleft_ref[...].astype(jnp.bfloat16)
    heads(0)
    rings = (x_ring, z_ring)
    landed = {}
    for i in range(third):
        for ring in range(2):
            arrivals[ring, i].wait()
            part = unit(far, first[ring] + i)
            for d in (2, 1, 3):
                landed[ring, d, i] = send(
                    part, part, (ring_s, ring_r), (ring * 3 + d - 1) * third + i, rings[ring][d - 1]
                )
            copies.append(send(part, part, (pass_s, pass_r), ring * 4 * third + i, sibling))
        if i == 0:
            counts(0)
        elif i == 1:
            lax.fori_loop(0, sums.shape[0], clear, 0)
    for i in range(third):
        for ring in range(2):
            for d in (1, 3, 2):
                landed[ring, d, i].wait()
                origin = ((x, z)[ring] - d + 4) % 4
                part = unit(far, ring * (units // 2) + origin * third + i)
                copies.append(send(part, part, (pass_s, pass_r), (ring * 4 + d) * third + i, sibling))
    for copy in copies:
        copy.wait()

    def operator(t, k):
        return table[info_ref[t * nblk + k]][:, :width]

    def earlier(n):
        return jnp.where(n < total_blocks, sums[jnp.minimum(n, total_blocks - 1)], 0.0)

    def moves(t):
        return (
            remote(fresh_ref, in_rows.at[t], (move_s, move_r), t, ahead),
            remote(freshacc_ref, in_acc.at[t], (acc_s, acc_r), t, ahead),
        )

    last_moves = (
        remote(fresh_ref, newright_ref, (move_s, move_r), BUCKETS - 1, ahead),
        remote(freshacc_ref, newracc_ref, (acc_s, acc_r), BUCKETS - 1, ahead),
    )

    def bucket(t, carry):
        for k in range(nblk):
            cols = slice(k * block, (k + 1) * block)
            query[:, cols] = dot(operator(t, k), heads_now[:, cols], TN).astype(jnp.bfloat16)
        rhalf[...] = rows_now[...].astype(jnp.bfloat16)
        rhalf_t[...] = rhalf[...].T

        def meet(k, slot):
            cols = pl.ds(pl.multiple_of(k * block, block), block)
            value = dot(rhalf_t[...], query[:, cols])
            score[slot] = value
            hit = lax.broadcasted_iota(jnp.int32, (rows, block), 0) == tgt_ref[t, :, cols]
            pos = jnp.sum(jnp.where(hit, value, 0.0), axis=0, keepdims=True)
            scale[:, cols] = jax.nn.sigmoid(-pos)

        def weigh(k, slot):
            cols = pl.ds(pl.multiple_of(k * block, block), block)
            pull = scale[:, cols]
            size = jnp.maximum(pull, 2.0**-8)
            inverse = 1.0 / size
            times = jnp.concatenate([count[k]] * (block // 128), axis=1)
            twice = (jnp.tanh(0.5 * score[slot]) + 1.0).astype(jnp.bfloat16)
            hit = onehot(tgt_ref[t, :, cols], rows)
            push[:, cols] = twice * (0.5 * inverse).astype(jnp.bfloat16) * times - hit * (pull * inverse).astype(
                jnp.bfloat16
            )
            scale[:, cols] = size
            scaled[:, cols] = (query[:, cols].astype(jnp.float32) * size).astype(jnp.bfloat16)

        def two(j, carry):
            meet(2 * j + 1, 1)
            weigh(2 * j, 0)
            meet(2 * j + 2, 0)
            weigh(2 * j + 1, 1)
            return carry

        meet(0, 0)
        lax.fori_loop(0, nblk // 2 - 1, two, 0)
        meet(nblk - 1, 1)
        weigh(nblk - 2, 0)
        weigh(nblk - 1, 1)
        for c in range(0, rows, CHUNK):
            part = slice(c, c + CHUNK)
            fresh, acc = adagrad(rows_now[:, part], acc_now[:, part], dot(scaled[...], push[part, :], NT))
            fresh_ref[:, part] = fresh.astype(jnp.bfloat16)
            freshacc_ref[:, part] = acc

        @pl.when(t < BUCKETS - 1)
        def _():
            for move in moves(t):
                move.start()

        @pl.when(t == BUCKETS - 1)
        def _():
            for move in last_moves:
                move.start()

        for c in range(0, edges, CHUNK):
            cols = slice(c, c + CHUNK)
            scaled[:, cols] = (dot(rhalf[...], push[:, cols]) * scale[:, cols]).astype(jnp.bfloat16)
        for k in range(nblk):
            cols = slice(k * block, (k + 1) * block)
            query[:, cols] = dot(operator(t, k), scaled[:, cols]).astype(jnp.bfloat16)
        for c in range(0, rows, CHUNK):
            part = slice(c, c + CHUNK)
            left, acc = adagrad(newleft_ref[:, part], newlacc_ref[:, part], dot(query[...], hot[part, :], NT))
            newleft_ref[:, part] = left
            newlacc_ref[:, part] = acc
            half[:, part] = left.astype(jnp.bfloat16)
        for k in range(nblk):
            cols = slice(k * block, (k + 1) * block)
            before = earlier(info_ref[total_blocks + t * nblk + k])
            sums[t * nblk + k] = before + dot(heads_now[:, cols], scaled[:, cols], NT)

        @pl.when(t < BUCKETS - 1)
        def _():
            heads(t + 1)
            counts(t + 1)
            for move in moves(t):
                move.wait()
            rows_now[...] = in_rows[t].astype(jnp.float32)
            acc_now[...] = in_acc[t]

        return carry

    lax.fori_loop(0, BUCKETS, bucket, 0)

    copies = []
    for here in (False, True):
        for n in range(nrel // 2):
            part, h, i = n // 4, n // 2 % 2, n % 2
            j = (h * 2 + (core if here else 1 - core)) * owned + part * 2 + i
            table[j, :, :width] = earlier(info_ref[2 * total_blocks + j]).astype(jnp.bfloat16)
            if here:
                copy = pltpu.make_async_copy(table.at[j], grads_ref.at[part, h * 2 + i], store_sem.at[n])
                copy.start()
            else:
                copy = send(table.at[j], near_ref.at[part, h * 2 + i], (near_s, near_r), n, sibling)
            copies.append(copy)
    for copy in copies:
        copy.wait()
    for move in last_moves:
        move.wait()


def train_call(info, own, left, lacc, right, racc, src, tgt, neg, nrel):
    width, rows = left.shape
    owned = own.shape[0]
    units = owned * UNITS
    third = units // 8
    buckets, _, edges = src.shape
    nblk = neg.shape[0] // buckets
    dma = lambda n: [pltpu.SemaphoreType.DMA((n,))] * 2
    vmem = pl.BlockSpec(memory_space=pltpu.VMEM)
    anywhere = pl.BlockSpec(memory_space=pl.ANY)
    f32, bf16 = jnp.float32, jnp.bfloat16
    return pl.pallas_call(
        train_kernel,
        in_specs=[pl.BlockSpec(memory_space=pltpu.SMEM), vmem, anywhere, vmem, anywhere] + [vmem] * 4,
        out_specs=[vmem] * 2 + [anywhere] * 4,
        out_shape=[
            jax.ShapeDtypeStruct((width, rows), f32),
            jax.ShapeDtypeStruct((1, rows), f32),
            jax.ShapeDtypeStruct((width, rows), bf16),
            jax.ShapeDtypeStruct((1, rows), f32),
            jax.ShapeDtypeStruct((3, nrel // 6, width, LANES), bf16),
            jax.ShapeDtypeStruct((3, nrel // 6, width, LANES), bf16),
        ],
        scratch_shapes=[
            pltpu.VMEM((nrel, width, LANES), bf16),
            pltpu.VMEM((width, rows), bf16),
            pltpu.VMEM((1, rows), f32),
            pltpu.VMEM((width, rows), bf16),
            pltpu.VMEM((width, rows), bf16),
            pltpu.VMEM((rows, width), bf16),
            pltpu.VMEM((rows, edges), bf16),
            pltpu.VMEM((width, edges), bf16),
            pltpu.VMEM((width, edges), bf16),
            pltpu.VMEM((width, edges), bf16),
            pltpu.VMEM((rows, edges), bf16),
            pltpu.VMEM((1, edges), f32),
            pltpu.VMEM((2, rows, edges // nblk), f32),
            pltpu.VMEM((nblk, rows, 128), bf16),
            pltpu.VMEM((neg.shape[0], width, width), f32),
            pltpu.VMEM((width, rows), f32),
            pltpu.VMEM((1, rows), f32),
            pltpu.VMEM((buckets - 1, width, rows), bf16),
            pltpu.VMEM((buckets - 1, 1, rows), f32),
            pltpu.SemaphoreType.DMA((2,)),
            pltpu.SemaphoreType.DMA((nrel // 2,)),
        ]
        + dma(2 * third) + dma(6 * third) + dma(1) + dma(8 * third) + dma(buckets) + dma(buckets) + dma(nrel // 2),
        compiler_params=pltpu.CompilerParams(
            collective_id=0, has_side_effects=True, vmem_limit_bytes=VMEM_LIMIT
        ),
        name="train_buckets",
    )(info, own, left, lacc, right, racc, src, tgt, neg)


def row_of(t):
    return 25 * t // 2


def last_window(s, t):
    if s == 0:
        base, top = 96 * (t // 8) + 48 * ((t // 4) % 2), 48
    elif s == 1:
        base, top = 192 * (t // 16) + 48 * ((t // 4) % 4), 48
    else:
        z = (t // 2) % 4
        base, top = 96 * (t // 8) + 16 * z + 16 * (z // 2), 32
    part = row_of(t) - base
    local = 16 * (part // 16) - 16 * (part // top)
    return base + local, local


def window(start, size):
    return pl.ds(pl.multiple_of(start, 16), size)


def total(out, own, parts):
    value = own.astype(jnp.float32)
    for part in parts:
        value = value + part.astype(jnp.float32)
    out[...] = value.astype(out.dtype)


def reduce_kernel(
    grads_ref, near_ref, out_ref, own, near,
    a0, b0, c0, a1, b1, c1, a2, b2, c2, m0, n0, m1, n1, m2, n2, own_sem, near_sem, send_sem, recv_sem,
):
    z, ylo, x, yhi, core = place()
    sems = (send_sem, recv_sem)
    z_at = [(z + d) % 4 for d in (1, 2, 3)]
    x_at = [(x + d) % 4 for d in (1, 2, 3)]
    y_at = [(yhi, 1 - ylo), (1 - yhi, ylo), (1 - yhi, 1 - ylo)]
    z_ring = [device(v, ylo, x, yhi, core) for v in z_at]
    x_ring = [device(z, ylo, v, yhi, core) for v in x_at]
    y_ring = [device(z, v, x, h, core) for h, v in y_at]
    mine, pairs = [], []
    for s in range(3):
        pairs.append(pltpu.make_async_copy(near_ref.at[s], near.at[s], near_sem.at[s]))
        mine.append(pltpu.make_async_copy(grads_ref.at[s], own.at[s], own_sem.at[s]))
        pairs[-1].start()
        mine[-1].start()
    greet(z_ring + x_ring + y_ring)

    first = []
    for s in range(3):
        mine[s].wait()
        pairs[s].wait()
        for i in range(4):
            total(own.at[s, i], own[s, i], [near[s, i]])
        for d in range(3):
            if s == 0:
                src = own.at[s, :, window(96 * z_at[d], 112)]
                copy = send(src, a0.at[d], sems, 3 + s * 3 + d, z_ring[d])
            elif s == 1:
                h, v = y_at[d]
                src = own.at[s, pl.ds(2 * h, 2), window(192 * v, 208)]
                copy = send(src, a1.at[d], sems, 3 + s * 3 + d, y_ring[d])
            else:
                src = own.at[s, :, window(96 * x_at[d], 112)]
                copy = send(src, a2.at[d], sems, 3 + s * 3 + d, x_ring[d])
            first.append(copy)

    second = []
    for s in range(3):
        for d in range(3):
            first[s * 3 + d].wait()
        if s == 0:
            total(m0, own[s, :, window(96 * z, 112)], [a0[d] for d in range(3)])
        elif s == 1:
            total(m1, own[s, pl.ds(2 * yhi, 2), window(192 * ylo, 208)], [a1[d] for d in range(3)])
        else:
            total(m2, own[s, :, window(96 * x, 112)], [a2[d] for d in range(3)])
        for d in range(3):
            if s == 0:
                h, v = y_at[d]
                copy = send(m0.at[pl.ds(2 * h, 2), window(48 * v, 64)], b0.at[d], sems, 12 + s * 3 + d, y_ring[d])
            elif s == 1:
                copy = send(m1.at[:, window(48 * x_at[d], 64)], b1.at[d], sems, 12 + s * 3 + d, x_ring[d])
            else:
                v = z_at[d]
                copy = send(m2.at[:, window(16 * v + 16 * (v // 2), 48)], b2.at[d], sems, 12 + s * 3 + d, z_ring[d])
            second.append(copy)

    third = []
    for s in range(3):
        for d in range(3):
            second[s * 3 + d].wait()
        if s == 0:
            total(n0, m0[pl.ds(2 * yhi, 2), window(48 * ylo, 64)], [b0[d] for d in range(3)])
        elif s == 1:
            total(n1, m1[:, window(48 * x, 64)], [b1[d] for d in range(3)])
        else:
            total(n2, m2[:, window(16 * z + 16 * (z // 2), 48)], [b2[d] for d in range(3)])
        for d in range(3):
            if s == 0:
                _, at = last_window(0, z * 8 + ylo * 4 + x_at[d])
                copy = send(n0.at[:, window(at, 32)], c0.at[d], sems, 21 + s * 3 + d, x_ring[d])
            elif s == 1:
                _, at = last_window(1, ylo * 16 + x * 4 + z_at[d])
                copy = send(n1.at[:, window(at, 32)], c1.at[d], sems, 21 + s * 3 + d, z_ring[d])
            else:
                h, v = y_at[d]
                _, at = last_window(2, x * 8 + z * 2 + v)
                copy = send(n2.at[pl.ds(2 * h, 2), window(at, 32)], c2.at[d], sems, 21 + s * 3 + d, y_ring[d])
            third.append(copy)

    for s in range(3):
        for d in range(3):
            third[s * 3 + d].wait()
        if s == 0:
            _, at = last_window(0, z * 8 + ylo * 4 + x)
            total(out_ref.at[s], n0[:, window(at, 32)], [c0[d] for d in range(3)])
        elif s == 1:
            _, at = last_window(1, ylo * 16 + x * 4 + z)
            total(out_ref.at[s], n1[:, window(at, 32)], [c1[d] for d in range(3)])
        else:
            _, at = last_window(2, x * 8 + z * 2 + ylo)
            total(out_ref.at[s], n2[pl.ds(2 * yhi, 2), window(at, 32)], [c2[d] for d in range(3)])


def reduce_call(grads, near):
    _, four, rows, lanes = grads.shape
    buf = lambda *shape: pltpu.VMEM(shape + (lanes,), jnp.bfloat16)
    return pl.pallas_call(
        reduce_kernel,
        in_specs=[pl.BlockSpec(memory_space=pl.ANY)] * 2,
        out_specs=pl.BlockSpec(memory_space=pltpu.VMEM),
        out_shape=jax.ShapeDtypeStruct((3, 2, 32, lanes), jnp.float32),
        scratch_shapes=[
            buf(3, four, rows), buf(3, four, rows),
            buf(3, 4, 112), buf(3, 2, 64), buf(3, 2, 32),
            buf(3, 2, 208), buf(3, 2, 64), buf(3, 2, 32),
            buf(3, 4, 112), buf(3, 4, 48), buf(3, 2, 32),
            buf(4, 112), buf(2, 64), buf(2, 208), buf(2, 64), buf(4, 112), buf(4, 48),
            pltpu.SemaphoreType.DMA((3,)), pltpu.SemaphoreType.DMA((3,)), pltpu.SemaphoreType.DMA((30,)), pltpu.SemaphoreType.DMA((30,)),
        ],
        compiler_params=pltpu.CompilerParams(
            collective_id=1, has_side_effects=True, vmem_limit_bytes=VMEM_LIMIT
        ),
        name="reduce_operator_gradients",
    )(grads, near)


def final_share(pieces, width):
    blk = lax.axis_size("blk")
    place_1 = lambda b: ((b // 4) % 2) * 16 + (b % 4) * 4 + b // 8
    place_2 = lambda b: (b % 4) * 8 + (b // 8) * 2 + (b // 4) % 2
    t = lax.axis_index("blk")
    shares = []
    for s, at in enumerate((None, place_1, place_2)):
        piece = pieces[s, :, :, :width]
        if at is not None:
            piece = lax.ppermute(piece, "blk", [(b, at(b)) for b in range(blk)])
        start, _ = last_window(s, t)
        skip = t * (width * width // blk) - start * width
        flat = piece.reshape(2, 32 * width)
        shares.append(lax.dynamic_slice(flat, (0, skip), (2, width * width // blk)))
    return jnp.concatenate(shares, axis=0)


def body(left, left_state, right, right_state, operators, need_list, block_slot, sources, targets, negatives):
    owned_count, width, _ = operators.shape
    owners = lax.axis_size("rel")
    nrel = owned_count * owners
    rel = need_list[0].reshape(-1)[block_slot[0].reshape(-1)]
    blocks = rel.shape[0]
    at = jnp.arange(blocks, dtype=jnp.int32)
    latest = lambda found: jnp.max(jnp.where(found, at, -1), axis=1)
    before = latest((rel[:, None] == rel[None, :]) & (at[None, :] < at[:, None]))
    last = latest(rel[None, :] == jnp.arange(nrel, dtype=jnp.int32)[:, None])
    before, last = (jnp.where(found < 0, blocks, found) for found in (before, last))
    info = jnp.concatenate([rel, before, last])
    src = sources[0][:, None]
    tgt = targets[0][:, None]
    neg = negatives[0].reshape(-1, 1, negatives.shape[-1])
    L, LS, R, RS, partial, near = train_call(
        info, operators, left.T, left_state[None], right.T, right_state[None], src, tgt, neg, nrel
    )
    op_grad = final_share(reduce_call(partial, near), width)
    return (L.T, LS[0], R.T.astype(jnp.float32), RS[0], op_grad)


def solution(mesh):
    in_specs = (
        P(("blk", "rel"), None),
        P(("blk", "rel")),
        P(("blk", "rel"), None),
        P(("blk", "rel")),
        P("rel", None, None),
        P(("blk", "rel"), None, None),
        P(("blk", "rel"), None, None),
        P(("blk", "rel"), None, None),
        P(("blk", "rel"), None, None),
        P(("blk", "rel"), None, None, None),
    )
    out_specs = (
        P(("blk", "rel"), None),
        P(("blk", "rel")),
        P(("blk", "rel"), None),
        P(("blk", "rel")),
        P("rel", "blk"),
    )
    return jax.shard_map(body, mesh=mesh, in_specs=in_specs, out_specs=out_specs, check_vma=False)
```

time: 234 us -> 191 us (0.82)
  Pallas kernels: 187 us -> 163 us
  waiting for transfers between devices: 24.4 us -> 8.03 us
  starting transfers between devices: 10.8 us -> 8.05 us
    ppermute x2 -> x0, waiting for transfers between devices: 21.3 us -> none  [from_behind(): return lax.ppermute(value, axis, pairs)]
    pallas_call x1 -> x0, Pallas kernels: 16.3 us -> none  [opgrad_call(): pl.pallas_call(functools.partial(opgrad_kernel, nrel), grid_spec=pltpu.Pr...]
    pallas_call x1, Pallas kernels: 51.4 us -> 42.2 us  [reduce_call(): pl.pallas_call(reduce_kernel, in_specs=[pl.BlockSpec(memory_space=pl.ANY)...]
    ppermute x2, waiting for transfers between devices: 3.14 us -> 8.03 us  [final_share(): piece = lax.ppermute(piece, 'blk', [(b, at(b)) for b in range(blk)])]
    ppermute x2 -> x0, starting transfers between devices: 3.63 us -> none  [from_behind(): return lax.ppermute(value, axis, pairs)]
  transfers between devices with their start and end apart: 4 -> 2, of which waited for: 2 -> 2; matrix products, arithmetic and copies ran while one was open for 1% -> 1% of each run, Pallas kernels for 0% -> 0%
where the time goes in v3:
time: 191 us; the launch traced here: 190 us
  Pallas kernels  163 us (85%)
  starting transfers between devices  8.05 us (4%)
  waiting for transfers between devices  8.03 us (4%)
  local copies, waits for them, and re-layouts  7.3 us (4%)
  other arithmetic  3.57 us (2%)
    pallas_call x1, Pallas kernels, train_call(): pl.pallas_call(train_kernel, in_specs=[pl.BlockSpec(memory_space=pltpu.SM...  120 us
    pallas_call x1, Pallas kernels, reduce_call(): pl.pallas_call(reduce_kernel, in_specs=[pl.BlockSpec(memory_space=pl.ANY)...  42.2 us
    ppermute x2, starting transfers between devices, final_share(): piece = lax.ppermute(piece, 'blk', [(b, at(b)) for b in range(blk)])  8.05 us
    ppermute x2, waiting for transfers between devices, final_share(): piece = lax.ppermute(piece, 'blk', [(b, at(b)) for b in range(blk)])  8.03 us
  transfers between devices with their start and end apart: 2, of which 2 were waited for; matrix products, arithmetic and copies ran while one was open for 1% of the time, Pallas kernels for 0%

profile of v3, /device:TPU:8, one launch (start us, length us, event | category | flops | bytes accessed | tf_op | source)
XLA Modules:
  0.0 190.4 jit_solution(8078068770424410085)
XLA Ops:
  0.6 0.7 reduce
  1.3 0.1 reshape_squeeze.13
  1.4 0.8 reshape_squeeze.12
  2.2 0.7 gather_fusion
  2.9 0.2 select_reduce_fusion.1
  3.1 1.4 reshape_squeeze.14.neg_ref
  4.5 0.6 pad_add_fusion.info_ref
  5.1 120.4 %train_buckets.1 = (f32[400,1024]{1,0:T(8,128)}, f32[1,1024]{1,0:T(1,128)}, bf16[400,1024]{1,0:T(8,128)(2,1)}, f32[1,1024]{1,0:T(1,128)}, bf16[3,4,400,512]{3,2,...) custom-call(s32[72]{0:T(128)} %pad_add_fusion.info_ref, bf16[6,400,400]{2,1,0:T(8,128)(2,1)} %own_ref.1, ...), custom_call_target="tpu_custom_call" | custom-call | tf_op jit(solution)/shard_map/train_buckets/pallas_call | solution.py:304
  125.5 42.2 %reduce_operator_gradients.1 = f32[3,2,32,512]{3,2,1,0:T(8,128)} custom-call(bf16[3,4,400,512]{3,2,1,0:T(8,128)(2,1)} %get-tuple-element.15.grads_ref, bf16[3,4,400,512]{3,2,1,0:T(8,128)(2,1)} %get-tuple-element.16.near_ref), custom_call_target="tpu_custom_call" | custom-call | tf_op jit(solution)/shard_map/reduce_operator_gradients/pallas_call | solution.py:475
  167.7 0.0 copy-start.1
  167.7 1.1 fusion.2
  168.8 6.1 %collective-permute-start = (f32[2,32,400]{2,1,0:T(8,128)S(1)}, f32[2,32,400]{2,1,0:T(8,128)S(1)}, u32[]{:S(2)}, u32[]{:S(2)}) collective-permute-start(f32[2,32,400]{2,1,0:T(8,128)S(1)} %get-tuple-element.21), channel_id=1, source_target_pairs={{0,0},{4,16},{8,32},{12,48},{16,64},{20,80},{24,96},{28,112},{32,4... | collective-permute-start | bytes 307208 | tf_op jit(solution)/shard_map/ppermute | solution.py:504
  174.9 1.9 %collective-permute-start.1 = (f32[2,32,400]{2,1,0:T(8,128)S(1)}, f32[2,32,400]{2,1,0:T(8,128)S(1)}, u32[]{:S(2)}, u32[]{:S(2)}) collective-permute-start(f32[2,32,400]{2,1,0:T(8,128)S(1)} %get-tuple-element.20), channel_id=1, source_target_pairs={{0,0},{4,32},{8,64},{12,96},{16,4},{20,36},{24,68},{28,100},{32,8}... | collective-permute-start | bytes 307208 | tf_op jit(solution)/shard_map/ppermute | solution.py:504
  177.0 0.2 reshape_squeeze.15
  177.2 0.1 constant_dynamic-slice_fusion.2
  177.3 0.0 copy-done.1
  177.3 0.0 copy-start
  177.3 1.3 convert_bitcast_fusion
  178.7 0.2 collective-permute-done
  178.8 0.2 reshape.46
  179.0 0.1 constant_dynamic-slice_fusion.1
  179.1 7.9 %collective-permute-done.1 = f32[2,32,400]{2,1,0:T(8,128)S(1)} collective-permute-done((f32[2,32,400]{2,1,0:T(8,128)S(1)}, f32[2,32,400]{2,1,0:T(8,128)S(1)}, u32[]{:S(2)}, u32[]{:S(2)}) %collective-permute-start.1) | collective-permute-done | bytes 102432 | tf_op jit(solution)/shard_map/ppermute | solution.py:504
  187.0 0.2 reshape.47
  187.2 0.1 constant_dynamic-slice_fusion
  187.3 0.7 pad_maximum_fusion
  188.0 0.0 copy-done
  188.0 0.0 copy-start.3
  188.0 0.0 copy-start.2
  188.0 1.2 copy.18
  189.2 0.0 copy-done.3
  189.2 0.6 copy.19
  189.8 0.0 copy-done.2
  189.8 0.6 copy.20
  (3 shorter events, 0.0 us)
Async XLA Ops:
  167.7 9.6 %copy-start.1 = (bf16[400,1024]{1,0:T(8,128)(2,1)S(1)}, bf16[400,1024]{1,0:T(8,128)(2,1)}, u32[]{:S(2)}) copy-start(bf16[400,1024]{1,0:T(8,128)(2,1)} %get-tuple-element.13) | copy-start | bytes 2457604
  168.8 10.0 %collective-permute-start = (f32[2,32,400]{2,1,0:T(8,128)S(1)}, f32[2,32,400]{2,1,0:T(8,128)S(1)}, u32[]{:S(2)}, u32[]{:S(2)}) collective-permute-start(f32[2,32,400]{2,1,0:T(8,128)S(1)} %get-tuple-element.21), channel_id=1, source_target_pairs={{0,0},{4,16},{8,32},{12,48},{16,64},{20,80},{24,96},{28,112},{32,4... | collective-permute-start | bytes 307208 | tf_op jit(solution)/shard_map/ppermute | solution.py:504
  174.9 12.0 %collective-permute-start.1 = (f32[2,32,400]{2,1,0:T(8,128)S(1)}, f32[2,32,400]{2,1,0:T(8,128)S(1)}, u32[]{:S(2)}, u32[]{:S(2)}) collective-permute-start(f32[2,32,400]{2,1,0:T(8,128)S(1)} %get-tuple-element.20), channel_id=1, source_target_pairs={{0,0},{4,32},{8,64},{12,96},{16,4},{20,36},{24,68},{28,100},{32,8}... | collective-permute-start | bytes 307208 | tf_op jit(solution)/shard_map/ppermute | solution.py:504
  177.3 10.7 %copy-start = (f32[400,1024]{1,0:T(8,128)S(1)}, f32[400,1024]{1,0:T(8,128)}, u32[]{:S(2)}) copy-start(f32[400,1024]{1,0:T(8,128)} %get-tuple-element.11) | copy-start | bytes 4915204
  188.0 1.2 copy-start.3
  188.0 1.8 copy-start.2

commit v4 on v3

--- a/solution.py
+++ b/solution.py
@@ -83,8 +83,9 @@
     units = owned * UNITS
     third = units // 8
     edges = src_ref.shape[2]
-    block = neg_ref.shape[2]
-    nblk = edges // block
+    nblk = (info_ref.shape[0] - table.shape[0]) // 2 // BUCKETS
+    block = edges // nblk
+    half_rows = rows // 2
     nrel = table.shape[0]
     total_blocks = BUCKETS * nblk
     blks = 32
@@ -125,13 +126,12 @@
             heads_now[:, cols] = dot(half[...], hot[:, cols]).astype(jnp.bfloat16)
 
     def counts(t):
-        def step(k, carry):
-            hits = onehot(neg_ref[t * nblk + k], rows)
-            ones = jnp.ones((block, 128), jnp.bfloat16)
-            count[k] = (dot(hits, ones) * (1.0 / block)).astype(jnp.bfloat16)
-            return carry
-
-        lax.fori_loop(0, nblk, step, 0)
+        found = jnp.zeros((rows, 128), jnp.float32)
+        for c in range(0, edges, CHUNK):
+            of = (lax.broadcasted_iota(jnp.int32, (CHUNK, 128), 0) + c) // block
+            share = jnp.where(of == lax.broadcasted_iota(jnp.int32, (CHUNK, 128), 1), 1.0 / block, 0.0)
+            found += dot(onehot(neg_ref[t, :, c : c + CHUNK], rows), share.astype(jnp.bfloat16))
+        count[t] = found
 
     def clear(n, carry):
         sums[n] = jnp.zeros(sums.shape[1:], jnp.float32)
@@ -154,9 +154,8 @@
                     part, part, (ring_s, ring_r), (ring * 3 + d - 1) * third + i, rings[ring][d - 1]
                 )
             copies.append(send(part, part, (pass_s, pass_r), ring * 4 * third + i, sibling))
-        if i == 0:
-            counts(0)
-        elif i == 1:
+        counts(i)
+        if i == 1:
             lax.fori_loop(0, sums.shape[0], clear, 0)
     for i in range(third):
         for ring in range(2):
@@ -174,77 +173,85 @@
     def earlier(n):
         return jnp.where(n < total_blocks, sums[jnp.minimum(n, total_blocks - 1)], 0.0)
 
-    def moves(t):
+    def moves(t, c, to_rows, to_acc):
+        part = pl.ds(c * half_rows, half_rows)
         return (
-            remote(fresh_ref, in_rows.at[t], (move_s, move_r), t, ahead),
-            remote(freshacc_ref, in_acc.at[t], (acc_s, acc_r), t, ahead),
+            remote(fresh_ref.at[:, part], to_rows.at[:, part], (move_s, move_r), 2 * t + c, ahead),
+            remote(freshacc_ref.at[:, part], to_acc.at[:, part], (acc_s, acc_r), 2 * t + c, ahead),
         )
 
-    last_moves = (
-        remote(fresh_ref, newright_ref, (move_s, move_r), BUCKETS - 1, ahead),
-        remote(freshacc_ref, newracc_ref, (acc_s, acc_r), BUCKETS - 1, ahead),
-    )
-
-    def bucket(t, carry):
+    def queries(t):
         for k in range(nblk):
             cols = slice(k * block, (k + 1) * block)
             query[:, cols] = dot(operator(t, k), heads_now[:, cols], TN).astype(jnp.bfloat16)
-        rhalf[...] = rows_now[...].astype(jnp.bfloat16)
-        rhalf_t[...] = rhalf[...].T
-
-        def meet(k, slot):
-            cols = pl.ds(pl.multiple_of(k * block, block), block)
-            value = dot(rhalf_t[...], query[:, cols])
-            score[slot] = value
-            hit = lax.broadcasted_iota(jnp.int32, (rows, block), 0) == tgt_ref[t, :, cols]
-            pos = jnp.sum(jnp.where(hit, value, 0.0), axis=0, keepdims=True)
-            scale[:, cols] = jax.nn.sigmoid(-pos)
-
-        def weigh(k, slot):
-            cols = pl.ds(pl.multiple_of(k * block, block), block)
-            pull = scale[:, cols]
-            size = jnp.maximum(pull, 2.0**-8)
-            inverse = 1.0 / size
-            times = jnp.concatenate([count[k]] * (block // 128), axis=1)
-            twice = (jnp.tanh(0.5 * score[slot]) + 1.0).astype(jnp.bfloat16)
-            hit = onehot(tgt_ref[t, :, cols], rows)
-            push[:, cols] = twice * (0.5 * inverse).astype(jnp.bfloat16) * times - hit * (pull * inverse).astype(
-                jnp.bfloat16
-            )
-            scale[:, cols] = size
-            scaled[:, cols] = (query[:, cols].astype(jnp.float32) * size).astype(jnp.bfloat16)
-
-        def two(j, carry):
-            meet(2 * j + 1, 1)
-            weigh(2 * j, 0)
-            meet(2 * j + 2, 0)
-            weigh(2 * j + 1, 1)
-            return carry
-
-        meet(0, 0)
-        lax.fori_loop(0, nblk // 2 - 1, two, 0)
-        meet(nblk - 1, 1)
-        weigh(nblk - 2, 0)
-        weigh(nblk - 1, 1)
-        for c in range(0, rows, CHUNK):
-            part = slice(c, c + CHUNK)
+
+    def start(copies):
+        for copy in copies:
+            copy.start()
+
+    def bucket(t, carry):
+        for c in range(2):
+            part = slice(c * half_rows, (c + 1) * half_rows)
+
+            @pl.when(t > 0)
+            def _():
+                for move in moves(t - 1, c, in_rows.at[t - 1], in_acc.at[t - 1]):
+                    move.wait()
+                rows_now[:, part] = in_rows[t - 1, :, part].astype(jnp.float32)
+                acc_now[:, part] = in_acc[t - 1, :, part]
+
+            rhalf[:, part] = rows_now[:, part].astype(jnp.bfloat16)
+            rhalf_t[part, :] = rhalf[:, part].T
+
+            def meet(j):
+                cols = slice(j * CHUNK, (j + 1) * CHUNK)
+                value = dot(rhalf_t[part, :], query[:, cols])
+                score[j % 2] = value
+                target = tgt_ref[t, :, cols] - c * half_rows
+                hit = lax.broadcasted_iota(jnp.int32, (half_rows, CHUNK), 0) == target
+                pos = jnp.sum(jnp.where(hit, value, 0.0), axis=0, keepdims=True)
+                scale[c, :, cols] = jax.nn.sigmoid(-pos)
+
+            def weigh(j):
+                cols = slice(j * CHUNK, (j + 1) * CHUNK)
+                target = tgt_ref[t, :, cols] - c * half_rows
+                pull = scale[c, :, cols]
+                size = jnp.where((target >= 0) & (target < half_rows), jnp.maximum(pull, 2.0**-8), 1.0)
+                inverse = 1.0 / size
+                times = [
+                    jnp.broadcast_to(count[t, part, k : k + 1], (half_rows, block)).astype(jnp.bfloat16)
+                    for k in range(j * CHUNK // block, (j + 1) * CHUNK // block)
+                ]
+                twice = (jnp.tanh(0.5 * score[j % 2]) + 1.0).astype(jnp.bfloat16)
+                push[part, cols] = twice * (0.5 * inverse).astype(jnp.bfloat16) * jnp.concatenate(
+                    times, axis=1
+                ) - onehot(target, half_rows) * (pull * inverse).astype(jnp.bfloat16)
+                scale[c, :, cols] = size
+                scaled[:, cols] = (query[:, cols].astype(jnp.float32) * size).astype(jnp.bfloat16)
+
+            meet(0)
+            for j in range(1, edges // CHUNK):
+                meet(j)
+                weigh(j - 1)
+            weigh(edges // CHUNK - 1)
             fresh, acc = adagrad(rows_now[:, part], acc_now[:, part], dot(scaled[...], push[part, :], NT))
             fresh_ref[:, part] = fresh.astype(jnp.bfloat16)
             freshacc_ref[:, part] = acc
 
-        @pl.when(t < BUCKETS - 1)
-        def _():
-            for move in moves(t):
-                move.start()
-
-        @pl.when(t == BUCKETS - 1)
-        def _():
-            for move in last_moves:
-                move.start()
-
-        for c in range(0, edges, CHUNK):
-            cols = slice(c, c + CHUNK)
-            scaled[:, cols] = (dot(rhalf[...], push[:, cols]) * scale[:, cols]).astype(jnp.bfloat16)
+            @pl.when(t < BUCKETS - 1)
+            def _():
+                start(moves(t, c, in_rows.at[t], in_acc.at[t]))
+
+            @pl.when(t == BUCKETS - 1)
+            def _():
+                start(moves(BUCKETS - 1, c, newright_ref, newracc_ref))
+
+        for j in range(0, edges, CHUNK):
+            cols = slice(j, j + CHUNK)
+            scaled[:, cols] = (
+                dot(rhalf[:, :half_rows], push[:half_rows, cols]) * scale[0, :, cols]
+                + dot(rhalf[:, half_rows:], push[half_rows:, cols]) * scale[1, :, cols]
+            ).astype(jnp.bfloat16)
         for k in range(nblk):
             cols = slice(k * block, (k + 1) * block)
             query[:, cols] = dot(operator(t, k), scaled[:, cols]).astype(jnp.bfloat16)
@@ -262,14 +269,11 @@
         @pl.when(t < BUCKETS - 1)
         def _():
             heads(t + 1)
-            counts(t + 1)
-            for move in moves(t):
-                move.wait()
-            rows_now[...] = in_rows[t].astype(jnp.float32)
-            acc_now[...] = in_acc[t]
+            queries(t + 1)
 
         return carry
 
+    queries(0)
     lax.fori_loop(0, BUCKETS, bucket, 0)
 
     copies = []
@@ -286,17 +290,17 @@
             copies.append(copy)
     for copy in copies:
         copy.wait()
-    for move in last_moves:
-        move.wait()
-
-
-def train_call(info, own, left, lacc, right, racc, src, tgt, neg, nrel):
+    for c in range(2):
+        for move in moves(BUCKETS - 1, c, newright_ref, newracc_ref):
+            move.wait()
+
+
+def train_call(info, own, left, lacc, right, racc, src, tgt, neg, nrel, nblk):
     width, rows = left.shape
     owned = own.shape[0]
     units = owned * UNITS
     third = units // 8
     buckets, _, edges = src.shape
-    nblk = neg.shape[0] // buckets
     dma = lambda n: [pltpu.SemaphoreType.DMA((n,))] * 2
     vmem = pl.BlockSpec(memory_space=pltpu.VMEM)
     anywhere = pl.BlockSpec(memory_space=pl.ANY)
@@ -325,10 +329,10 @@
             pltpu.VMEM((width, edges), bf16),
             pltpu.VMEM((width, edges), bf16),
             pltpu.VMEM((rows, edges), bf16),
-            pltpu.VMEM((1, edges), f32),
-            pltpu.VMEM((2, rows, edges // nblk), f32),
-            pltpu.VMEM((nblk, rows, 128), bf16),
-            pltpu.VMEM((neg.shape[0], width, width), f32),
+            pltpu.VMEM((2, 1, edges), f32),
+            pltpu.VMEM((2, rows // 2, CHUNK), f32),
+            pltpu.VMEM((buckets, rows, 128), f32),
+            pltpu.VMEM((buckets * nblk, width, width), f32),
             pltpu.VMEM((width, rows), f32),
             pltpu.VMEM((1, rows), f32),
             pltpu.VMEM((buckets - 1, width, rows), bf16),
@@ -336,7 +340,7 @@
             pltpu.SemaphoreType.DMA((2,)),
             pltpu.SemaphoreType.DMA((nrel // 2,)),
         ]
-        + dma(2 * third) + dma(6 * third) + dma(1) + dma(8 * third) + dma(buckets) + dma(buckets) + dma(nrel // 2),
+        + dma(2 * third) + dma(6 * third) + dma(1) + dma(8 * third) + dma(2 * buckets) + dma(2 * buckets) + dma(nrel // 2),
         compiler_params=pltpu.CompilerParams(
             collective_id=0, has_side_effects=True, vmem_limit_bytes=VMEM_LIMIT
         ),
@@ -523,9 +527,9 @@
     info = jnp.concatenate([rel, before, last])
     src = sources[0][:, None]
     tgt = targets[0][:, None]
-    neg = negatives[0].reshape(-1, 1, negatives.shape[-1])
+    neg = negatives[0].reshape(BUCKETS, 1, -1)
     L, LS, R, RS, partial, near = train_call(
-        info, operators, left.T, left_state[None], right.T, right_state[None], src, tgt, neg, nrel
+        info, operators, left.T, left_state[None], right.T, right_state[None], src, tgt, neg, nrel, block_slot.shape[-1]
     )
     op_grad = final_share(reduce_call(partial, near), width)
     return (L.T, LS[0], R.T.astype(jnp.float32), RS[0], op_grad)

time: 191 us -> 169 us (0.88)
  Pallas kernels: 163 us -> 139 us
  waiting for transfers between devices: 8.03 us -> 10.5 us
    pallas_call x1, Pallas kernels: 120 us -> 95.7 us  [train_call(): pl.pallas_call(train_kernel, in_specs=[pl.BlockSpec(memory_space=pltpu.SM...]
    ppermute x2, waiting for transfers between devices: 8.03 us -> 10.5 us  [final_share(): piece = lax.ppermute(piece, 'blk', [(b, at(b)) for b in range(blk)])]
where the time goes in v4:
time: 169 us
  Pallas kernels  139 us (82%)
  waiting for transfers between devices  10.5 us (6%)
  starting transfers between devices  7.46 us (4%)
  local copies, waits for them, and re-layouts  7.3 us (4%)
  other arithmetic  3.57 us (2%)
    pallas_call x1, Pallas kernels, train_call(): pl.pallas_call(train_kernel, in_specs=[pl.BlockSpec(memory_space=pltpu.SM...  95.7 us
    pallas_call x1, Pallas kernels, reduce_call(): pl.pallas_call(reduce_kernel, in_specs=[pl.BlockSpec(memory_space=pl.ANY)...  43.4 us
    ppermute x2, waiting for transfers between devices, final_share(): piece = lax.ppermute(piece, 'blk', [(b, at(b)) for b in range(blk)])  10.5 us
    ppermute x2, starting transfers between devices, final_share(): piece = lax.ppermute(piece, 'blk', [(b, at(b)) for b in range(blk)])  7.46 us
  transfers between devices with their start and end apart: 2, of which 2 were waited for; matrix products, arithmetic and copies ran while one was open for 1% of the time, Pallas kernels for 0%

profile of v4, /device:TPU:8, one launch (start us, length us, event | category | flops | bytes accessed | tf_op | source)
XLA Modules:
  0.0 168.8 jit_solution(13353698518124780103)
XLA Ops:
  0.6 0.7 reduce
  1.3 0.1 reshape_squeeze.13
  1.4 0.8 reshape_squeeze.12
  2.2 0.7 gather_fusion
  2.9 0.2 select_reduce_fusion.1
  3.1 1.4 reshape_squeeze.14.neg_ref
  4.5 0.6 pad_add_fusion.info_ref
  5.1 95.7 %train_buckets.1 = (f32[400,1024]{1,0:T(8,128)}, f32[1,1024]{1,0:T(1,128)}, bf16[400,1024]{1,0:T(8,128)(2,1)}, f32[1,1024]{1,0:T(1,128)}, bf16[3,4,400,512]{3,2,...) custom-call(s32[72]{0:T(128)} %pad_add_fusion.info_ref, bf16[6,400,400]{2,1,0:T(8,128)(2,1)} %own_ref.1, ...), custom_call_target="tpu_custom_call" | custom-call | tf_op jit(solution)/shard_map/train_buckets/pallas_call | solution.py:308
  100.7 43.4 %reduce_operator_gradients.1 = f32[3,2,32,512]{3,2,1,0:T(8,128)} custom-call(bf16[3,4,400,512]{3,2,1,0:T(8,128)(2,1)} %get-tuple-element.15.grads_ref, bf16[3,4,400,512]{3,2,1,0:T(8,128)(2,1)} %get-tuple-element.16.near_ref), custom_call_target="tpu_custom_call" | custom-call | tf_op jit(solution)/shard_map/reduce_operator_gradients/pallas_call | solution.py:479
  144.1 0.0 copy-start.1
  144.1 1.1 fusion.2
  145.3 5.5 %collective-permute-start = (f32[2,32,400]{2,1,0:T(8,128)S(1)}, f32[2,32,400]{2,1,0:T(8,128)S(1)}, u32[]{:S(2)}, u32[]{:S(2)}) collective-permute-start(f32[2,32,400]{2,1,0:T(8,128)S(1)} %get-tuple-element.21), channel_id=1, source_target_pairs={{0,0},{4,16},{8,32},{12,48},{16,64},{20,80},{24,96},{28,112},{32,4... | collective-permute-start | bytes 307208 | tf_op jit(solution)/shard_map/ppermute | solution.py:508
  150.8 1.9 %collective-permute-start.1 = (f32[2,32,400]{2,1,0:T(8,128)S(1)}, f32[2,32,400]{2,1,0:T(8,128)S(1)}, u32[]{:S(2)}, u32[]{:S(2)}) collective-permute-start(f32[2,32,400]{2,1,0:T(8,128)S(1)} %get-tuple-element.20), channel_id=1, source_target_pairs={{0,0},{4,32},{8,64},{12,96},{16,4},{20,36},{24,68},{28,100},{32,8}... | collective-permute-start | bytes 307208 | tf_op jit(solution)/shard_map/ppermute | solution.py:508
  152.9 0.2 reshape_squeeze.15
  153.1 0.1 constant_dynamic-slice_fusion.2
  153.2 0.0 copy-done.1
  153.2 0.0 copy-start
  153.2 1.3 convert_bitcast_fusion
  154.5 1.5 collective-permute-done
  156.0 0.2 reshape.46
  156.2 0.1 constant_dynamic-slice_fusion.1
  156.3 9.1 %collective-permute-done.1 = f32[2,32,400]{2,1,0:T(8,128)S(1)} collective-permute-done((f32[2,32,400]{2,1,0:T(8,128)S(1)}, f32[2,32,400]{2,1,0:T(8,128)S(1)}, u32[]{:S(2)}, u32[]{:S(2)}) %collective-permute-start.1) | collective-permute-done | bytes 102432 | tf_op jit(solution)/shard_map/ppermute | solution.py:508
  165.4 0.2 reshape.47
  165.6 0.1 constant_dynamic-slice_fusion
  165.7 0.7 pad_maximum_fusion
  166.4 0.0 copy-done
  166.4 0.0 copy-start.3
  166.4 0.0 copy-start.2
  166.4 1.2 copy.18
  167.6 0.0 copy-done.3
  167.6 0.6 copy.19
  168.2 0.0 copy-done.2
  168.2 0.6 copy.20
  (3 shorter events, 0.0 us)
Async XLA Ops:
  144.1 9.0 %copy-start.1 = (bf16[400,1024]{1,0:T(8,128)(2,1)S(1)}, bf16[400,1024]{1,0:T(8,128)(2,1)}, u32[]{:S(2)}) copy-start(bf16[400,1024]{1,0:T(8,128)(2,1)} %get-tuple-element.13) | copy-start | bytes 2457604
  145.3 10.7 %collective-permute-start = (f32[2,32,400]{2,1,0:T(8,128)S(1)}, f32[2,32,400]{2,1,0:T(8,128)S(1)}, u32[]{:S(2)}, u32[]{:S(2)}) collective-permute-start(f32[2,32,400]{2,1,0:T(8,128)S(1)} %get-tuple-element.21), channel_id=1, source_target_pairs={{0,0},{4,16},{8,32},{12,48},{16,64},{20,80},{24,96},{28,112},{32,4... | collective-permute-start | bytes 307208 | tf_op jit(solution)/shard_map/ppermute | solution.py:508
  150.8 14.5 %collective-permute-start.1 = (f32[2,32,400]{2,1,0:T(8,128)S(1)}, f32[2,32,400]{2,1,0:T(8,128)S(1)}, u32[]{:S(2)}, u32[]{:S(2)}) collective-permute-start(f32[2,32,400]{2,1,0:T(8,128)S(1)} %get-tuple-element.20), channel_id=1, source_target_pairs={{0,0},{4,32},{8,64},{12,96},{16,4},{20,36},{24,68},{28,100},{32,8}... | collective-permute-start | bytes 307208 | tf_op jit(solution)/shard_map/ppermute | solution.py:508
  153.2 13.2 %copy-start = (f32[400,1024]{1,0:T(8,128)S(1)}, f32[400,1024]{1,0:T(8,128)}, u32[]{:S(2)}) copy-start(f32[400,1024]{1,0:T(8,128)} %get-tuple-element.11) | copy-start | bytes 4915204
  166.4 1.2 copy-start.3
  166.4 1.8 %copy-start.2 = (f32[1,1024]{1,0:T(1,128)S(1)}, f32[1,1024]{1,0:T(1,128)}, u32[]{:S(2)}) copy-start(f32[1,1024]{1,0:T(1,128)} %get-tuple-element.14) | copy-start | bytes 12292

commit v5 on v4

--- a/solution.py
+++ b/solution.py
@@ -68,12 +68,40 @@
     return rows - STEP * grad * lax.rsqrt(acc), acc
 
 
+def row_of(t):
+    return 25 * t // 2
+
+
+def last_window(s, t):
+    if s == 0:
+        base, top = 96 * (t // 8) + 48 * ((t // 4) % 2), 48
+    elif s == 1:
+        base, top = 192 * (t // 16) + 48 * ((t // 4) % 4), 48
+    else:
+        z = (t // 2) % 4
+        base, top = 96 * (t // 8) + 16 * z + 16 * (z // 2), 32
+    part = row_of(t) - base
+    local = 16 * (part // 16) - 16 * (part // top)
+    return base + local, local
+
+
+def window(start, size):
+    return pl.ds(pl.multiple_of(start, 16), size)
+
+
+def total(out, own, parts):
+    value = own.astype(jnp.float32)
+    for part in parts:
+        value = value + part.astype(jnp.float32)
+    out[...] = value.astype(out.dtype)
+
+
 def train_kernel(
     info_ref, own_ref, left_ref, lacc_ref, right_ref, racc_ref, src_ref, tgt_ref, neg_ref,
-    newleft_ref, newlacc_ref, newright_ref, newracc_ref, grads_ref, near_ref,
+    newleft_ref, newlacc_ref, newright_ref, newracc_ref, out_ref,
     table, fresh_ref, freshacc_ref, half, rhalf, rhalf_t, hot, query, scaled, heads_now, push, scale, score, count, sums, rows_now, acc_now,
-    in_rows, in_acc, load_sem, store_sem,
-    cross_s, cross_r, ring_s, ring_r, whole_s, whole_r, pass_s, pass_r, move_s, move_r, acc_s, acc_r, near_s, near_r,
+    in_rows, in_acc, near, a0, b0, c0, a1, b1, c1, a2, b2, c2, load_sem,
+    cross_s, cross_r, ring_s, ring_r, whole_s, whole_r, pass_s, pass_r, move_s, move_r, acc_s, acc_r, near_s, near_r, sum_s, sum_r,
 ):
     z, ylo, x, yhi, core = place()
     me = yhi * 2 + core
@@ -101,7 +129,11 @@
     ]
     for load in loads:
         load.start()
-    greet([sibling, cross, ahead, behind] + x_ring + z_ring)
+    x_at = [(x + d) % 4 for d in (1, 2, 3)]
+    z_at = [(z + d) % 4 for d in (1, 2, 3)]
+    y_at = [(yhi, 1 - ylo), (1 - yhi, ylo), (1 - yhi, 1 - ylo)]
+    y_ring = [device(z, v, x, h, core) for h, v in y_at]
+    greet([sibling, ahead, behind] + x_ring + y_ring + z_ring)
 
     for j in range(owned):
         table[me * owned + j] = jnp.pad(own_ref[j], ((0, 0), (0, LANES - width)))
@@ -134,7 +166,7 @@
         count[t] = found
 
     def clear(n, carry):
-        sums[n] = jnp.zeros(sums.shape[1:], jnp.float32)
+        sums[n] = jnp.zeros(sums.shape[1:], sums.dtype)
         return carry
 
     newlacc_ref[...] = lacc_ref[...]
@@ -171,7 +203,7 @@
         return table[info_ref[t * nblk + k]][:, :width]
 
     def earlier(n):
-        return jnp.where(n < total_blocks, sums[jnp.minimum(n, total_blocks - 1)], 0.0)
+        return jnp.where(n < total_blocks, sums[jnp.minimum(n, total_blocks - 1)].astype(jnp.float32), 0.0)
 
     def moves(t, c, to_rows, to_acc):
         part = pl.ds(c * half_rows, half_rows)
@@ -264,7 +296,7 @@
         for k in range(nblk):
             cols = slice(k * block, (k + 1) * block)
             before = earlier(info_ref[total_blocks + t * nblk + k])
-            sums[t * nblk + k] = before + dot(heads_now[:, cols], scaled[:, cols], NT)
+            sums[t * nblk + k] = (before + dot(heads_now[:, cols], scaled[:, cols], NT)).astype(sums.dtype)
 
         @pl.when(t < BUCKETS - 1)
         def _():
@@ -276,20 +308,95 @@
     queries(0)
     lax.fori_loop(0, BUCKETS, bucket, 0)
 
-    copies = []
-    for here in (False, True):
-        for n in range(nrel // 2):
-            part, h, i = n // 4, n // 2 % 2, n % 2
-            j = (h * 2 + (core if here else 1 - core)) * owned + part * 2 + i
-            table[j, :, :width] = earlier(info_ref[2 * total_blocks + j]).astype(jnp.bfloat16)
-            if here:
-                copy = pltpu.make_async_copy(table.at[j], grads_ref.at[part, h * 2 + i], store_sem.at[n])
-                copy.start()
+    quarter = nrel // 6
+    half_count = nrel // 2
+
+    def relation(n, of_core):
+        part, h, i = n // quarter, n // 2 % 2, n % 2
+        return earlier(info_ref[2 * total_blocks + (h * 2 + of_core) * owned + part * 2 + i])
+
+    pairs = []
+    for n in range(half_count):
+        table[half_count + n, :, :width] = relation(n, 1 - core).astype(jnp.bfloat16)
+        pairs.append(send(table.at[half_count + n], near.at[n], (near_s, near_r), n, sibling))
+
+    sems = (sum_s, sum_r)
+    own = [table.at[pl.ds(s * quarter, quarter)] for s in range(3)]
+    first = []
+    for s in range(3):
+        for n in range(s * quarter, (s + 1) * quarter):
+            pairs[n].wait()
+            table[n, :, :width] = (relation(n, core) + near[n, :, :width].astype(jnp.float32)).astype(jnp.bfloat16)
+        for d in range(3):
+            if s == 0:
+                copy = send(own[s].at[:, window(96 * z_at[d], 112)], a0.at[d], sems, s * 3 + d, z_ring[d])
+            elif s == 1:
+                h, v = y_at[d]
+                copy = send(own[s].at[pl.ds(2 * h, 2), window(192 * v, 208)], a1.at[d], sems, s * 3 + d, y_ring[d])
             else:
-                copy = send(table.at[j], near_ref.at[part, h * 2 + i], (near_s, near_r), n, sibling)
-            copies.append(copy)
-    for copy in copies:
-        copy.wait()
+                copy = send(own[s].at[:, window(96 * x_at[d], 112)], a2.at[d], sems, s * 3 + d, x_ring[d])
+            first.append(copy)
+
+    second = []
+    for s in range(3):
+        for d in range(3):
+            first[s * 3 + d].wait()
+        if s == 0:
+            total(a0.at[0], own[s][:, window(96 * z, 112)], [a0[d] for d in range(3)])
+        elif s == 1:
+            total(a1.at[0], own[s][pl.ds(2 * yhi, 2), window(192 * ylo, 208)], [a1[d] for d in range(3)])
+        else:
+            total(a2.at[0], own[s][:, window(96 * x, 112)], [a2[d] for d in range(3)])
+        for d in range(3):
+            if s == 0:
+                h, v = y_at[d]
+                src = a0.at[0, pl.ds(2 * h, 2), window(48 * v, 64)]
+                copy = send(src, b0.at[d], sems, 9 + s * 3 + d, y_ring[d])
+            elif s == 1:
+                copy = send(a1.at[0, :, window(48 * x_at[d], 64)], b1.at[d], sems, 9 + s * 3 + d, x_ring[d])
+            else:
+                v = z_at[d]
+                src = a2.at[0, :, window(16 * v + 16 * (v // 2), 48)]
+                copy = send(src, b2.at[d], sems, 9 + s * 3 + d, z_ring[d])
+            second.append(copy)
+
+    third = []
+    for s in range(3):
+        for d in range(3):
+            second[s * 3 + d].wait()
+        if s == 0:
+            total(b0.at[0], a0[0, pl.ds(2 * yhi, 2), window(48 * ylo, 64)], [b0[d] for d in range(3)])
+        elif s == 1:
+            total(b1.at[0], a1[0, :, window(48 * x, 64)], [b1[d] for d in range(3)])
+        else:
+            total(b2.at[0], a2[0, :, window(16 * z + 16 * (z // 2), 48)], [b2[d] for d in range(3)])
+        for d in range(3):
+            if s == 0:
+                _, at = last_window(0, z * 8 + ylo * 4 + x_at[d])
+                copy = send(b0.at[0, :, window(at, 32)], c0.at[d], sems, 18 + s * 3 + d, x_ring[d])
+            elif s == 1:
+                _, at = last_window(1, ylo * 16 + x * 4 + z_at[d])
+                copy = send(b1.at[0, :, window(at, 32)], c1.at[d], sems, 18 + s * 3 + d, z_ring[d])
+            else:
+                h, v = y_at[d]
+                _, at = last_window(2, x * 8 + z * 2 + v)
+                src = b2.at[0, pl.ds(2 * h, 2), window(at, 32)]
+                copy = send(src, c2.at[d], sems, 18 + s * 3 + d, y_ring[d])
+            third.append(copy)
+
+    for s in range(3):
+        for d in range(3):
+            third[s * 3 + d].wait()
+        if s == 0:
+            _, at = last_window(0, z * 8 + ylo * 4 + x)
+            total(out_ref.at[s], b0[0, :, window(at, 32)], [c0[d] for d in range(3)])
+        elif s == 1:
+            _, at = last_window(1, ylo * 16 + x * 4 + z)
+            total(out_ref.at[s], b1[0, :, window(at, 32)], [c1[d] for d in range(3)])
+        else:
+            _, at = last_window(2, x * 8 + z * 2 + ylo)
+            total(out_ref.at[s], b2[0, pl.ds(2 * yhi, 2), window(at, 32)], [c2[d] for d in range(3)])
+
     for c in range(2):
         for move in moves(BUCKETS - 1, c, newright_ref, newracc_ref):
             move.wait()
@@ -305,17 +412,18 @@
     vmem = pl.BlockSpec(memory_space=pltpu.VMEM)
     anywhere = pl.BlockSpec(memory_space=pl.ANY)
     f32, bf16 = jnp.float32, jnp.bfloat16
+    four = nrel // 6
+    buf = lambda *shape: pltpu.VMEM(shape + (LANES,), bf16)
     return pl.pallas_call(
         train_kernel,
         in_specs=[pl.BlockSpec(memory_space=pltpu.SMEM), vmem, anywhere, vmem, anywhere] + [vmem] * 4,
-        out_specs=[vmem] * 2 + [anywhere] * 4,
+        out_specs=[vmem] * 2 + [anywhere] * 2 + [vmem],
         out_shape=[
             jax.ShapeDtypeStruct((width, rows), f32),
             jax.ShapeDtypeStruct((1, rows), f32),
             jax.ShapeDtypeStruct((width, rows), bf16),
             jax.ShapeDtypeStruct((1, rows), f32),
-            jax.ShapeDtypeStruct((3, nrel // 6, width, LANES), bf16),
-            jax.ShapeDtypeStruct((3, nrel // 6, width, LANES), bf16),
+            jax.ShapeDtypeStruct((3, 2, 32, LANES), f32),
         ],
         scratch_shapes=[
             pltpu.VMEM((nrel, width, LANES), bf16),
@@ -332,168 +440,23 @@
             pltpu.VMEM((2, 1, edges), f32),
             pltpu.VMEM((2, rows // 2, CHUNK), f32),
             pltpu.VMEM((buckets, rows, 128), f32),
-            pltpu.VMEM((buckets * nblk, width, width), f32),
+            pltpu.VMEM((buckets * nblk, width, width), bf16),
             pltpu.VMEM((width, rows), f32),
             pltpu.VMEM((1, rows), f32),
             pltpu.VMEM((buckets - 1, width, rows), bf16),
             pltpu.VMEM((buckets - 1, 1, rows), f32),
+            pltpu.VMEM((nrel // 2, width, LANES), bf16),
+            buf(3, four, 112), buf(3, 2, 64), buf(3, 2, 32),
+            buf(3, 2, 208), buf(3, 2, 64), buf(3, 2, 32),
+            buf(3, four, 112), buf(3, four, 48), buf(3, 2, 32),
             pltpu.SemaphoreType.DMA((2,)),
-            pltpu.SemaphoreType.DMA((nrel // 2,)),
         ]
-        + dma(2 * third) + dma(6 * third) + dma(1) + dma(8 * third) + dma(2 * buckets) + dma(2 * buckets) + dma(nrel // 2),
+        + dma(2 * third) + dma(6 * third) + dma(1) + dma(8 * third) + dma(2 * buckets) + dma(2 * buckets) + dma(nrel // 2) + dma(27),
         compiler_params=pltpu.CompilerParams(
             collective_id=0, has_side_effects=True, vmem_limit_bytes=VMEM_LIMIT
         ),
         name="train_buckets",
     )(info, own, left, lacc, right, racc, src, tgt, neg)
-
-
-def row_of(t):
-    return 25 * t // 2
-
-
-def last_window(s, t):
-    if s == 0:
-        base, top = 96 * (t // 8) + 48 * ((t // 4) % 2), 48
-    elif s == 1:
-        base, top = 192 * (t // 16) + 48 * ((t // 4) % 4), 48
-    else:
-        z = (t // 2) % 4
-        base, top = 96 * (t // 8) + 16 * z + 16 * (z // 2), 32
-    part = row_of(t) - base
-    local = 16 * (part // 16) - 16 * (part // top)
-    return base + local, local
-
-
-def window(start, size):
-    return pl.ds(pl.multiple_of(start, 16), size)
-
-
-def total(out, own, parts):
-    value = own.astype(jnp.float32)
-    for part in parts:
-        value = value + part.astype(jnp.float32)
-    out[...] = value.astype(out.dtype)
-
-
-def reduce_kernel(
-    grads_ref, near_ref, out_ref, own, near,
-    a0, b0, c0, a1, b1, c1, a2, b2, c2, m0, n0, m1, n1, m2, n2, own_sem, near_sem, send_sem, recv_sem,
-):
-    z, ylo, x, yhi, core = place()
-    sems = (send_sem, recv_sem)
-    z_at = [(z + d) % 4 for d in (1, 2, 3)]
-    x_at = [(x + d) % 4 for d in (1, 2, 3)]
-    y_at = [(yhi, 1 - ylo), (1 - yhi, ylo), (1 - yhi, 1 - ylo)]
-    z_ring = [device(v, ylo, x, yhi, core) for v in z_at]
-    x_ring = [device(z, ylo, v, yhi, core) for v in x_at]
-    y_ring = [device(z, v, x, h, core) for h, v in y_at]
-    mine, pairs = [], []
-    for s in range(3):
-        pairs.append(pltpu.make_async_copy(near_ref.at[s], near.at[s], near_sem.at[s]))
-        mine.append(pltpu.make_async_copy(grads_ref.at[s], own.at[s], own_sem.at[s]))
-        pairs[-1].start()
-        mine[-1].start()
-    greet(z_ring + x_ring + y_ring)
-
-    first = []
-    for s in range(3):
-        mine[s].wait()
-        pairs[s].wait()
-        for i in range(4):
-            total(own.at[s, i], own[s, i], [near[s, i]])
-        for d in range(3):
-            if s == 0:
-                src = own.at[s, :, window(96 * z_at[d], 112)]
-                copy = send(src, a0.at[d], sems, 3 + s * 3 + d, z_ring[d])
-            elif s == 1:
-                h, v = y_at[d]
-                src = own.at[s, pl.ds(2 * h, 2), window(192 * v, 208)]
-                copy = send(src, a1.at[d], sems, 3 + s * 3 + d, y_ring[d])
-            else:
-                src = own.at[s, :, window(96 * x_at[d], 112)]
-                copy = send(src, a2.at[d], sems, 3 + s * 3 + d, x_ring[d])
-            first.append(copy)
-
-    second = []
-    for s in range(3):
-        for d in range(3):
-            first[s * 3 + d].wait()
-        if s == 0:
-            total(m0, own[s, :, window(96 * z, 112)], [a0[d] for d in range(3)])
-        elif s == 1:
-            total(m1, own[s, pl.ds(2 * yhi, 2), window(192 * ylo, 208)], [a1[d] for d in range(3)])
-        else:
-            total(m2, own[s, :, window(96 * x, 112)], [a2[d] for d in range(3)])
-        for d in range(3):
-            if s == 0:
-                h, v = y_at[d]
-                copy = send(m0.at[pl.ds(2 * h, 2), window(48 * v, 64)], b0.at[d], sems, 12 + s * 3 + d, y_ring[d])
-            elif s == 1:
-                copy = send(m1.at[:, window(48 * x_at[d], 64)], b1.at[d], sems, 12 + s * 3 + d, x_ring[d])
-            else:
-                v = z_at[d]
-                copy = send(m2.at[:, window(16 * v + 16 * (v // 2), 48)], b2.at[d], sems, 12 + s * 3 + d, z_ring[d])
-            second.append(copy)
-
-    third = []
-    for s in range(3):
-        for d in range(3):
-            second[s * 3 + d].wait()
-        if s == 0:
-            total(n0, m0[pl.ds(2 * yhi, 2), window(48 * ylo, 64)], [b0[d] for d in range(3)])
-        elif s == 1:
-            total(n1, m1[:, window(48 * x, 64)], [b1[d] for d in range(3)])
-        else:
-            total(n2, m2[:, window(16 * z + 16 * (z // 2), 48)], [b2[d] for d in range(3)])
-        for d in range(3):
-            if s == 0:
-                _, at = last_window(0, z * 8 + ylo * 4 + x_at[d])
-                copy = send(n0.at[:, window(at, 32)], c0.at[d], sems, 21 + s * 3 + d, x_ring[d])
-            elif s == 1:
-                _, at = last_window(1, ylo * 16 + x * 4 + z_at[d])
-                copy = send(n1.at[:, window(at, 32)], c1.at[d], sems, 21 + s * 3 + d, z_ring[d])
-            else:
-                h, v = y_at[d]
-                _, at = last_window(2, x * 8 + z * 2 + v)
-                copy = send(n2.at[pl.ds(2 * h, 2), window(at, 32)], c2.at[d], sems, 21 + s * 3 + d, y_ring[d])
-            third.append(copy)
-
-    for s in range(3):
-        for d in range(3):
-            third[s * 3 + d].wait()
-        if s == 0:
-            _, at = last_window(0, z * 8 + ylo * 4 + x)
-            total(out_ref.at[s], n0[:, window(at, 32)], [c0[d] for d in range(3)])
-        elif s == 1:
-            _, at = last_window(1, ylo * 16 + x * 4 + z)
-            total(out_ref.at[s], n1[:, window(at, 32)], [c1[d] for d in range(3)])
-        else:
-            _, at = last_window(2, x * 8 + z * 2 + ylo)
-            total(out_ref.at[s], n2[pl.ds(2 * yhi, 2), window(at, 32)], [c2[d] for d in range(3)])
-
-
-def reduce_call(grads, near):
-    _, four, rows, lanes = grads.shape
-    buf = lambda *shape: pltpu.VMEM(shape + (lanes,), jnp.bfloat16)
-    return pl.pallas_call(
-        reduce_kernel,
-        in_specs=[pl.BlockSpec(memory_space=pl.ANY)] * 2,
-        out_specs=pl.BlockSpec(memory_space=pltpu.VMEM),
-        out_shape=jax.ShapeDtypeStruct((3, 2, 32, lanes), jnp.float32),
-        scratch_shapes=[
-            buf(3, four, rows), buf(3, four, rows),
-            buf(3, 4, 112), buf(3, 2, 64), buf(3, 2, 32),
-            buf(3, 2, 208), buf(3, 2, 64), buf(3, 2, 32),
-            buf(3, 4, 112), buf(3, 4, 48), buf(3, 2, 32),
-            buf(4, 112), buf(2, 64), buf(2, 208), buf(2, 64), buf(4, 112), buf(4, 48),
-            pltpu.SemaphoreType.DMA((3,)), pltpu.SemaphoreType.DMA((3,)), pltpu.SemaphoreType.DMA((30,)), pltpu.SemaphoreType.DMA((30,)),
-        ],
-        compiler_params=pltpu.CompilerParams(
-            collective_id=1, has_side_effects=True, vmem_limit_bytes=VMEM_LIMIT
-        ),
-        name="reduce_operator_gradients",
-    )(grads, near)
 
 
 def final_share(pieces, width):
@@ -528,10 +491,10 @@
     src = sources[0][:, None]
     tgt = targets[0][:, None]
     neg = negatives[0].reshape(BUCKETS, 1, -1)
-    L, LS, R, RS, partial, near = train_call(
+    L, LS, R, RS, pieces = train_call(
         info, operators, left.T, left_state[None], right.T, right_state[None], src, tgt, neg, nrel, block_slot.shape[-1]
     )
-    op_grad = final_share(reduce_call(partial, near), width)
+    op_grad = final_share(pieces, width)
     return (L.T, LS[0], R.T.astype(jnp.float32), RS[0], op_grad)
 
 

time: 169 us -> 161 us (0.953)
  waiting for transfers between devices: 10.5 us -> 5.21 us
  Pallas kernels: 139 us -> 134 us
    pallas_call x1 -> x0, Pallas kernels: 43.4 us -> none  [reduce_call(): pl.pallas_call(reduce_kernel, in_specs=[pl.BlockSpec(memory_space=pl.ANY)...]
    pallas_call x1, Pallas kernels: 95.7 us -> 134 us  [train_call(): pl.pallas_call(train_kernel, in_specs=[pl.BlockSpec(memory_space=pltpu.SM...]
    ppermute x2, waiting for transfers between devices: 10.5 us -> 5.21 us  [final_share(): piece = lax.ppermute(piece, 'blk', [(b, at(b)) for b in range(blk)])]
  transfers between devices with their start and end apart: 2 -> 2, of which waited for: 2 -> 1; matrix products, arithmetic and copies ran while one was open for 1% -> 1% of each run, Pallas kernels for 0% -> 0%
where the time goes in v5:
time: 161 us; the launch traced here: 159 us
  Pallas kernels  134 us (83%)
  starting transfers between devices  8.25 us (5%)
  local copies, waits for them, and re-layouts  7.3 us (5%)
  waiting for transfers between devices  5.21 us (3%)
  other arithmetic  3.57 us (2%)
    pallas_call x1, Pallas kernels, train_call(): pl.pallas_call(train_kernel, in_specs=[pl.BlockSpec(memory_space=pltpu.SM...  134 us
    ppermute x2, starting transfers between devices, final_share(): piece = lax.ppermute(piece, 'blk', [(b, at(b)) for b in range(blk)])  8.25 us
    ppermute x2, waiting for transfers between devices, final_share(): piece = lax.ppermute(piece, 'blk', [(b, at(b)) for b in range(blk)])  5.21 us
  transfers between devices with their start and end apart: 2, of which 1 were waited for; matrix products, arithmetic and copies ran while one was open for 1% of the time, Pallas kernels for 0%

profile of v5, /device:TPU:8, one launch (start us, length us, event | category | flops | bytes accessed | tf_op | source)
XLA Modules:
  0.0 159.4 jit_solution(13017620559144852849)
XLA Ops:
  0.6 0.8 reshape_squeeze.12
  1.4 0.7 reduce
  2.1 0.1 reshape_squeeze.13
  2.2 0.7 gather_fusion
  2.9 0.2 select_reduce_fusion.1
  3.1 1.4 reshape_squeeze.14.neg_ref
  4.5 0.6 pad_add_fusion.info_ref
  5.1 134.3 %train_buckets.1 = (f32[400,1024]{1,0:T(8,128)}, f32[1,1024]{1,0:T(1,128)}, bf16[400,1024]{1,0:T(8,128)(2,1)}, f32[1,1024]{1,0:T(1,128)}, f32[3,2,32,512]{3,2,1,0:T(8,128)}) custom-call(s32[72]{0:T(128)} %pad_add_fusion.info_ref, bf16[6,400,400]{2,1,0:T(8,128)(2,1)} %own_ref.1, f32[400,1024]{1,0:T(8,128)} %bitcast.21, f32[1,1024]{1,0:T(1,128)} %bitcast.26, ...), custom_call_target="tpu_custom_call" | custom-call | tf_op jit(solution)/shard_map/train_buckets/pallas_call | solution.py:417
  139.3 0.0 copy-start.1
  139.3 1.1 fusion.2
  140.5 2.3 %collective-permute-start.1 = (f32[2,32,400]{2,1,0:T(8,128)S(1)}, f32[2,32,400]{2,1,0:T(8,128)S(1)}, u32[]{:S(2)}, u32[]{:S(2)}) collective-permute-start(f32[2,32,400]{2,1,0:T(8,128)S(1)} %get-tuple-element.18), channel_id=1, source_target_pairs={{0,0},{4,32},{8,64},{12,96},{16,4},{20,36},{24,68},{28,100},{32,8}... | collective-permute-start | bytes 307208 | tf_op jit(solution)/shard_map/ppermute | solution.py:471
  142.8 6.0 %collective-permute-start = (f32[2,32,400]{2,1,0:T(8,128)S(1)}, f32[2,32,400]{2,1,0:T(8,128)S(1)}, u32[]{:S(2)}, u32[]{:S(2)}) collective-permute-start(f32[2,32,400]{2,1,0:T(8,128)S(1)} %get-tuple-element.19), channel_id=1, source_target_pairs={{0,0},{4,16},{8,32},{12,48},{16,64},{20,80},{24,96},{28,112},{32,4... | collective-permute-start | bytes 307208 | tf_op jit(solution)/shard_map/ppermute | solution.py:471
  148.8 0.2 reshape_squeeze.15
  149.0 0.1 constant_dynamic-slice_fusion.2
  149.2 0.0 copy-done.1
  149.2 0.0 copy-start
  149.2 1.3 convert_bitcast_fusion
  150.5 5.2 %collective-permute-done.1 = f32[2,32,400]{2,1,0:T(8,128)S(1)} collective-permute-done((f32[2,32,400]{2,1,0:T(8,128)S(1)}, f32[2,32,400]{2,1,0:T(8,128)S(1)}, u32[]{:S(2)}, u32[]{:S(2)}) %collective-permute-start.1) | collective-permute-done | bytes 102432 | tf_op jit(solution)/shard_map/ppermute | solution.py:471
  155.7 0.2 reshape.47
  155.9 0.1 constant_dynamic-slice_fusion
  156.0 0.0 collective-permute-done
  156.0 0.2 reshape.46
  156.2 0.1 constant_dynamic-slice_fusion.1
  156.4 0.7 pad_maximum_fusion
  157.1 0.0 copy-done
  157.1 0.0 copy-start.3
  157.1 0.0 copy-start.2
  157.1 1.2 copy.18
  158.2 0.0 copy-done.3
  158.3 0.6 copy.19
  158.8 0.0 copy-done.2
  158.8 0.6 copy.20
  (3 shorter events, 0.0 us)
Async XLA Ops:
  139.3 9.8 %copy-start.1 = (bf16[400,1024]{1,0:T(8,128)(2,1)S(1)}, bf16[400,1024]{1,0:T(8,128)(2,1)}, u32[]{:S(2)}) copy-start(bf16[400,1024]{1,0:T(8,128)(2,1)} %get-tuple-element.12) | copy-start | bytes 2457604
  140.5 15.3 %collective-permute-start.1 = (f32[2,32,400]{2,1,0:T(8,128)S(1)}, f32[2,32,400]{2,1,0:T(8,128)S(1)}, u32[]{:S(2)}, u32[]{:S(2)}) collective-permute-start(f32[2,32,400]{2,1,0:T(8,128)S(1)} %get-tuple-element.18), channel_id=1, source_target_pairs={{0,0},{4,32},{8,64},{12,96},{16,4},{20,36},{24,68},{28,100},{32,8}... | collective-permute-start | bytes 307208 | tf_op jit(solution)/shard_map/ppermute | solution.py:471
  142.8 13.3 %collective-permute-start = (f32[2,32,400]{2,1,0:T(8,128)S(1)}, f32[2,32,400]{2,1,0:T(8,128)S(1)}, u32[]{:S(2)}, u32[]{:S(2)}) collective-permute-start(f32[2,32,400]{2,1,0:T(8,128)S(1)} %get-tuple-element.19), channel_id=1, source_target_pairs={{0,0},{4,16},{8,32},{12,48},{16,64},{20,80},{24,96},{28,112},{32,4... | collective-permute-start | bytes 307208 | tf_op jit(solution)/shard_map/ppermute | solution.py:471
  149.2 7.9 %copy-start = (f32[400,1024]{1,0:T(8,128)S(1)}, f32[400,1024]{1,0:T(8,128)}, u32[]{:S(2)}) copy-start(f32[400,1024]{1,0:T(8,128)} %get-tuple-element.10) | copy-start | bytes 4915204
  157.1 1.2 copy-start.3
  157.1 1.8 %copy-start.2 = (f32[1,1024]{1,0:T(1,128)S(1)}, f32[1,1024]{1,0:T(1,128)}, u32[]{:S(2)}) copy-start(f32[1,1024]{1,0:T(1,128)} %get-tuple-element.13) | copy-start | bytes 12292

commit v6 on v5

--- a/solution.py
+++ b/solution.py
@@ -39,11 +39,25 @@
     return (z * 8 + ylo * 4 + x, yhi * 2 + core)
 
 
-def greet(peers):
+def greet(peers, swaps):
     barrier = pltpu.get_barrier_semaphore()
+
+    def tell(peer):
+        pl.semaphore_signal(barrier, inc=1, device_id=peer, device_id_type=MESH)
+
     for peer in peers:
-        pl.semaphore_signal(barrier, inc=1, device_id=peer, device_id_type=MESH)
-    pl.semaphore_wait(barrier, len(peers))
+        tell(peer)
+    for apart, both in swaps:
+        @pl.when(apart)
+        def _():
+            for peer in both:
+                tell(peer)
+
+    apart = sum(jnp.where(apart, 1, 0) for apart, _ in swaps)
+    for n in range(len(swaps) + 1):
+        @pl.when(apart == n)
+        def _():
+            pl.semaphore_wait(barrier, len(peers) + 2 * n)
 
 
 def remote(src, dst, sems, index, peer):
@@ -97,11 +111,11 @@
 
 
 def train_kernel(
-    info_ref, own_ref, left_ref, lacc_ref, right_ref, racc_ref, src_ref, tgt_ref, neg_ref,
-    newleft_ref, newlacc_ref, newright_ref, newracc_ref, out_ref,
+    need_ref, slot_ref, own_ref, left_ref, lacc_ref, right_ref, racc_ref, src_ref, tgt_ref, neg_ref,
+    newleft_ref, newlacc_ref, newright_ref, newracc_ref, out_ref, home_ref,
     table, fresh_ref, freshacc_ref, half, rhalf, rhalf_t, hot, query, scaled, heads_now, push, scale, score, count, sums, rows_now, acc_now,
-    in_rows, in_acc, near, a0, b0, c0, a1, b1, c1, a2, b2, c2, load_sem,
-    cross_s, cross_r, ring_s, ring_r, whole_s, whole_r, pass_s, pass_r, move_s, move_r, acc_s, acc_r, near_s, near_r, sum_s, sum_r,
+    in_rows, in_acc, near, a0, b0, c0, a1, b1, c1, a2, b2, c2, piece, before_ref, last_ref, load_sem,
+    cross_s, cross_r, ring_s, ring_r, whole_s, whole_r, pass_s, pass_r, move_s, move_r, acc_s, acc_r, near_s, near_r, sum_s, sum_r, home_s, home_r,
 ):
     z, ylo, x, yhi, core = place()
     me = yhi * 2 + core
@@ -111,7 +125,7 @@
     units = owned * UNITS
     third = units // 8
     edges = src_ref.shape[2]
-    nblk = (info_ref.shape[0] - table.shape[0]) // 2 // BUCKETS
+    nblk = slot_ref.shape[0] // BUCKETS
     block = edges // nblk
     half_rows = rows // 2
     nrel = table.shape[0]
@@ -133,7 +147,10 @@
     z_at = [(z + d) % 4 for d in (1, 2, 3)]
     y_at = [(yhi, 1 - ylo), (1 - yhi, ylo), (1 - yhi, 1 - ylo)]
     y_ring = [device(z, v, x, h, core) for h, v in y_at]
-    greet([sibling, ahead, behind] + x_ring + y_ring + z_ring)
+    targets = (ylo * 16 + x * 4 + z, x * 8 + z * 2 + ylo)
+    origins = ((b % 4) * 8 + (b // 16) * 4 + (b // 4) % 4, (b // 2) % 4 * 8 + (b % 2) * 4 + b // 8)
+    swaps = [(to != b, ((to, r), (origin, r))) for to, origin in zip(targets, origins)]
+    greet([sibling, ahead, behind] + x_ring + y_ring + z_ring, swaps)
 
     for j in range(owned):
         table[me * owned + j] = jnp.pad(own_ref[j], ((0, 0), (0, LANES - width)))
@@ -162,8 +179,22 @@
         for c in range(0, edges, CHUNK):
             of = (lax.broadcasted_iota(jnp.int32, (CHUNK, 128), 0) + c) // block
             share = jnp.where(of == lax.broadcasted_iota(jnp.int32, (CHUNK, 128), 1), 1.0 / block, 0.0)
-            found += dot(onehot(neg_ref[t, :, c : c + CHUNK], rows), share.astype(jnp.bfloat16))
+            names = [neg_ref[t, k : k + 1, :] for k in range(c // block, (c + CHUNK) // block)]
+            found += dot(onehot(jnp.concatenate(names, axis=1), rows), share.astype(jnp.bfloat16))
         count[t] = found
+
+    def chains():
+        ids = [need_ref[slot_ref[n]] for n in range(total_blocks)]
+        for n in range(total_blocks):
+            found = jnp.int32(total_blocks)
+            for m in range(n):
+                found = jnp.where(ids[m] == ids[n], m, found)
+            before_ref[n] = found
+        for j in range(nrel):
+            found = jnp.int32(total_blocks)
+            for n in range(total_blocks):
+                found = jnp.where(ids[n] == j, n, found)
+            last_ref[j] = found
 
     def clear(n, carry):
         sums[n] = jnp.zeros(sums.shape[1:], sums.dtype)
@@ -188,6 +219,7 @@
             copies.append(send(part, part, (pass_s, pass_r), ring * 4 * third + i, sibling))
         counts(i)
         if i == 1:
+            chains()
             lax.fori_loop(0, sums.shape[0], clear, 0)
     for i in range(third):
         for ring in range(2):
@@ -200,7 +232,7 @@
         copy.wait()
 
     def operator(t, k):
-        return table[info_ref[t * nblk + k]][:, :width]
+        return table[need_ref[slot_ref[t * nblk + k]]][:, :width]
 
     def earlier(n):
         return jnp.where(n < total_blocks, sums[jnp.minimum(n, total_blocks - 1)].astype(jnp.float32), 0.0)
@@ -216,6 +248,21 @@
         for k in range(nblk):
             cols = slice(k * block, (k + 1) * block)
             query[:, cols] = dot(operator(t, k), heads_now[:, cols], TN).astype(jnp.bfloat16)
+
+    quarter = nrel // 6
+    half_count = nrel // 2
+
+    def relation(n, of_core):
+        part, h, i = n // quarter, n // 2 % 2, n % 2
+        return earlier(last_ref[(h * 2 + of_core) * owned + part * 2 + i])
+
+    def staged(n):
+        if n < 8:
+            return push.at[pl.ds(n // 4 * width, width), pl.ds(n % 4 * LANES, LANES)]
+        return in_rows.at[(n - 8) // 2, :, pl.ds(n % 2 * LANES, LANES)]
+
+    def pair(n):
+        return remote(staged(n), near.at[n], (near_s, near_r), n, sibling)
 
     def start(copies):
         for copy in copies:
@@ -286,6 +333,17 @@
             ).astype(jnp.bfloat16)
         for k in range(nblk):
             cols = slice(k * block, (k + 1) * block)
+            before = earlier(before_ref[t * nblk + k])
+            sums[t * nblk + k] = (before + dot(heads_now[:, cols], scaled[:, cols], NT)).astype(sums.dtype)
+
+        @pl.when(t == BUCKETS - 1)
+        def _():
+            for n in range(half_count):
+                staged(n)[:, :width] = relation(n, 1 - core).astype(jnp.bfloat16)
+                pair(n).start()
+
+        for k in range(nblk):
+            cols = slice(k * block, (k + 1) * block)
             query[:, cols] = dot(operator(t, k), scaled[:, cols]).astype(jnp.bfloat16)
         for c in range(0, rows, CHUNK):
             part = slice(c, c + CHUNK)
@@ -293,11 +351,6 @@
             newleft_ref[:, part] = left
             newlacc_ref[:, part] = acc
             half[:, part] = left.astype(jnp.bfloat16)
-        for k in range(nblk):
-            cols = slice(k * block, (k + 1) * block)
-            before = earlier(info_ref[total_blocks + t * nblk + k])
-            sums[t * nblk + k] = (before + dot(heads_now[:, cols], scaled[:, cols], NT)).astype(sums.dtype)
-
         @pl.when(t < BUCKETS - 1)
         def _():
             heads(t + 1)
@@ -308,25 +361,13 @@
     queries(0)
     lax.fori_loop(0, BUCKETS, bucket, 0)
 
-    quarter = nrel // 6
-    half_count = nrel // 2
-
-    def relation(n, of_core):
-        part, h, i = n // quarter, n // 2 % 2, n % 2
-        return earlier(info_ref[2 * total_blocks + (h * 2 + of_core) * owned + part * 2 + i])
-
-    pairs = []
-    for n in range(half_count):
-        table[half_count + n, :, :width] = relation(n, 1 - core).astype(jnp.bfloat16)
-        pairs.append(send(table.at[half_count + n], near.at[n], (near_s, near_r), n, sibling))
-
     sems = (sum_s, sum_r)
-    own = [table.at[pl.ds(s * quarter, quarter)] for s in range(3)]
+    own = [near.at[pl.ds(s * quarter, quarter)] for s in range(3)]
     first = []
     for s in range(3):
         for n in range(s * quarter, (s + 1) * quarter):
-            pairs[n].wait()
-            table[n, :, :width] = (relation(n, core) + near[n, :, :width].astype(jnp.float32)).astype(jnp.bfloat16)
+            pair(n).wait()
+            near[n, :, :width] = (relation(n, core) + near[n, :, :width].astype(jnp.float32)).astype(jnp.bfloat16)
         for d in range(3):
             if s == 0:
                 copy = send(own[s].at[:, window(96 * z_at[d], 112)], a0.at[d], sems, s * 3 + d, z_ring[d])
@@ -359,6 +400,9 @@
                 src = a2.at[0, :, window(16 * v + 16 * (v // 2), 48)]
                 copy = send(src, b2.at[d], sems, 9 + s * 3 + d, z_ring[d])
             second.append(copy)
+
+    def homeward(s):
+        return remote(piece.at[s - 1], home_ref.at[s - 1], (home_s, home_r), s - 1, (targets[s - 1], r))
 
     third = []
     for s in range(3):
@@ -389,20 +433,35 @@
             third[s * 3 + d].wait()
         if s == 0:
             _, at = last_window(0, z * 8 + ylo * 4 + x)
-            total(out_ref.at[s], b0[0, :, window(at, 32)], [c0[d] for d in range(3)])
+            total(out_ref, b0[0, :, window(at, 32)], [c0[d] for d in range(3)])
         elif s == 1:
             _, at = last_window(1, ylo * 16 + x * 4 + z)
-            total(out_ref.at[s], b1[0, :, window(at, 32)], [c1[d] for d in range(3)])
+            total(piece.at[0], b1[0, :, window(at, 32)], [c1[d] for d in range(3)])
         else:
             _, at = last_window(2, x * 8 + z * 2 + ylo)
-            total(out_ref.at[s], b2[0, pl.ds(2 * yhi, 2), window(at, 32)], [c2[d] for d in range(3)])
+            total(piece.at[1], b2[0, pl.ds(2 * yhi, 2), window(at, 32)], [c2[d] for d in range(3)])
+        if s > 0:
+
+            @pl.when(targets[s - 1] != b)
+            def _():
+                homeward(s).start()
+
+            @pl.when(targets[s - 1] == b)
+            def _():
+                home_ref[s - 1] = piece[s - 1]
+
+    for s in (1, 2):
+
+        @pl.when(targets[s - 1] != b)
+        def _():
+            homeward(s).wait()
 
     for c in range(2):
         for move in moves(BUCKETS - 1, c, newright_ref, newracc_ref):
             move.wait()
 
 
-def train_call(info, own, left, lacc, right, racc, src, tgt, neg, nrel, nblk):
+def train_call(need, slot, own, left, lacc, right, racc, src, tgt, neg, nrel, nblk):
     width, rows = left.shape
     owned = own.shape[0]
     units = owned * UNITS
@@ -416,14 +475,15 @@
     buf = lambda *shape: pltpu.VMEM(shape + (LANES,), bf16)
     return pl.pallas_call(
         train_kernel,
-        in_specs=[pl.BlockSpec(memory_space=pltpu.SMEM), vmem, anywhere, vmem, anywhere] + [vmem] * 4,
-        out_specs=[vmem] * 2 + [anywhere] * 2 + [vmem],
+        in_specs=[pl.BlockSpec(memory_space=pltpu.SMEM)] * 2 + [vmem, anywhere, vmem, anywhere] + [vmem] * 4,
+        out_specs=[vmem] * 2 + [anywhere] * 2 + [vmem] * 2,
         out_shape=[
             jax.ShapeDtypeStruct((width, rows), f32),
             jax.ShapeDtypeStruct((1, rows), f32),
             jax.ShapeDtypeStruct((width, rows), bf16),
             jax.ShapeDtypeStruct((1, rows), f32),
-            jax.ShapeDtypeStruct((3, 2, 32, LANES), f32),
+            jax.ShapeDtypeStruct((2, 32, LANES), f32),
+            jax.ShapeDtypeStruct((2, 2, 32, LANES), bf16),
         ],
         scratch_shapes=[
             pltpu.VMEM((nrel, width, LANES), bf16),
@@ -449,52 +509,41 @@
             buf(3, four, 112), buf(3, 2, 64), buf(3, 2, 32),
             buf(3, 2, 208), buf(3, 2, 64), buf(3, 2, 32),
             buf(3, four, 112), buf(3, four, 48), buf(3, 2, 32),
+            buf(2, 2, 32),
+            pltpu.SMEM((buckets * nblk,), jnp.int32),
+            pltpu.SMEM((nrel,), jnp.int32),
             pltpu.SemaphoreType.DMA((2,)),
         ]
-        + dma(2 * third) + dma(6 * third) + dma(1) + dma(8 * third) + dma(2 * buckets) + dma(2 * buckets) + dma(nrel // 2) + dma(27),
+        + dma(2 * third) + dma(6 * third) + dma(1) + dma(8 * third) + dma(2 * buckets) + dma(2 * buckets) + dma(nrel // 2) + dma(27) + dma(2),
         compiler_params=pltpu.CompilerParams(
             collective_id=0, has_side_effects=True, vmem_limit_bytes=VMEM_LIMIT
         ),
         name="train_buckets",
-    )(info, own, left, lacc, right, racc, src, tgt, neg)
+    )(need, slot, own, left, lacc, right, racc, src, tgt, neg)
 
 
 def final_share(pieces, width):
-    blk = lax.axis_size("blk")
-    place_1 = lambda b: ((b // 4) % 2) * 16 + (b % 4) * 4 + b // 8
-    place_2 = lambda b: (b % 4) * 8 + (b // 8) * 2 + (b // 4) % 2
     t = lax.axis_index("blk")
-    shares = []
-    for s, at in enumerate((None, place_1, place_2)):
-        piece = pieces[s, :, :, :width]
-        if at is not None:
-            piece = lax.ppermute(piece, "blk", [(b, at(b)) for b in range(blk)])
+    share = width * width // lax.axis_size("blk")
+    rows = []
+    for s in range(3):
         start, _ = last_window(s, t)
-        skip = t * (width * width // blk) - start * width
-        flat = piece.reshape(2, 32 * width)
-        shares.append(lax.dynamic_slice(flat, (0, skip), (2, width * width // blk)))
-    return jnp.concatenate(shares, axis=0)
+        flat = pieces[s][:, :, :width].astype(jnp.float32).reshape(2, 32 * width)
+        rows.append(lax.dynamic_slice(flat, (0, t * share - start * width), (2, share)))
+    return jnp.concatenate(rows, axis=0)
 
 
 def body(left, left_state, right, right_state, operators, need_list, block_slot, sources, targets, negatives):
     owned_count, width, _ = operators.shape
     owners = lax.axis_size("rel")
     nrel = owned_count * owners
-    rel = need_list[0].reshape(-1)[block_slot[0].reshape(-1)]
-    blocks = rel.shape[0]
-    at = jnp.arange(blocks, dtype=jnp.int32)
-    latest = lambda found: jnp.max(jnp.where(found, at, -1), axis=1)
-    before = latest((rel[:, None] == rel[None, :]) & (at[None, :] < at[:, None]))
-    last = latest(rel[None, :] == jnp.arange(nrel, dtype=jnp.int32)[:, None])
-    before, last = (jnp.where(found < 0, blocks, found) for found in (before, last))
-    info = jnp.concatenate([rel, before, last])
     src = sources[0][:, None]
     tgt = targets[0][:, None]
-    neg = negatives[0].reshape(BUCKETS, 1, -1)
-    L, LS, R, RS, pieces = train_call(
-        info, operators, left.T, left_state[None], right.T, right_state[None], src, tgt, neg, nrel, block_slot.shape[-1]
+    neg = negatives[0]
+    L, LS, R, RS, here, home = train_call(
+        need_list.reshape(-1), block_slot.reshape(-1), operators, left.T, left_state[None], right.T, right_state[None], src, tgt, neg, nrel, block_slot.shape[-1]
     )
-    op_grad = final_share(pieces, width)
+    op_grad = final_share((here, home[0], home[1]), width)
     return (L.T, LS[0], R.T.astype(jnp.float32), RS[0], op_grad)
 
 

time: 161 us -> 151 us (0.938); the launches traced: 159 us -> 151 us
  starting transfers between devices: 8.25 us -> 0 us
  Pallas kernels: 134 us -> 141 us
  waiting for transfers between devices: 5.21 us -> 0 us
  local copies, waits for them, and re-layouts: 7.3 us -> 5.13 us
    ppermute x2 -> x0, starting transfers between devices: 8.25 us -> none  [final_share(): piece = lax.ppermute(piece, 'blk', [(b, at(b)) for b in range(blk)])]
    pallas_call x1, Pallas kernels: 134 us -> 141 us  [train_call(): pl.pallas_call(train_kernel, in_specs=[pl.BlockSpec(memory_space=pltpu.SM...]
    ppermute x2 -> x0, waiting for transfers between devices: 5.21 us -> none  [final_share(): piece = lax.ppermute(piece, 'blk', [(b, at(b)) for b in range(blk)])]
    another operation x4 -> x0, local copies, waits for them, and re-layouts: 2.41 us -> none  [the longest x1 1.37 us: body(): neg = negatives[0].reshape(BUCKETS, 1, -1)]
    reshape x2 -> x5, local copies, waits for them, and re-layouts: 0.37 us -> 2.42 us  [the longest x1 1.27 us: body(): need_list.reshape(-1)]
  transfers between devices with their start and end apart: 2 -> 0, of which waited for: 1 -> 0; matrix products, arithmetic and copies ran while one was open for 1% -> 0% of each run, Pallas kernels for 0% -> 0%
where the time goes in v6:
time: 151 us
  Pallas kernels  141 us (93%)
  local copies, waits for them, and re-layouts  5.13 us (3%)
  other arithmetic  3.98 us (3%)
    pallas_call x1, Pallas kernels, train_call(): pl.pallas_call(train_kernel, in_specs=[pl.BlockSpec(memory_space=pltpu.SM...  141 us

profile of v6, /device:TPU:8, one launch (start us, length us, event | category | flops | bytes accessed | tf_op | source)
XLA Modules:
  0.0 151.3 jit_solution(3052610412360017410)
XLA Ops:
  0.6 1.3 reshape.31.need_ref
  1.9 0.7 reduce
  2.6 0.6 reshape.32.slot_ref
  3.2 141.2 %train_buckets.1 = (f32[400,1024]{1,0:T(8,128)}, f32[1,1024]{1,0:T(1,128)}, bf16[400,1024]{1,0:T(8,128)(2,1)}, f32[1,1024]{1,0:T(1,128)}, f32[2,32,512]{2,1,0:T(8,128)}, /*index=5*/bf16[2,2,32,512]{3,2,1,0:T(8,128)(2,1)}) custom-call(s32[16]{0:T(128)} %reshape.31.need_ref, s32[24]{0:T(128)} %reshape.32.slot_ref, bf16[6,400,400]{2,1,0:T(8,128)(2,1)} %own_ref.1, ...), custom_call_target="tpu_custom_call" | custom-call | tf_op jit(solution)/shard_map/train_buckets/pallas_call | solution.py:476
  144.4 0.0 copy-start.2
  144.4 0.0 copy-start.1
  144.4 2.5 %convert_bitcast_fusion = f32[1024,400]{0,1:T(8,128)} fusion(bf16[400,1024]{1,0:T(8,128)(2,1)} %get-tuple-element.13), kind=kLoop, calls=%fused_computation | loop fusion | flops 409600 | bytes 2457600 | tf_op jit(solution)/shard_map/convert_element_type | solution.py:547
  146.9 0.0 copy-start
  146.9 0.0 copy-done.2
  147.0 0.2 reshape.41
  147.3 0.1 constant_dynamic-slice_fusion
  147.4 0.2 reshape.39
  147.7 0.1 constant_dynamic-slice_fusion.1
  147.8 0.0 copy-done.1
  147.8 0.2 reshape.33
  148.1 0.1 constant_dynamic-slice_fusion.2
  148.2 0.7 pad_maximum_fusion
  148.9 0.0 copy-done
  148.9 0.0 copy-start.4
  148.9 0.0 copy-start.3
  148.9 1.2 copy.18
  150.1 0.0 copy-done.4
  150.1 0.6 copy.19
  150.7 0.0 copy-done.3
  150.7 0.6 copy.20
  (2 shorter events, 0.0 us)
Async XLA Ops:
  144.4 2.6 %copy-start.2 = (bf16[2,2,32,512]{3,2,1,0:T(8,128)(2,1)S(1)}, bf16[2,2,32,512]{3,2,1,0:T(8,128)(2,1)}, u32[]{:S(2)}) copy-start(bf16[2,2,32,512]{3,2,1,0:T(8,128)(2,1)} %get-tuple-element.16) | copy-start | bytes 393220
  144.4 3.4 %copy-start.1 = (f32[2,32,512]{2,1,0:T(8,128)S(1)}, f32[2,32,512]{2,1,0:T(8,128)}, u32[]{:S(2)}) copy-start(f32[2,32,512]{2,1,0:T(8,128)} %get-tuple-element.15) | copy-start | bytes 393220
  146.9 2.0 %copy-start = (f32[400,1024]{1,0:T(8,128)S(1)}, f32[400,1024]{1,0:T(8,128)}, u32[]{:S(2)}) copy-start(f32[400,1024]{1,0:T(8,128)} %get-tuple-element.11) | copy-start | bytes 4915204
  148.9 1.2 copy-start.4
  148.9 1.8 %copy-start.3 = (f32[1,1024]{1,0:T(1,128)S(1)}, f32[1,1024]{1,0:T(1,128)}, u32[]{:S(2)}) copy-start(f32[1,1024]{1,0:T(1,128)} %get-tuple-element.14) | copy-start | bytes 12292

commit v7 on v6

--- a/solution.py
+++ b/solution.py
@@ -208,6 +208,15 @@
     heads(0)
     rings = (x_ring, z_ring)
     landed = {}
+
+    def pass_arrivals(i):
+        for ring in range(2):
+            for d in (1, 3, 2):
+                landed[ring, d, i].wait()
+                origin = ((x, z)[ring] - d + 4) % 4
+                part = unit(far, ring * (units // 2) + origin * third + i)
+                copies.append(send(part, part, (pass_s, pass_r), (ring * 4 + d) * third + i, sibling))
+
     for i in range(third):
         for ring in range(2):
             arrivals[ring, i].wait()
@@ -217,17 +226,13 @@
                     part, part, (ring_s, ring_r), (ring * 3 + d - 1) * third + i, rings[ring][d - 1]
                 )
             copies.append(send(part, part, (pass_s, pass_r), ring * 4 * third + i, sibling))
+        if i > 0:
+            pass_arrivals(i - 1)
         counts(i)
         if i == 1:
             chains()
             lax.fori_loop(0, sums.shape[0], clear, 0)
-    for i in range(third):
-        for ring in range(2):
-            for d in (1, 3, 2):
-                landed[ring, d, i].wait()
-                origin = ((x, z)[ring] - d + 4) % 4
-                part = unit(far, ring * (units // 2) + origin * third + i)
-                copies.append(send(part, part, (pass_s, pass_r), (ring * 4 + d) * third + i, sibling))
+    pass_arrivals(third - 1)
     for copy in copies:
         copy.wait()
 
@@ -338,7 +343,7 @@
 
         @pl.when(t == BUCKETS - 1)
         def _():
-            for n in range(half_count):
+            for n in [(m + quarter) % half_count for m in range(half_count)]:
                 staged(n)[:, :width] = relation(n, 1 - core).astype(jnp.bfloat16)
                 pair(n).start()
 
@@ -363,8 +368,8 @@
 
     sems = (sum_s, sum_r)
     own = [near.at[pl.ds(s * quarter, quarter)] for s in range(3)]
-    first = []
-    for s in range(3):
+    first = {}
+    for s in (1, 2, 0):
         for n in range(s * quarter, (s + 1) * quarter):
             pair(n).wait()
             near[n, :, :width] = (relation(n, core) + near[n, :, :width].astype(jnp.float32)).astype(jnp.bfloat16)
@@ -376,12 +381,12 @@
                 copy = send(own[s].at[pl.ds(2 * h, 2), window(192 * v, 208)], a1.at[d], sems, s * 3 + d, y_ring[d])
             else:
                 copy = send(own[s].at[:, window(96 * x_at[d], 112)], a2.at[d], sems, s * 3 + d, x_ring[d])
-            first.append(copy)
-
-    second = []
-    for s in range(3):
+            first[s, d] = copy
+
+    second = {}
+    for s in (1, 2, 0):
         for d in range(3):
-            first[s * 3 + d].wait()
+            first[s, d].wait()
         if s == 0:
             total(a0.at[0], own[s][:, window(96 * z, 112)], [a0[d] for d in range(3)])
         elif s == 1:
@@ -399,15 +404,15 @@
                 v = z_at[d]
                 src = a2.at[0, :, window(16 * v + 16 * (v // 2), 48)]
                 copy = send(src, b2.at[d], sems, 9 + s * 3 + d, z_ring[d])
-            second.append(copy)
+            second[s, d] = copy
 
     def homeward(s):
         return remote(piece.at[s - 1], home_ref.at[s - 1], (home_s, home_r), s - 1, (targets[s - 1], r))
 
-    third = []
-    for s in range(3):
+    third = {}
+    for s in (1, 2, 0):
         for d in range(3):
-            second[s * 3 + d].wait()
+            second[s, d].wait()
         if s == 0:
             total(b0.at[0], a0[0, pl.ds(2 * yhi, 2), window(48 * ylo, 64)], [b0[d] for d in range(3)])
         elif s == 1:
@@ -426,11 +431,11 @@
                 _, at = last_window(2, x * 8 + z * 2 + v)
                 src = b2.at[0, pl.ds(2 * h, 2), window(at, 32)]
                 copy = send(src, c2.at[d], sems, 18 + s * 3 + d, y_ring[d])
-            third.append(copy)
-
-    for s in range(3):
+            third[s, d] = copy
+
+    for s in (1, 2, 0):
         for d in range(3):
-            third[s * 3 + d].wait()
+            third[s, d].wait()
         if s == 0:
             _, at = last_window(0, z * 8 + ylo * 4 + x)
             total(out_ref, b0[0, :, window(at, 32)], [c0[d] for d in range(3)])

time: 151 us -> 152 us (level)
  no operation moved by 1% of the time
where the time goes in v7:
time: 152 us
  Pallas kernels  142 us (93%)
  local copies, waits for them, and re-layouts  5.13 us (3%)
  other arithmetic  3.98 us (3%)
    pallas_call x1, Pallas kernels, train_call(): pl.pallas_call(train_kernel, in_specs=[pl.BlockSpec(memory_space=pltpu.SM...  142 us

profile of v7, /device:TPU:8, one launch (start us, length us, event | category | flops | bytes accessed | tf_op | source)
XLA Modules:
  0.0 151.9 jit_solution(5603280378898361291)
XLA Ops:
  0.6 1.3 reshape.31.need_ref
  1.9 0.7 reduce
  2.6 0.6 reshape.32.slot_ref
  3.2 141.8 %train_buckets.1 = (f32[400,1024]{1,0:T(8,128)}, f32[1,1024]{1,0:T(1,128)}, bf16[400,1024]{1,0:T(8,128)(2,1)}, f32[1,1024]{1,0:T(1,128)}, f32[2,32,512]{2,1,0:T(8,128)}, /*index=5*/bf16[2,2,32,512]{3,2,1,0:T(8,128)(2,1)}) custom-call(s32[16]{0:T(128)} %reshape.31.need_ref, s32[24]{0:T(128)} %reshape.32.slot_ref, bf16[6,400,400]{2,1,0:T(8,128)(2,1)} %own_ref.1, ...), custom_call_target="tpu_custom_call" | custom-call | tf_op jit(solution)/shard_map/train_buckets/pallas_call | solution.py:481
  145.0 0.0 copy-start.2
  145.0 0.0 copy-start.1
  145.1 2.5 %convert_bitcast_fusion = f32[1024,400]{0,1:T(8,128)} fusion(bf16[400,1024]{1,0:T(8,128)(2,1)} %get-tuple-element.13), kind=kLoop, calls=%fused_computation | loop fusion | flops 409600 | bytes 2457600 | tf_op jit(solution)/shard_map/convert_element_type | solution.py:552
  147.6 0.0 copy-start
  147.6 0.0 copy-done.2
  147.6 0.2 reshape.41
  147.9 0.1 constant_dynamic-slice_fusion
  148.1 0.2 reshape.39
  148.3 0.1 constant_dynamic-slice_fusion.1
  148.5 0.0 copy-done.1
  148.5 0.2 reshape.33
  148.7 0.1 constant_dynamic-slice_fusion.2
  148.8 0.7 pad_maximum_fusion
  149.6 0.0 copy-done
  149.6 0.0 copy-start.4
  149.6 0.0 copy-start.3
  149.6 1.2 copy.18
  150.7 0.0 copy-done.4
  150.7 0.6 copy.19
  151.3 0.0 copy-done.3
  151.3 0.6 copy.20
  (2 shorter events, 0.0 us)
Async XLA Ops:
  145.0 2.6 %copy-start.2 = (bf16[2,2,32,512]{3,2,1,0:T(8,128)(2,1)S(1)}, bf16[2,2,32,512]{3,2,1,0:T(8,128)(2,1)}, u32[]{:S(2)}) copy-start(bf16[2,2,32,512]{3,2,1,0:T(8,128)(2,1)} %get-tuple-element.16) | copy-start | bytes 393220
  145.0 3.4 %copy-start.1 = (f32[2,32,512]{2,1,0:T(8,128)S(1)}, f32[2,32,512]{2,1,0:T(8,128)}, u32[]{:S(2)}) copy-start(f32[2,32,512]{2,1,0:T(8,128)} %get-tuple-element.15) | copy-start | bytes 393220
  147.6 2.0 %copy-start = (f32[400,1024]{1,0:T(8,128)S(1)}, f32[400,1024]{1,0:T(8,128)}, u32[]{:S(2)}) copy-start(f32[400,1024]{1,0:T(8,128)} %get-tuple-element.11) | copy-start | bytes 4915204
  149.6 1.2 copy-start.4
  149.6 1.8 %copy-start.3 = (f32[1,1024]{1,0:T(1,128)S(1)}, f32[1,1024]{1,0:T(1,128)}, u32[]{:S(2)}) copy-start(f32[1,1024]{1,0:T(1,128)} %get-tuple-element.14) | copy-start | bytes 12292
